TPU v7x, 512 devices: a whole 4x8x8 slice. The times are simulated.
512 devices in a mesh: row: 32 (over z_lo, y, core), col: 16 (over x, z_hi).
Axes of the slice: x: 4, y: 8, z: 8 (z_hi: 4, z_lo: 2; z = z_hi * 2 + z_lo), core: 2. Of those that a mesh axis runs over, the one named last changes fastest.
Arguments:
- positions: float32 [3, 32768], P(None, ('row', 'col')), may hold values from -1 to 1
- normals: float32 [3, 32768], P(None, ('row', 'col')), may hold values from -4 to 4
- areas: float32 [32768], P(('row', 'col')), may hold values from 0.00012207031 to 0.0012207031
- direct: bfloat16 [32768, 64], P(('row', 'col')), may hold values from -6 to 6
- adjoint: bfloat16 [32768, 64], P(('row', 'col')), may hold values from -6 to 6
- spline: bfloat16 [512, 256, 512], P(('row', 'col')), may hold values from -0.375 to 0.375
- block_lists: int32 [128, 4], replicated, may hold values from 0 to 511, all different within a row
- patch_counts: int32 [64], replicated, may hold values from 1 to 8, 128 in all
- patch_owner: int32 [64], replicated, may hold values from 0 to 63, each once
Outputs:
- densities: float32 [32768], P(('row', 'col'))
- patch_grad: float32 [64, 512], P('row')
Inputs may be any that keep to these rules, and one draw needn't show every extreme that they name: `block_lists`: each row names 4 different spline blocks, and every spline block is named by some row. `patch_counts`: the counts sum to 128; the largest is exactly 8. `patch_owner`: A permutation of the patches.
All inputs are finite; a program needn't handle non-finite values.
Results may differ from a plain program's by a relative error of at most 0.0029.
Values may be sent and summed in bfloat16 or wider, within the bound.
No kernel may reach another device: no remote copies, remote signals or barrier semaphores. Data moves between devices by JAX's collectives and lax.ppermute only.
A program may use at most 64 MiB of HBM per device.

v0:
```python
import jax
import jax.numpy as jnp
from jax import lax
from jax.sharding import PartitionSpec as P

BPAN = 256
NPATCH = 64
NBLK = 128


wave_number = 6.0
inv_four_pi = 0.07957747154594767


def kernel_block(tgt_pos, tgt_nrm, src_pos, src_area):
    depth_t = 0.5 * (tgt_pos[2] - 1.2)
    depth_s = 0.5 * (src_pos[2] - 1.2)
    delta_x = tgt_pos[0][:, None] - src_pos[0][None, :]
    delta_y = tgt_pos[1][:, None] - src_pos[1][None, :]
    delta_z = depth_t[:, None] - depth_s[None, :]
    image_z = depth_t[:, None] + depth_s[None, :]
    area_row = src_area[None, :]
    level = delta_x * delta_x + delta_y * delta_y
    near = level + delta_z * delta_z + area_row
    mirror = level + image_z * image_z + area_row
    slope = tgt_nrm[0][:, None] * delta_x + tgt_nrm[1][:, None] * delta_y
    vertical = tgt_nrm[2][:, None]
    rankine = (slope + vertical * delta_z) / (near * jnp.sqrt(near))
    reflect = (slope + vertical * image_z) / (mirror * jnp.sqrt(mirror))
    waves = (
        2.0
        * wave_number
        * jnp.exp(wave_number * image_z)
        * vertical
        * jnp.cos(wave_number * jnp.sqrt(level + area_row))
    )
    return area_row * (rankine + reflect - waves) * inv_four_pi


def on_device(
    positions, normals, areas, direct, adjoint, spline, block_lists, patch_counts, patch_owner
):
    tgt_pos, tgt_nrm = (
        lax.all_gather(positions, "col", axis=1, tiled=True),
        lax.all_gather(normals, "col", axis=1, tiled=True),
    )
    adj_tgt = lax.all_gather(adjoint, "col", axis=0, tiled=True)
    src_pos, src_area = (
        lax.all_gather(positions, "row", axis=1, tiled=True),
        lax.all_gather(areas, "row", axis=0, tiled=True),
    )
    dir_src = lax.all_gather(direct, "row", axis=0, tiled=True)
    targets = tgt_pos.shape[1]
    sources = src_pos.shape[1]
    columns = direct.shape[1]
    step_rows = min(targets, 256)
    count = targets // step_rows

    def advance(carry, index):
        start = index * step_rows
        part_pos = lax.dynamic_slice_in_dim(tgt_pos, start, step_rows, 1)
        part_nrm = lax.dynamic_slice_in_dim(tgt_nrm, start, step_rows, 1)
        adj_rows = lax.dynamic_slice_in_dim(adj_tgt, start, step_rows, 0)
        tile = kernel_block(part_pos, part_nrm, src_pos, src_area).astype(jnp.bfloat16)
        image_rows = jnp.dot(tile, dir_src, preferred_element_type=jnp.float32)
        carry = carry + lax.dot_general(
            tile, adj_rows, (((0,), (0,)), ((), ())), preferred_element_type=jnp.float32
        )
        return (carry, image_rows)

    adj_part, pieces = lax.scan(
        advance, jnp.zeros((sources, columns), jnp.float32), jnp.arange(count, dtype=jnp.int32)
    )
    dir_part = pieces.reshape(targets, columns)
    dir_mine = lax.psum_scatter(dir_part, "col", scatter_dimension=0, tiled=True)
    adj_mine = lax.psum_scatter(adj_part, "row", scatter_dimension=0, tiled=True)
    densities = jnp.sum(
        adjoint.astype(jnp.float32) * dir_mine + direct.astype(jnp.float32) * adj_mine, axis=1
    )
    every_density = lax.all_gather(densities, ("row", "col"), axis=0, tiled=True)
    blocks = every_density.reshape(NBLK, BPAN)
    ends = jnp.cumsum(patch_counts)
    starts = ends - patch_counts
    block_ids = jnp.arange(NBLK, dtype=jnp.int32)
    inside = (
        (starts[:, None] <= block_ids[None, :]) & (block_ids[None, :] < ends[:, None])
    ).astype(jnp.float32)
    owners = (patch_owner[None, :] == jnp.arange(NPATCH, dtype=jnp.int32)[:, None]).astype(
        jnp.float32
    )
    owned = jnp.dot(owners, inside, precision=lax.Precision.HIGHEST)
    holder = lax.axis_index(("row", "col"))
    listed = jnp.any(block_lists == holder, axis=1).astype(jnp.float32)
    weights = owned * listed[None, :]
    gathered = jnp.dot(weights, blocks, precision=lax.Precision.HIGHEST)
    contrib = jnp.dot(gathered, spline[0].astype(jnp.float32), precision=lax.Precision.HIGHEST)
    partial_rows = lax.psum_scatter(contrib, "row", scatter_dimension=0, tiled=True)
    patch_grad = lax.psum(partial_rows, "col")
    return (densities, patch_grad)


def solution(mesh):
    placed = (
        P(None, ("row", "col")),
        P(None, ("row", "col")),
        P(("row", "col")),
        P(("row", "col"), None),
        P(("row", "col"), None),
        P(("row", "col"), None, None),
        P(),
        P(),
        P(),
    )
    return jax.shard_map(
        on_device,
        mesh=mesh,
        in_specs=placed,
        out_specs=(P(("row", "col")), P("row", None)),
        check_vma=False,
    )
```

profile of v0, /device:TPU:1, one launch (start us, length us, event | category | flops | bytes accessed | tf_op | source)
XLA Modules:
  0.0 1069.3 jit_solution(15851021440877553116)
XLA Ops:
  7.2 37.6 %all-gather.2 = f32[32,64,3]{1,2,0:T(4,128)S(1)} all-gather(f32[1,64,3]{1,2,0:T(4,128)} %bitcast.89), channel_id=1, replica_groups=mesh['row'=32,'col'=16] {'row'}, dimensions={0}, use_global_device_ids=true | all-gather | bytes 25344 | tf_op jit(solution)/shard_map/all_gather | solution.py:49
  44.8 41.2 %all-gather.1 = f32[16,64,3]{1,2,0:T(4,128)S(1)} all-gather(f32[1,64,3]{1,2,0:T(4,128)} %bitcast.90), channel_id=1, replica_groups=mesh['row'=32,'col'=16] {'col'}, dimensions={0}, use_global_device_ids=true | all-gather | bytes 13056 | tf_op jit(solution)/shard_map/all_gather | solution.py:44
  86.1 1.3 fusion.40
  88.1 0.9 dynamic-update-slice
  88.9 60.7 %all-reduce = f32[2048]{0:T(1024)S(1)} all-reduce(f32[2048]{0:T(1024)S(1)} %dynamic-update-slice), channel_id=1, replica_groups=mesh['row'=32,'col'=16] {'row'}, use_global_device_ids=true, to_apply=%add | all-reduce | flops 2048 | bytes 16384
  149.9 32.6 %all_gather.26 = bf16[2048,64]{1,0:T(8,128)(2,1)S(1)} all-gather(bf16[64,64]{1,0:T(8,128)(2,1)} %param.14), channel_id=1, replica_groups=mesh['row'=32,'col'=16] {'row'}, dimensions={0}, use_global_device_ids=true | all-gather | bytes 270336 | tf_op jit(solution)/shard_map/all_gather | solution.py:52
  182.5 33.4 %all_gather.25 = bf16[1024,64]{1,0:T(8,128)(2,1)S(1)} all-gather(bf16[64,64]{1,0:T(8,128)(2,1)} %param.15), channel_id=1, replica_groups=mesh['row'=32,'col'=16] {'col'}, dimensions={0}, use_global_device_ids=true | all-gather | bytes 139264 | tf_op jit(solution)/shard_map/all_gather | solution.py:47
  215.9 33.4 %all-gather = f32[16,64,3]{1,2,0:T(4,128)S(1)} all-gather(f32[1,64,3]{1,2,0:T(4,128)S(1)} %bitcast.91), channel_id=1, replica_groups=mesh['row'=32,'col'=16] {'col'}, dimensions={0}, use_global_device_ids=true | all-gather | bytes 13056 | tf_op jit(solution)/shard_map/all_gather | solution.py:45
  249.3 94.6 %while.16 = (s32[]{:T(128)}, f32[2048,64]{0,1:T(8,128)S(1)}, f32[4,256,64]{1,2,0:T(8,128)S(1)}, f32[2048]{0:T(1024)S(1)}, s32[4]{0:T(128)S(1)}, /*index=5*/f32[3...) while((s32[]{:T(128)}, f32[2048,64]{0,1:T(8,128)S(1)}, ...), condition=%wide.region_1.2_spmd.clone, body=%wide.region_0.1_spmd.clone.sunk | while | flops 170136320 | bytes 1847557 | solution.py:71
  249.4 0.7 dynamic_slice.38
  250.9 11.1 %convolution_add_fusion.2 = f32[2048,64]{0,1:T(8,128)S(1)} fusion(f32[2048,64]{0,1:T(8,128)S(1)} %get-tuple-element.319, pred[]{:T(512)S(6)} %compare.3, bf16[1024,64]{1,0:T(8,128)(2,1)S(1)} %get-tuple-element.342, s32[]{:T(128)S(6)} %select_n.11, f32[256]{0:T(256)S(1)} %broadcast_multiply_fusion.2, f32[2048]{0:T(1024)S(1)} %bitcast.70, ...), kind=kOutput, calls=%fused_computation.11.clone.1 | convolution fusion | flops 85196800 | bytes 1154053 | tf_op jit(solution)/shard_map/while/body/eval_jaxpr/dot_general | solution.py:66
  261.9 11.0 %fusion.57 = f32[4,256,64]{1,2,0:T(8,128)S(1)} fusion(f32[4,256,64]{1,2,0:T(8,128)S(1)} %get-tuple-element.320, s32[]{:T(128)} %get-tuple-element.318, bf16[2048,64]{1,0:T(8,128)(2,1)S(1)} %get-tuple-element.343, f32[256]{0:T(256)S(1)} %broadcast_multiply_fusion.2, f32[2048]{0:T(1024)S(1)} %bitcast.71, f32[256]{0:T(256)S(1)} %bitcast.84, ...), kind=kOutput, calls=%fused_computation.35.clone.1 | convolution fusion | flops 84934656 | bytes 629764 | tf_op jit(solution)/shard_map/while/body/eval_jaxpr/dot_general | solution.py:65
  273.0 0.7 dynamic_slice.38
  274.5 11.1 %convolution_add_fusion.2 = f32[2048,64]{0,1:T(8,128)S(1)} fusion(f32[2048,64]{0,1:T(8,128)S(1)} %get-tuple-element.319, pred[]{:T(512)S(6)} %compare.3, bf16[1024,64]{1,0:T(8,128)(2,1)S(1)} %get-tuple-element.342, s32[]{:T(128)S(6)} %select_n.11, f32[256]{0:T(256)S(1)} %broadcast_multiply_fusion.2, f32[2048]{0:T(1024)S(1)} %bitcast.70, ...), kind=kOutput, calls=%fused_computation.11.clone.1 | convolution fusion | flops 85196800 | bytes 1154053 | tf_op jit(solution)/shard_map/while/body/eval_jaxpr/dot_general | solution.py:66
  285.6 11.0 %fusion.57 = f32[4,256,64]{1,2,0:T(8,128)S(1)} fusion(f32[4,256,64]{1,2,0:T(8,128)S(1)} %get-tuple-element.320, s32[]{:T(128)} %get-tuple-element.318, bf16[2048,64]{1,0:T(8,128)(2,1)S(1)} %get-tuple-element.343, f32[256]{0:T(256)S(1)} %broadcast_multiply_fusion.2, f32[2048]{0:T(1024)S(1)} %bitcast.71, f32[256]{0:T(256)S(1)} %bitcast.84, ...), kind=kOutput, calls=%fused_computation.35.clone.1 | convolution fusion | flops 84934656 | bytes 629764 | tf_op jit(solution)/shard_map/while/body/eval_jaxpr/dot_general | solution.py:65
  296.7 0.7 dynamic_slice.38
  298.2 11.1 %convolution_add_fusion.2 = f32[2048,64]{0,1:T(8,128)S(1)} fusion(f32[2048,64]{0,1:T(8,128)S(1)} %get-tuple-element.319, pred[]{:T(512)S(6)} %compare.3, bf16[1024,64]{1,0:T(8,128)(2,1)S(1)} %get-tuple-element.342, s32[]{:T(128)S(6)} %select_n.11, f32[256]{0:T(256)S(1)} %broadcast_multiply_fusion.2, f32[2048]{0:T(1024)S(1)} %bitcast.70, ...), kind=kOutput, calls=%fused_computation.11.clone.1 | convolution fusion | flops 85196800 | bytes 1154053 | tf_op jit(solution)/shard_map/while/body/eval_jaxpr/dot_general | solution.py:66
  309.3 11.0 %fusion.57 = f32[4,256,64]{1,2,0:T(8,128)S(1)} fusion(f32[4,256,64]{1,2,0:T(8,128)S(1)} %get-tuple-element.320, s32[]{:T(128)} %get-tuple-element.318, bf16[2048,64]{1,0:T(8,128)(2,1)S(1)} %get-tuple-element.343, f32[256]{0:T(256)S(1)} %broadcast_multiply_fusion.2, f32[2048]{0:T(1024)S(1)} %bitcast.71, f32[256]{0:T(256)S(1)} %bitcast.84, ...), kind=kOutput, calls=%fused_computation.35.clone.1 | convolution fusion | flops 84934656 | bytes 629764 | tf_op jit(solution)/shard_map/while/body/eval_jaxpr/dot_general | solution.py:65
  321.8 11.1 %convolution_add_fusion.2 = f32[2048,64]{0,1:T(8,128)S(1)} fusion(f32[2048,64]{0,1:T(8,128)S(1)} %get-tuple-element.319, pred[]{:T(512)S(6)} %compare.3, bf16[1024,64]{1,0:T(8,128)(2,1)S(1)} %get-tuple-element.342, s32[]{:T(128)S(6)} %select_n.11, f32[256]{0:T(256)S(1)} %broadcast_multiply_fusion.2, f32[2048]{0:T(1024)S(1)} %bitcast.70, ...), kind=kOutput, calls=%fused_computation.11.clone.1 | convolution fusion | flops 85196800 | bytes 1154053 | tf_op jit(solution)/shard_map/while/body/eval_jaxpr/dot_general | solution.py:66
  332.9 11.0 %fusion.57 = f32[4,256,64]{1,2,0:T(8,128)S(1)} fusion(f32[4,256,64]{1,2,0:T(8,128)S(1)} %get-tuple-element.320, s32[]{:T(128)} %get-tuple-element.318, bf16[2048,64]{1,0:T(8,128)(2,1)S(1)} %get-tuple-element.343, f32[256]{0:T(256)S(1)} %broadcast_multiply_fusion.2, f32[2048]{0:T(1024)S(1)} %bitcast.71, f32[256]{0:T(256)S(1)} %bitcast.84, ...), kind=kOutput, calls=%fused_computation.35.clone.1 | convolution fusion | flops 84934656 | bytes 629764 | tf_op jit(solution)/shard_map/while/body/eval_jaxpr/dot_general | solution.py:65
  344.0 1.0 copy.39
  345.1 1.3 copy.37
  347.1 91.1 %reduce-scatter.7.cloned.1.call-done = f32[64,64]{1,0:T(8,128)} async-done(((f32[1024,64]{1,0:T(8,128)}), f32[64,64]{1,0:T(8,128)}) %reduce-scatter.7.cloned.1.call-update) | async-done | bytes 16400
  438.3 0.8 copy.36
  439.1 117.8 %reduce-scatter.9.cloned.1.call-done = f32[64,64]{1,0:T(8,128)} async-done(((f32[2048,64]{1,0:T(8,128)}), f32[64,64]{1,0:T(8,128)}) %reduce-scatter.9.cloned.1.call-update) | async-done | bytes 16400
  556.8 0.8 copy.38
  559.0 263.0 %all-reduce.6.cloned.1.call-done = f32[32768]{0:T(1024)} async-done(((f32[32768]{0:T(1024)}), f32[32768]{0:T(1024)}) %all-reduce.6.cloned.1.call-update) | async-done | bytes 131088
  822.0 0.9 reshape.62
  823.1 0.9 fusion.32
  824.7 197.9 %all-reduce.8.cloned.1.call-done = f32[64,512]{1,0:T(8,128)} async-done(((f32[64,512]{1,0:T(8,128)}), f32[64,512]{1,0:T(8,128)}) %all-reduce.8.cloned.1.call-update) | async-done | bytes 131088
  1022.6 0.7 constant_dynamic-slice_fusion.2
  1023.3 39.4 %psum.7 = f32[2,512]{1,0:T(2,128)} all-reduce(f32[2,512]{1,0:T(2,128)S(1)} %constant_dynamic-slice_fusion.2), channel_id=1, replica_groups=mesh['row'=32,'col'=16] {'col'}, use_global_device_ids=true, to_apply=%region_8.9 | all-reduce | flops 1024 | bytes 8192 | tf_op jit(solution)/shard_map/psum | solution.py:98
  (62 shorter events, 3.6 us)
Async XLA Ops:
  7.2 816.0 %copy-start = (bf16[1,256,512]{2,1,0:T(8,128)(2,1)S(1)}, bf16[1,256,512]{2,1,0:T(8,128)(2,1)}, u32[]{:S(2)}) copy-start(bf16[1,256,512]{2,1,0:T(8,128)(2,1)} %param.16) | copy-start | bytes 786436
  7.2 208.7 %copy-start.4 = (f32[3,64]{1,0:T(4,128)S(1)}, f32[3,64]{1,0:T(4,128)}, u32[]{:S(2)}) copy-start(f32[3,64]{1,0:T(4,128)} %param.12) | copy-start | bytes 2308
  7.2 431.1 %reduce-scatter.7.cloned.1.call-start = ((), (), s32[]{:S(2)}) async-start(), calls=%async_computation.3 | async-start | bytes 557056
  345.0 211.8 %reduce-scatter.9.cloned.1.call-start = ((), (), s32[]{:S(2)}) async-start(), calls=%async_computation.4 | async-start | bytes 1081344
  345.1 1.5 copy-start.2
  345.1 1.5 copy-start.3
  345.1 1.6 copy-start.5
  345.1 1.7 copy-start.6
  346.5 212.3 %copy-start.8 = (s32[64]{0:T(128)S(1)}, s32[64]{0:T(128)}, u32[]{:S(2)}) copy-start(s32[64]{0:T(128)} %param.19) | copy-start | bytes 772
  346.5 475.5 %all-reduce.6.cloned.1.call-start = ((), (), s32[]{:S(2)}) async-start(), calls=%async_computation.2 | async-start | bytes 262144
  557.7 505.1 %copy-start.7 = (f32[64]{0:T(128)}, f32[64]{0:T(128)S(1)}, u32[]{:S(2)}) copy-start(f32[64]{0:T(128)S(1)} %add_reduce_fusion) | copy-start | bytes 772
  558.0 0.7 copy-start.1
  558.7 463.9 %all-reduce.8.cloned.1.call-start = ((), (), s32[]{:S(2)}) async-start(), calls=%async_computation.5 | async-start | bytes 262144
Sparse Core Ops, SparseCore 0:
  345.2 93.0 reduce-scatter.6
  441.3 115.5 reduce-scatter.8
  561.8 260.0 all-reduce.5
  825.0 197.5 all-reduce.7
where the time goes:
time: 1080 us; the launch traced here: 1070 us
  waiting for transfers between devices  670 us (62%)
  blocking collectives  278 us (26%)
  matrix products  89.9 us (8%)
  between operations  15.3 us (1%)
  local copies, waits for them, and re-layouts  12.1 us (1%)
    unnamed x8, waiting for transfers between devices  670 us
    unnamed x1, blocking collectives  60.7 us
    dot_general x4, matrix products, advance(): lax.dot_general(tile, adj_rows, (((0,), (0,)), ((), ())), preferred_eleme...  44.3 us
    dot_general x4, matrix products, advance(): image_rows = jnp.dot(tile, dir_src, preferred_element_type=jnp.float32)  44.2 us
    all_gather x1, blocking collectives, on_device(): lax.all_gather(positions, 'col', axis=1, tiled=True)  41.2 us
    psum x1, blocking collectives, on_device(): patch_grad = lax.psum(partial_rows, 'col')  39.4 us
    all_gather x1, blocking collectives, on_device(): lax.all_gather(positions, 'row', axis=1, tiled=True)  37.6 us
    all_gather x1, blocking collectives, on_device(): adj_tgt = lax.all_gather(adjoint, 'col', axis=0, tiled=True)  33.4 us
  transfers between devices with their start and end apart: 4, of which 4 were waited for; matrix products, arithmetic and copies ran while one was open for 0% of the time, Pallas kernels for 0%

commit v1 on v0

v1 whole, which is shorter than its diff:
```python
import jax
import jax.numpy as jnp
import numpy as np
from jax import lax
from jax.experimental import pallas as pl
from jax.experimental.pallas import tpu as pltpu
from jax.sharding import PartitionSpec as P

F32 = jnp.float32
BF16 = jnp.bfloat16
BPAN = 256
NPATCH = 64
NBLK = 128
LANES = 128
wave_number = 6.0
inv_four_pi = 0.07957747154594767

TURNS = wave_number / (2.0 * np.pi)
DEGREE = 6


def cosine_coefficients():
    k = np.arange(64)
    nodes = 0.125 + 0.125 * np.cos(np.pi * (2 * k + 1) / 128)
    fit = np.polynomial.chebyshev.Chebyshev.fit(
        nodes, np.cos(2 * np.pi * np.sqrt(nodes)), DEGREE, domain=[0.0, 0.25]
    )
    return fit.convert(kind=np.polynomial.Polynomial).coef


COEF = cosine_coefficients()
LEAD = float(COEF[-1])
MONIC = [float(c / COEF[-1]) for c in COEF[:-1]]
ROUNDER = float(3 << 22)
AREA_SCALE = float(TURNS**2 * inv_four_pi)
WAVE_SCALE = float(2.0 * wave_number * inv_four_pi * LEAD)

GEO = 64
T_NAMES = 6
S_NAMES = 4


def split3(v):
    hi = v.astype(BF16)
    rest = v - hi.astype(F32)
    mid = rest.astype(BF16)
    lo = (rest - mid.astype(F32)).astype(BF16)
    return hi, mid, lo


def pack_kernel(pos_ref, nrm_ref, area_ref, dir_ref, adj_ref, tgt_ref, src_ref):
    pos = pos_ref[...]
    row = lax.broadcasted_iota(jnp.int32, pos.shape, 0)
    pos = jnp.where(row == 2, 0.5 * (pos - 1.2), pos) * TURNS

    def rows(values):
        h, m, l = split3(values)
        return jnp.concatenate([h.astype(F32), m.astype(F32), l.astype(F32)], axis=0)

    def lay(parts, cols, ref):
        stacked = jnp.concatenate(parts, axis=0)
        depth = stacked.shape[0]
        place = lax.broadcasted_iota(jnp.int32, (depth, LANES), 1) == (
            lax.broadcasted_iota(jnp.int32, (depth, LANES), 0) + GEO
        )
        geo = lax.dot_general(
            stacked.astype(BF16),
            place.astype(F32).astype(BF16),
            (((0,), (0,)), ((), ())),
            preferred_element_type=F32,
        ).astype(BF16)
        wide = jnp.concatenate([cols, cols], axis=1)
        lane = lax.broadcasted_iota(jnp.int32, geo.shape, 1)
        ref[...] = jnp.where(lane < GEO, wide.astype(F32), geo.astype(F32)).astype(BF16)

    lay([rows(pos), rows(nrm_ref[...])], adj_ref[...], tgt_ref)
    lay([rows(pos), rows(area_ref[...] * TURNS**2)], dir_ref[...], src_ref)


def pack(positions, normals, areas, direct, adjoint):
    panels = positions.shape[1]
    out = jax.ShapeDtypeStruct((panels, LANES), BF16)
    return pl.pallas_call(pack_kernel, out_shape=(out, out), name="pack")(
        positions, normals, areas.reshape(1, panels), direct, adjoint
    )


def target_lane(k, part):
    return GEO + (0 if k < 3 else 9) + 3 * part + k % 3


def source_lane(k, part):
    return GEO + 3 * part + k if k < 3 else GEO + 9 + part


def picks(shape, axis, lanes):
    where = lax.broadcasted_iota(jnp.int32, shape, axis)
    hit = (where == lanes[0]) | (where == lanes[1]) | (where == lanes[2])
    return jnp.where(hit, 1.0, 0.0).astype(BF16)


ROWS = 16
CHUNK = 256


def tile_kernel(tgt_ref, src_ref, row_ref, col_ref, tgeo, sgeo, images, rowacc):
    targets, sources = tgt_ref.shape[0], src_ref.shape[0]
    contract_last = (((1,), (1,)), ((), ()))
    for k in range(T_NAMES):
        spread = picks((LANES, LANES), 0, [target_lane(k, p) for p in range(3)])
        tgeo[k] = jnp.dot(tgt_ref[...], spread, preferred_element_type=F32)
    tgeo[6] = (WAVE_SCALE * tgeo[5]) * jnp.exp((wave_number / TURNS) * tgeo[2])
    for k in range(S_NAMES):
        spread = picks((8, LANES), 1, [source_lane(k, p) for p in range(3)])
        sgeo[k] = lax.dot_general(spread, src_ref[...], contract_last, preferred_element_type=F32)
    sgeo[4] = (sgeo[3] * (1.0 / TURNS**2)) * jnp.exp((wave_number / TURNS) * sgeo[2])
    sgeo[5] = sgeo[3] * (AREA_SCALE / TURNS**2)
    rowacc[...] = jnp.zeros_like(rowacc)

    def chunk(j, _):
        s0 = pl.multiple_of(j * CHUNK, CHUNK)
        images[...] = lax.dot_general(
            tgt_ref[:, :GEO],
            src_ref[pl.ds(s0, CHUNK), :GEO],
            contract_last,
            preferred_element_type=F32,
        )
        halves = range(CHUNK // LANES)

        def wide(k, h):
            v = sgeo[k, :, pl.ds(pl.multiple_of(s0 + h * LANES, LANES), LANES)]
            return jnp.concatenate([v] * (ROWS // 8), axis=0)

        src = [[wide(k, h) for k in range(6)] for h in halves]

        def step(i, acc):
            t0 = pl.multiple_of(i * ROWS, ROWS)
            xt, yt, zt, nx, ny, nz, amp = (tgeo[k, pl.ds(t0, ROWS), :] for k in range(7))
            zt4, nz2 = 4.0 * zt, 2.0 * nz
            new, total = [], rowacc[pl.ds(t0, ROWS), :]
            for h in halves:
                xs, ys, zs, area, ebb, share = src[h]
                dx, dy, dz = xt - xs, yt - ys, zt - zs
                flat = dx * dx + dy * dy + area
                near = flat + dz * dz
                mirror = near + zt4 * zs
                top = nx * dx + ny * dy + nz * dz
                topi = top + nz2 * zs
                i1, i2, i3 = lax.rsqrt(near), lax.rsqrt(mirror), lax.rsqrt(flat)
                pair = top * (i1 * i1 * i1) + topi * (i2 * i2 * i2)
                phase = flat * i3
                f = phase - ((phase + ROUNDER) - ROUNDER)
                g = f * f
                p = g + MONIC[-1]
                for c in MONIC[-2::-1]:
                    p = p * g + c
                kern = share * pair - (amp * ebb) * p
                w = kern.astype(BF16).astype(F32) * images[pl.ds(t0, ROWS), h * LANES : (h + 1) * LANES]
                new.append(acc[h] + w)
                total = total + w
            rowacc[pl.ds(t0, ROWS), :] = total
            return tuple(new)

        zero = jnp.zeros((ROWS, LANES), F32)
        acc = lax.fori_loop(0, targets // ROWS, step, (zero,) * len(halves), unroll=2)
        for h in halves:
            col_ref[0:1, pl.ds(pl.multiple_of(s0 + h * LANES, LANES), LANES)] = jnp.sum(acc[h], axis=0, keepdims=True)
        return 0

    lax.fori_loop(0, sources // CHUNK, chunk, 0)
    for g in range(targets // LANES):
        line = jnp.sum(rowacc[g * LANES : (g + 1) * LANES, :].T, axis=0, keepdims=True)
        row_ref[g // 2 : g // 2 + 1, (g % 2) * LANES : (g % 2 + 1) * LANES] = line


def tile(tgt, src):
    targets, sources = tgt.shape[0], src.shape[0]
    return pl.pallas_call(
        tile_kernel,
        out_shape=(
            jax.ShapeDtypeStruct((targets // BPAN, BPAN), F32),
            jax.ShapeDtypeStruct((1, sources), F32),
        ),
        scratch_shapes=[
            pltpu.VMEM((7, targets, LANES), F32),
            pltpu.VMEM((6, 8, sources), F32),
            pltpu.VMEM((targets, CHUNK), F32),
            pltpu.VMEM((targets, LANES), F32),
        ],
        compiler_params=pltpu.CompilerParams(vmem_limit_bytes=24 << 20),
        name="tile",
    )(tgt, src)


def patch_kernel(mix_ref, dens_ref, spline_ref, out_ref):
    hi, mid, lo = split3(dens_ref[...])
    mix = mix_ref[...].astype(BF16)
    got = sum(jnp.dot(mix, part, preferred_element_type=F32) for part in (lo, mid, hi))
    hi, mid, lo = split3(got)
    spline = spline_ref[...]
    out_ref[...] = sum(jnp.dot(part, spline, preferred_element_type=F32) for part in (lo, mid, hi))


def patch(mix, blocks, spline):
    return pl.pallas_call(
        patch_kernel,
        out_shape=jax.ShapeDtypeStruct((NPATCH, spline.shape[1]), F32),
        compiler_params=pltpu.CompilerParams(vmem_limit_bytes=16 << 20),
        name="patch",
    )(mix, blocks, spline)


def exchange(pieces, axis):
    return lax.all_to_all(pieces, axis, 0, 0, tiled=True)


def spread(value, axis, count):
    return exchange(jnp.broadcast_to(value[None], (count,) + value.shape), axis)


def solution(mesh):
    nrow, ncol = mesh.shape["row"], mesh.shape["col"]

    def on_device(
        positions, normals, areas, direct, adjoint, spline, block_lists, patch_counts, patch_owner
    ):
        panels = positions.shape[1]
        col = lax.axis_index("col")
        holder = lax.axis_index("row") * ncol + col
        patches = jnp.arange(NPATCH, dtype=jnp.int32)
        before = patches[None, :] < patches[:, None]
        starts = jnp.sum(jnp.where(before, patch_counts[None, :], 0), axis=1)
        ends = starts + patch_counts
        ids = jnp.arange(NBLK, dtype=jnp.int32)
        inside = (starts[:, None] <= ids[None, :]) & (ids[None, :] < ends[:, None])
        row_of = jnp.sum(jnp.where(inside, patch_owner[:, None], 0), axis=0)
        listed = jnp.any(block_lists == holder, axis=1)
        mix = ((row_of[None, :] == patches[:, None]) & listed[None, :]).astype(F32)

        tgt, src = pack(positions, normals, areas, direct, adjoint)
        tgt_all = spread(tgt, "col", ncol).reshape(ncol * panels, LANES)
        src_all = spread(src, "row", nrow).reshape(nrow * panels, LANES)
        row_part, col_part = tile(tgt_all, src_all)

        mine = jnp.sum(exchange(col_part.reshape(nrow, 1, panels), "row"), axis=0)
        per = BPAN // panels
        at_row = lax.broadcasted_iota(jnp.int32, row_part.shape, 0) == col // per
        at_lane = lax.broadcasted_iota(jnp.int32, row_part.shape, 1) // panels == col % per
        row_part = row_part + jnp.where(at_row & at_lane, jnp.tile(mine, (1, per)), 0.0)
        row_dens = jnp.sum(spread(row_part, "col", ncol), axis=0)
        densities = lax.dynamic_slice(row_dens, (col // per, (col % per) * panels), (1, panels)).reshape(panels)
        blocks = spread(row_dens, "row", nrow).reshape(NBLK, BPAN)

        contrib = patch(mix, blocks, spline[0])
        rows = NPATCH // nrow
        partial = jnp.sum(exchange(contrib.reshape(nrow, rows, contrib.shape[1]), "row"), axis=0)
        patch_grad = jnp.sum(spread(partial, "col", ncol), axis=0)
        return densities, patch_grad

    placed = (
        P(None, ("row", "col")),
        P(None, ("row", "col")),
        P(("row", "col")),
        P(("row", "col"), None),
        P(("row", "col"), None),
        P(("row", "col"), None, None),
        P(),
        P(),
        P(),
    )
    return jax.shard_map(
        on_device,
        mesh=mesh,
        in_specs=placed,
        out_specs=(P(("row", "col")), P("row", None)),
        check_vma=False,
    )
```

time: 1080 us -> 151 us (0.14)
  waiting for transfers between devices: 670 us -> 50.4 us
  blocking collectives: 278 us -> 38.1 us
  matrix products: 89.9 us -> 0 us
  starting transfers between devices: 0.16 us -> 28.9 us
  Pallas kernels: 0 us -> 24.1 us
  between operations: 15.3 us -> 0.85 us
    unnamed x8 -> x0, waiting for transfers between devices: 670 us -> none
    all_gather x5 -> x0, blocking collectives: 178 us -> none  [the longest x1 41.2 us: on_device(): lax.all_gather(positions, 'col', axis=1, tiled=True)]
    dot_general x11 -> x0, matrix products: 89.9 us -> none  [the longest x4 44.3 us: advance(): lax.dot_general(tile, adj_rows, (((0,), (0,)), ((), ())), preferred_eleme...]
    unnamed x1 -> x0, blocking collectives: 60.7 us -> none
    all_to_all x0 -> x5, waiting for transfers between devices: none -> 50.4 us  [exchange(): return lax.all_to_all(pieces, axis, 0, 0, tiled=True)]
    psum x1 -> x0, blocking collectives: 39.4 us -> none  [on_device(): patch_grad = lax.psum(partial_rows, 'col')]
    all_to_all x0 -> x2, blocking collectives: none -> 38.1 us  [exchange(): return lax.all_to_all(pieces, axis, 0, 0, tiled=True)]
    all_to_all x0 -> x5, starting transfers between devices: none -> 28.9 us  [exchange(): return lax.all_to_all(pieces, axis, 0, 0, tiled=True)]
  transfers between devices with their start and end apart: 4 -> 5, of which waited for: 4 -> 5; matrix products, arithmetic and copies ran while one was open for 0% -> 1% of each run, Pallas kernels for 0% -> 0%
where the time goes in v1:
time: 151 us; the launch traced here: 150 us
  waiting for transfers between devices  50.4 us (33%)
  blocking collectives  38.1 us (25%)
  starting transfers between devices  28.9 us (19%)
  Pallas kernels  24.1 us (16%)
  local copies, waits for them, and re-layouts  6.22 us (4%)
  other arithmetic  1.78 us (1%)
    all_to_all x5, waiting for transfers between devices, exchange(): return lax.all_to_all(pieces, axis, 0, 0, tiled=True)  50.4 us
    all_to_all x2, blocking collectives, exchange(): return lax.all_to_all(pieces, axis, 0, 0, tiled=True)  38.1 us
    all_to_all x5, starting transfers between devices, exchange(): return lax.all_to_all(pieces, axis, 0, 0, tiled=True)  28.9 us
    pallas_call x1, Pallas kernels, tile(): pl.pallas_call(tile_kernel, out_shape=(jax.ShapeDtypeStruct((targets // B...  22.1 us
    broadcast_in_dim x5, local copies, waits for them, and re-layouts, spread(): return exchange(jnp.broadcast_to(value[None], (count,) + value.shape), axis)  3.59 us
  transfers between devices with their start and end apart: 5, of which 5 were waited for; matrix products, arithmetic and copies ran while one was open for 1% of the time, Pallas kernels for 0%

profile of v1, /device:TPU:1, one launch (start us, length us, event | category | flops | bytes accessed | tf_op | source)
XLA Modules:
  0.0 150.4 jit_solution(10183588333424645531)
XLA Ops:
  0.6 1.6 %pack.1 = (bf16[64,128]{1,0:T(8,128)(2,1)}, bf16[64,128]{1,0:T(8,128)(2,1)}) custom-call(f32[3,64]{1,0:T(4,128)} %pos_ref.1, f32[3,64]{1,0:T(4,128)} %nrm_ref.1, f32[1,64]{1,0:T(1,128)} %bitcast.10, bf16[64,64]{1,0:T(8,128)(2,1)} %dir_ref.1, bf16[64,64]{1,0:T(8,128)(2,1)} %adj_ref.1), custom_call_target="tpu_custom_call" | custom-call | tf_op jit(solution)/shard_map/pack/pallas_call | solution.py:83
  2.2 0.8 broadcast_in_dim.46
  3.0 24.7 %all_to_all.35 = bf16[16,64,128]{2,1,0:T(8,128)(2,1)S(1)} all-to-all(bf16[16,64,128]{2,1,0:T(8,128)(2,1)S(1)} %broadcast_in_dim.46), channel_id=1, replica_groups=mesh['row'=32,'col'=16] {'col'}, dimensions={0} | all-to-all | bytes 524288 | tf_op jit(solution)/shard_map/all_to_all | solution.py:214
  27.7 0.9 broadcast_in_dim.47
  28.6 10.8 %all-to-all-start.1 = ((bf16[32,64,128]{2,1,0:T(8,128)(2,1)}), bf16[32,64,128]{2,1,0:T(8,128)(2,1)S(1)}, u32[]{:S(2)}, u32[]{:S(2)}) async-start(bf16[32,64,128]{2,1,0:T(8,128)(2,1)} %broadcast_in_dim.47), calls=%async_computation.1 | async-start | bytes 1048576 | tf_op jit(solution)/shard_map/all_to_all | solution.py:214
  39.5 16.5 %all-to-all-done.1 = bf16[32,64,128]{2,1,0:T(8,128)(2,1)S(1)} async-done(((bf16[32,64,128]{2,1,0:T(8,128)(2,1)}), bf16[32,64,128]{2,1,0:T(8,128)(2,1)S(1)}, u32[]{:S(2)}, u32[]{:S(2)}) %all-to-all-start.1) | async-done | bytes 524320 | tf_op jit(solution)/shard_map/all_to_all | solution.py:214
  56.0 22.1 %tile.12 = (f32[4,256]{1,0:T(4,128)S(1)}, f32[1,2048]{1,0:T(1,128)S(1)}) custom-call(bf16[1024,128]{1,0:T(8,128)(2,1)S(1)} %bitcast.8, bf16[2048,128]{1,0:T(8,128)(2,1)S(1)} %bitcast.7), custom_call_target="tpu_custom_call" | custom-call | tf_op jit(solution)/shard_map/tile/pallas_call | solution.py:178
  78.1 0.5 broadcast.45
  78.6 0.7 reduce.4
  79.3 0.7 reshape.47
  79.9 5.6 %all-to-all-start.2 = ((f32[32,1,64]{2,1,0:T(1,128)}), f32[32,1,64]{2,1,0:T(1,128)S(1)}, u32[]{:S(2)}, u32[]{:S(2)}) async-start(f32[32,1,64]{2,1,0:T(1,128)} %bitcast.3), calls=%async_computation.2 | async-start | bytes 32768 | tf_op jit(solution)/shard_map/all_to_all | solution.py:214
  85.6 7.9 %all-to-all-done.2 = f32[32,1,64]{2,1,0:T(1,128)S(1)} async-done(((f32[32,1,64]{2,1,0:T(1,128)}), f32[32,1,64]{2,1,0:T(1,128)S(1)}, u32[]{:S(2)}, u32[]{:S(2)}) %all-to-all-start.2) | async-done | bytes 8224 | tf_op jit(solution)/shard_map/all_to_all | solution.py:214
  93.6 0.1 tile.11
  93.7 0.1 select_add_fusion
  93.7 0.6 broadcast_in_dim.50
  94.4 3.6 %all-to-all-start.3 = ((f32[16,4,256]{2,1,0:T(4,128)}), f32[16,4,256]{2,1,0:T(4,128)S(1)}, u32[]{:S(2)}, u32[]{:S(2)}) async-start(f32[16,4,256]{2,1,0:T(4,128)} %broadcast_in_dim.50), calls=%async_computation.3 | async-start | bytes 131072 | tf_op jit(solution)/shard_map/all_to_all | solution.py:214
  98.0 0.1 select_reduce_fusion.1
  98.2 0.6 copy-done.3
  98.8 0.1 select_reduce_fusion
  98.9 8.3 %all-to-all-done.3 = f32[16,4,256]{2,1,0:T(4,128)S(1)} async-done(((f32[16,4,256]{2,1,0:T(4,128)}), f32[16,4,256]{2,1,0:T(4,128)S(1)}, u32[]{:S(2)}, u32[]{:S(2)}) %all-to-all-start.3) | async-done | bytes 65568 | tf_op jit(solution)/shard_map/all_to_all | solution.py:214
  107.2 0.7 broadcast_in_dim.86
  107.9 5.4 %all-to-all-start.4 = ((f32[32,4,256]{2,1,0:T(4,128)}), f32[32,4,256]{2,1,0:T(4,128)S(1)}, u32[]{:S(2)}, u32[]{:S(2)}) async-start(f32[32,4,256]{2,1,0:T(4,128)} %broadcast_in_dim.86), calls=%async_computation.4 | async-start | bytes 262144 | tf_op jit(solution)/shard_map/all_to_all | solution.py:214
  113.4 9.1 %all-to-all-done.4 = f32[32,4,256]{2,1,0:T(4,128)S(1)} async-done(((f32[32,4,256]{2,1,0:T(4,128)}), f32[32,4,256]{2,1,0:T(4,128)S(1)}, u32[]{:S(2)}, u32[]{:S(2)}) %all-to-all-start.4) | async-done | bytes 131104 | tf_op jit(solution)/shard_map/all_to_all | solution.py:214
  122.5 0.4 patch.1
  123.0 0.1 reshape.50
  123.1 13.4 %all_to_all.36 = f32[32,2,512]{2,1,0:T(2,128)S(1)} all-to-all(f32[32,2,512]{2,1,0:T(2,128)S(1)} %reshape.50), channel_id=1, replica_groups=mesh['row'=32,'col'=16] {'row'}, dimensions={0} | all-to-all | bytes 262144 | tf_op jit(solution)/shard_map/all_to_all | solution.py:214
  136.5 0.1 reduce_sum.58
  136.5 0.6 broadcast_in_dim.87
  137.2 3.5 %all-to-all-start.6 = ((f32[16,2,512]{2,1,0:T(2,128)}), f32[16,2,512]{2,1,0:T(2,128)S(1)}, u32[]{:S(2)}, u32[]{:S(2)}) async-start(f32[16,2,512]{2,1,0:T(2,128)} %broadcast_in_dim.87), calls=%async_computation.6 | async-start | bytes 131072 | tf_op jit(solution)/shard_map/all_to_all | solution.py:214
  140.7 0.6 dynamic-slice_bitcast_fusion
  141.3 8.5 %all-to-all-done.6 = f32[16,2,512]{2,1,0:T(2,128)S(1)} async-done(((f32[16,2,512]{2,1,0:T(2,128)}), f32[16,2,512]{2,1,0:T(2,128)S(1)}, u32[]{:S(2)}, u32[]{:S(2)}) %all-to-all-start.6) | async-done | bytes 65568 | tf_op jit(solution)/shard_map/all_to_all | solution.py:214
  149.8 0.6 reduce_sum.59
  (19 shorter events, 0.2 us)
Async XLA Ops:
  3.0 24.7 %copy-start.1 = (bf16[64,128]{1,0:T(8,128)(2,1)S(1)}, bf16[64,128]{1,0:T(8,128)(2,1)}, u32[]{:S(2)}) copy-start(bf16[64,128]{1,0:T(8,128)(2,1)} %get-tuple-element.7) | copy-start | bytes 49156
  28.6 27.4 %all-to-all-start.1 = ((bf16[32,64,128]{2,1,0:T(8,128)(2,1)}), bf16[32,64,128]{2,1,0:T(8,128)(2,1)S(1)}, u32[]{:S(2)}, u32[]{:S(2)}) async-start(bf16[32,64,128]{2,1,0:T(8,128)(2,1)} %broadcast_in_dim.47), calls=%async_computation.1 | async-start | bytes 1048576 | tf_op jit(solution)/shard_map/all_to_all | solution.py:214
  79.9 13.6 %all-to-all-start.2 = ((f32[32,1,64]{2,1,0:T(1,128)}), f32[32,1,64]{2,1,0:T(1,128)S(1)}, u32[]{:S(2)}, u32[]{:S(2)}) async-start(f32[32,1,64]{2,1,0:T(1,128)} %bitcast.3), calls=%async_computation.2 | async-start | bytes 32768 | tf_op jit(solution)/shard_map/all_to_all | solution.py:214
  94.4 3.6 %copy-start.4 = (s32[64]{0:T(128)S(1)}, s32[64]{0:T(128)}, u32[]{:S(2)}) copy-start(s32[64]{0:T(128)} %param.16) | copy-start | bytes 772
  94.4 12.8 %all-to-all-start.3 = ((f32[16,4,256]{2,1,0:T(4,128)}), f32[16,4,256]{2,1,0:T(4,128)S(1)}, u32[]{:S(2)}, u32[]{:S(2)}) async-start(f32[16,4,256]{2,1,0:T(4,128)} %broadcast_in_dim.50), calls=%async_computation.3 | async-start | bytes 131072 | tf_op jit(solution)/shard_map/all_to_all | solution.py:214
  98.1 0.7 copy-start.3
  107.2 6.1 %copy-start.2 = (s32[128,4]{0,1:T(4,128)S(1)}, s32[128,4]{0,1:T(4,128)}, u32[]{:S(2)}) copy-start(s32[128,4]{0,1:T(4,128)} %param.15) | copy-start | bytes 6148
  107.9 14.6 %copy-start = (bf16[1,256,512]{2,1,0:T(8,128)(2,1)S(1)}, bf16[1,256,512]{2,1,0:T(8,128)(2,1)}, u32[]{:S(2)}) copy-start(bf16[1,256,512]{2,1,0:T(8,128)(2,1)} %param.14) | copy-start | bytes 786436
  107.9 14.6 %all-to-all-start.4 = ((f32[32,4,256]{2,1,0:T(4,128)}), f32[32,4,256]{2,1,0:T(4,128)S(1)}, u32[]{:S(2)}, u32[]{:S(2)}) async-start(f32[32,4,256]{2,1,0:T(4,128)} %broadcast_in_dim.86), calls=%async_computation.4 | async-start | bytes 262144 | tf_op jit(solution)/shard_map/all_to_all | solution.py:214
  137.2 12.6 %all-to-all-start.6 = ((f32[16,2,512]{2,1,0:T(2,128)}), f32[16,2,512]{2,1,0:T(2,128)S(1)}, u32[]{:S(2)}, u32[]{:S(2)}) async-start(f32[16,2,512]{2,1,0:T(2,128)} %broadcast_in_dim.87), calls=%async_computation.6 | async-start | bytes 131072 | tf_op jit(solution)/shard_map/all_to_all | solution.py:214

commit v2 on v1

--- a/solution.py
+++ b/solution.py
@@ -4,6 +4,7 @@
 from jax import lax
 from jax.experimental import pallas as pl
 from jax.experimental.pallas import tpu as pltpu
+from jax.sharding import Mesh
 from jax.sharding import PartitionSpec as P
 
 F32 = jnp.float32
@@ -34,6 +35,13 @@
 ROUNDER = float(3 << 22)
 AREA_SCALE = float(TURNS**2 * inv_four_pi)
 WAVE_SCALE = float(2.0 * wave_number * inv_four_pi * LEAD)
+
+PARTS = {"z_lo": 2, "y": 8, "core": 2, "x": 4, "z_hi": 4}
+NAMES = tuple(PARTS)
+TGT_AXES = ("y", "core")
+SRC_AXES = ("z_lo", "x", "z_hi")
+NTGT = PARTS["y"] * PARTS["core"]
+NSRC = PARTS["z_lo"] * PARTS["x"] * PARTS["z_hi"]
 
 GEO = 64
 T_NAMES = 6
@@ -71,7 +79,9 @@
         ).astype(BF16)
         wide = jnp.concatenate([cols, cols], axis=1)
         lane = lax.broadcasted_iota(jnp.int32, geo.shape, 1)
-        ref[...] = jnp.where(lane < GEO, wide.astype(F32), geo.astype(F32)).astype(BF16)
+        features = jnp.where(lane < GEO, wide.astype(F32), geo.astype(F32)).astype(BF16)
+        for piece in range(ref.shape[0]):
+            ref[piece] = features
 
     lay([rows(pos), rows(nrm_ref[...])], adj_ref[...], tgt_ref)
     lay([rows(pos), rows(area_ref[...] * TURNS**2)], dir_ref[...], src_ref)
@@ -79,8 +89,8 @@
 
 def pack(positions, normals, areas, direct, adjoint):
     panels = positions.shape[1]
-    out = jax.ShapeDtypeStruct((panels, LANES), BF16)
-    return pl.pallas_call(pack_kernel, out_shape=(out, out), name="pack")(
+    out = [jax.ShapeDtypeStruct((n, panels, LANES), BF16) for n in (NTGT, NSRC)]
+    return pl.pallas_call(pack_kernel, out_shape=out, name="pack")(
         positions, normals, areas.reshape(1, panels), direct, adjoint
     )
 
@@ -103,7 +113,46 @@
 CHUNK = 256
 
 
-def tile_kernel(tgt_ref, src_ref, row_ref, col_ref, tgeo, sgeo, images, rowacc):
+def device_place():
+    at = {name: lax.axis_index(name) for name in NAMES}
+    rho = at["y"] * PARTS["core"] + at["core"]
+    return rho, at["z_lo"] * PARTS["x"] + at["x"], at["z_hi"]
+
+
+def mix_rows(counts_ref, owner_ref, lists_ref, mix_ref):
+    rho, row, quarter = device_place()
+    nx = PARTS["x"]
+    holder = ((row // nx) * NTGT + rho) * (nx * PARTS["z_hi"]) + (row % nx) * PARTS["z_hi"] + quarter
+
+    def iota(shape, dim):
+        return lax.broadcasted_iota(jnp.int32, shape, dim)
+
+    square = (NPATCH, NPATCH)
+    counts = jnp.broadcast_to(counts_ref[...], square)
+    eye = iota(square, 0) == iota(square, 1)
+    starts = jnp.sum(jnp.where(iota(square, 1) < iota(square, 0), counts, 0).astype(F32), axis=1, keepdims=True)
+    own_counts = jnp.sum(jnp.where(eye, counts, 0).astype(F32), axis=1, keepdims=True)
+    lines = (NPATCH, NBLK)
+    ids = iota(lines, 1).astype(F32)
+    inside = (starts <= ids) & (ids < starts + own_counts)
+    owner = jnp.broadcast_to(owner_ref[...], square)
+    place = iota(square, 0)
+    output = ((place % 4) // 2) * (2 * NTGT) + 2 * (place // 4) + place % 2
+    owned = jnp.where(owner == output, 1.0, 0.0).astype(BF16)
+    listed = jnp.max(jnp.where(lists_ref[...] == holder, 1.0, 0.0), axis=0, keepdims=True)
+    member = jnp.where(inside, jnp.broadcast_to(listed, lines), 0.0).astype(BF16)
+    by_block = jnp.dot(owned, member, preferred_element_type=F32).astype(BF16)
+    cut = (NBLK, NBLK)
+    k = iota(cut, 1)
+    block = ((k % 8) // nx) * (NTGT * nx) + (k // 8) * nx + k % nx
+    order = jnp.where(iota(cut, 0) == block, 1.0, 0.0).astype(BF16)
+    mix_ref[...] = jnp.dot(by_block, order, preferred_element_type=F32).astype(BF16)
+
+
+def tile_kernel(
+    tgt_ref, src_ref, counts_ref, owner_ref, lists_ref, row_ref, col_ref, mix_ref, tgeo, sgeo, images, rowacc, colacc
+):
+    mix_rows(counts_ref, owner_ref, lists_ref, mix_ref)
     targets, sources = tgt_ref.shape[0], src_ref.shape[0]
     contract_last = (((1,), (1,)), ((), ()))
     for k in range(T_NAMES):
@@ -164,114 +213,129 @@
         zero = jnp.zeros((ROWS, LANES), F32)
         acc = lax.fori_loop(0, targets // ROWS, step, (zero,) * len(halves), unroll=2)
         for h in halves:
-            col_ref[0:1, pl.ds(pl.multiple_of(s0 + h * LANES, LANES), LANES)] = jnp.sum(acc[h], axis=0, keepdims=True)
+            colacc[0:1, pl.ds(pl.multiple_of(s0 + h * LANES, LANES), LANES)] = jnp.sum(acc[h], axis=0, keepdims=True)
         return 0
 
     lax.fori_loop(0, sources // CHUNK, chunk, 0)
+    for j in range(sources // BPAN):
+        col_ref[j : j + 1, :] = colacc[0:1, j * BPAN : (j + 1) * BPAN]
+    panels = row_ref.shape[2]
     for g in range(targets // LANES):
         line = jnp.sum(rowacc[g * LANES : (g + 1) * LANES, :].T, axis=0, keepdims=True)
-        row_ref[g // 2 : g // 2 + 1, (g % 2) * LANES : (g % 2 + 1) * LANES] = line
-
-
-def tile(tgt, src):
-    targets, sources = tgt.shape[0], src.shape[0]
+        for half in range(LANES // panels):
+            row_ref[g * (LANES // panels) + half] = line[:, half * panels : (half + 1) * panels]
+
+
+def tile(tgt, src, patch_counts, patch_owner, block_lists):
+    pieces, panels = tgt.shape[:2]
+    targets, sources = pieces * panels, src.shape[0] * panels
     return pl.pallas_call(
         tile_kernel,
         out_shape=(
-            jax.ShapeDtypeStruct((targets // BPAN, BPAN), F32),
-            jax.ShapeDtypeStruct((1, sources), F32),
+            jax.ShapeDtypeStruct((pieces, 1, panels), F32),
+            jax.ShapeDtypeStruct((sources // BPAN, BPAN), F32),
+            jax.ShapeDtypeStruct((NPATCH, NBLK), BF16),
         ),
         scratch_shapes=[
             pltpu.VMEM((7, targets, LANES), F32),
             pltpu.VMEM((6, 8, sources), F32),
             pltpu.VMEM((targets, CHUNK), F32),
             pltpu.VMEM((targets, LANES), F32),
+            pltpu.VMEM((1, sources), F32),
         ],
         compiler_params=pltpu.CompilerParams(vmem_limit_bytes=24 << 20),
         name="tile",
-    )(tgt, src)
-
-
-def patch_kernel(mix_ref, dens_ref, spline_ref, out_ref):
+    )(
+        tgt.reshape(targets, LANES),
+        src.reshape(sources, LANES),
+        patch_counts.reshape(1, NPATCH),
+        patch_owner.reshape(1, NPATCH),
+        block_lists.T,
+    )
+
+
+def patch_kernel(mix_ref, dens_ref, spline_ref, out_ref, own_ref):
     hi, mid, lo = split3(dens_ref[...])
-    mix = mix_ref[...].astype(BF16)
+    mix = mix_ref[...]
     got = sum(jnp.dot(mix, part, preferred_element_type=F32) for part in (lo, mid, hi))
     hi, mid, lo = split3(got)
     spline = spline_ref[...]
-    out_ref[...] = sum(jnp.dot(part, spline, preferred_element_type=F32) for part in (lo, mid, hi))
-
-
-def patch(mix, blocks, spline):
+    rows = sum(jnp.dot(part, spline, preferred_element_type=F32) for part in (lo, mid, hi))
+    for piece in range(out_ref.shape[0]):
+        depth = out_ref.shape[1]
+        out_ref[piece] = rows[piece * depth : (piece + 1) * depth]
+    rho, row, quarter = device_place()
+    line = dens_ref[pl.ds(rho * 8 + row, 1), :]
+    panels = own_ref.shape[1]
+    mine = line[:, :panels]
+    for q in range(1, BPAN // panels):
+        mine = jnp.where(quarter == q, line[:, q * panels : (q + 1) * panels], mine)
+    own_ref[...] = mine
+
+
+def patch(mix, blocks, spline, panels):
     return pl.pallas_call(
         patch_kernel,
-        out_shape=jax.ShapeDtypeStruct((NPATCH, spline.shape[1]), F32),
+        out_shape=(
+            jax.ShapeDtypeStruct((NTGT, NPATCH // NTGT, spline.shape[1]), F32),
+            jax.ShapeDtypeStruct((1, panels), F32),
+        ),
         compiler_params=pltpu.CompilerParams(vmem_limit_bytes=16 << 20),
         name="patch",
     )(mix, blocks, spline)
 
 
-def exchange(pieces, axis):
-    return lax.all_to_all(pieces, axis, 0, 0, tiled=True)
-
-
-def spread(value, axis, count):
-    return exchange(jnp.broadcast_to(value[None], (count,) + value.shape), axis)
+def exchange(pieces, axes):
+    return lax.all_to_all(pieces, axes, 0, 0, tiled=True)
+
+
+def copies(value, count):
+    return jnp.broadcast_to(value[None], (count,) + value.shape)
+
+
+def on_device(
+    positions, normals, areas, direct, adjoint, spline, block_lists, patch_counts, patch_owner
+):
+    panels = positions.shape[1]
+    tgt, src = pack(positions, normals, areas, direct, adjoint)
+    src_all = exchange(src, SRC_AXES)
+    tgt_all = exchange(tgt, TGT_AXES)
+    row_part, col_part, mix = tile(tgt_all, src_all, patch_counts, patch_owner, block_lists)
+
+    mine = jnp.sum(exchange(row_part, TGT_AXES), axis=0)
+    _, row, quarter = device_place()
+    at_row = lax.broadcasted_iota(jnp.int32, col_part.shape, 0) == row
+    at_lane = lax.broadcasted_iota(jnp.int32, col_part.shape, 1) // panels == quarter
+    col_part = col_part + jnp.where(at_row & at_lane, jnp.tile(mine, (1, BPAN // panels)), 0.0)
+    dens = jnp.sum(exchange(copies(col_part, NSRC), SRC_AXES), axis=0)
+    blocks = exchange(copies(dens, NTGT), TGT_AXES).reshape(NBLK, BPAN)
+
+    contrib, own = patch(mix, blocks, spline[0], panels)
+    rows = jnp.sum(exchange(contrib, TGT_AXES), axis=0)
+    low = PARTS["z_lo"]
+    rows = rows.reshape(low, 1, rows.shape[0] // low, rows.shape[1])
+    rows = jnp.broadcast_to(rows, (low, NSRC // low) + rows.shape[2:]).reshape((NSRC,) + rows.shape[2:])
+    patch_grad = jnp.sum(exchange(rows, SRC_AXES), axis=0)
+    return own.reshape(panels), patch_grad
 
 
 def solution(mesh):
-    nrow, ncol = mesh.shape["row"], mesh.shape["col"]
-
-    def on_device(
-        positions, normals, areas, direct, adjoint, spline, block_lists, patch_counts, patch_owner
-    ):
-        panels = positions.shape[1]
-        col = lax.axis_index("col")
-        holder = lax.axis_index("row") * ncol + col
-        patches = jnp.arange(NPATCH, dtype=jnp.int32)
-        before = patches[None, :] < patches[:, None]
-        starts = jnp.sum(jnp.where(before, patch_counts[None, :], 0), axis=1)
-        ends = starts + patch_counts
-        ids = jnp.arange(NBLK, dtype=jnp.int32)
-        inside = (starts[:, None] <= ids[None, :]) & (ids[None, :] < ends[:, None])
-        row_of = jnp.sum(jnp.where(inside, patch_owner[:, None], 0), axis=0)
-        listed = jnp.any(block_lists == holder, axis=1)
-        mix = ((row_of[None, :] == patches[:, None]) & listed[None, :]).astype(F32)
-
-        tgt, src = pack(positions, normals, areas, direct, adjoint)
-        tgt_all = spread(tgt, "col", ncol).reshape(ncol * panels, LANES)
-        src_all = spread(src, "row", nrow).reshape(nrow * panels, LANES)
-        row_part, col_part = tile(tgt_all, src_all)
-
-        mine = jnp.sum(exchange(col_part.reshape(nrow, 1, panels), "row"), axis=0)
-        per = BPAN // panels
-        at_row = lax.broadcasted_iota(jnp.int32, row_part.shape, 0) == col // per
-        at_lane = lax.broadcasted_iota(jnp.int32, row_part.shape, 1) // panels == col % per
-        row_part = row_part + jnp.where(at_row & at_lane, jnp.tile(mine, (1, per)), 0.0)
-        row_dens = jnp.sum(spread(row_part, "col", ncol), axis=0)
-        densities = lax.dynamic_slice(row_dens, (col // per, (col % per) * panels), (1, panels)).reshape(panels)
-        blocks = spread(row_dens, "row", nrow).reshape(NBLK, BPAN)
-
-        contrib = patch(mix, blocks, spline[0])
-        rows = NPATCH // nrow
-        partial = jnp.sum(exchange(contrib.reshape(nrow, rows, contrib.shape[1]), "row"), axis=0)
-        patch_grad = jnp.sum(spread(partial, "col", ncol), axis=0)
-        return densities, patch_grad
-
+    fine = Mesh(mesh.devices.reshape(tuple(PARTS.values())), NAMES)
     placed = (
-        P(None, ("row", "col")),
-        P(None, ("row", "col")),
-        P(("row", "col")),
-        P(("row", "col"), None),
-        P(("row", "col"), None),
-        P(("row", "col"), None, None),
+        P(None, NAMES),
+        P(None, NAMES),
+        P(NAMES),
+        P(NAMES, None),
+        P(NAMES, None),
+        P(NAMES, None, None),
         P(),
         P(),
         P(),
     )
     return jax.shard_map(
         on_device,
-        mesh=mesh,
+        mesh=fine,
         in_specs=placed,
-        out_specs=(P(("row", "col")), P("row", None)),
+        out_specs=(P(NAMES), P(("z_lo", "y", "core"), None)),
         check_vma=False,
     )

time: 151 us -> 145 us (0.960)
  blocking collectives: 38.1 us -> 76.9 us
  waiting for transfers between devices: 50.4 us -> 23.5 us
  starting transfers between devices: 28.9 us -> 15.9 us
  local copies, waits for them, and re-layouts: 6.22 us -> 0.87 us
  Pallas kernels: 24.1 us -> 26 us
    all_to_all x2 -> x5, blocking collectives: 38.1 us -> 76.9 us  [exchange(): return lax.all_to_all(pieces, axes, 0, 0, tiled=True)]
    all_to_all x5 -> x2, waiting for transfers between devices: 50.4 us -> 23.5 us  [exchange(): return lax.all_to_all(pieces, axes, 0, 0, tiled=True)]
    all_to_all x5 -> x2, starting transfers between devices: 28.9 us -> 15.9 us  [exchange(): return lax.all_to_all(pieces, axes, 0, 0, tiled=True)]
    broadcast_in_dim x5 -> x4, local copies, waits for them, and re-layouts: 3.59 us -> 0.09 us  [the longest x2 0.06 us: on_device(): jnp.broadcast_to(rows, (low, NSRC // low) + rows.shape[2:])]
    pallas_call x3, Pallas kernels: 24.1 us -> 26 us  [the longest x1 23.3 us: tile(): pl.pallas_call(tile_kernel, out_shape=(jax.ShapeDtypeStruct((pieces, 1, p...]
  transfers between devices with their start and end apart: 5 -> 2, of which waited for: 5 -> 2; matrix products, arithmetic and copies ran while one was open for 1% -> 0% of each run, Pallas kernels for 0% -> 0%
where the time goes in v2:
time: 145 us
  blocking collectives  76.9 us (53%)
  Pallas kernels  26 us (18%)
  waiting for transfers between devices  23.5 us (16%)
  starting transfers between devices  15.9 us (11%)
    all_to_all x5, blocking collectives, exchange(): return lax.all_to_all(pieces, axes, 0, 0, tiled=True)  76.9 us
    all_to_all x2, waiting for transfers between devices, exchange(): return lax.all_to_all(pieces, axes, 0, 0, tiled=True)  23.5 us
    pallas_call x1, Pallas kernels, tile(): pl.pallas_call(tile_kernel, out_shape=(jax.ShapeDtypeStruct((pieces, 1, p...  23.3 us
    all_to_all x2, starting transfers between devices, exchange(): return lax.all_to_all(pieces, axes, 0, 0, tiled=True)  15.9 us
  transfers between devices with their start and end apart: 2, of which 2 were waited for; matrix products, arithmetic and copies ran while one was open for 0% of the time, Pallas kernels for 0%

profile of v2, /device:TPU:1, one launch (start us, length us, event | category | flops | bytes accessed | tf_op | source)
XLA Modules:
  0.0 144.8 jit_solution(354637183551218836)
XLA Ops:
  0.6 1.9 %pack.1 = (bf16[16,64,128]{2,1,0:T(8,128)(2,1)}, bf16[32,64,128]{2,1,0:T(8,128)(2,1)}) custom-call(f32[3,64]{1,0:T(4,128)} %pos_ref.1, f32[3,64]{1,0:T(4,128)} %nrm_ref.1, f32[1,64]{1,0:T(1,128)} %bitcast.18, bf16[64,64]{1,0:T(8,128)(2,1)} %dir_ref.1, bf16[64,64]{1,0:T(8,128)(2,1)} %adj_ref.1), custom_call_target="tpu_custom_call" | custom-call | tf_op jit(solution)/shard_map/pack/pallas_call | solution.py:93
  2.5 22.0 %all_to_all.35 = bf16[16,64,128]{2,1,0:T(8,128)(2,1)S(1)} all-to-all(bf16[16,64,128]{2,1,0:T(8,128)(2,1)} %get-tuple-element.9), channel_id=1, replica_groups=mesh['z_lo'=2,'y'=8,'core'=2,'x'=4,'z_hi'=4] {'y','core'}, dimensions={0} | all-to-all | bytes 524288 | tf_op jit(solution)/shard_map/all_to_all | solution.py:289
  24.6 11.2 %all-to-all-start.1 = ((bf16[32,64,128]{2,1,0:T(8,128)(2,1)}), bf16[32,64,128]{2,1,0:T(8,128)(2,1)S(1)}, u32[]{:S(2)}, u32[]{:S(2)}) async-start(bf16[32,64,128]{2,1,0:T(8,128)(2,1)} %get-tuple-element.10), calls=%async_computation.1 | async-start | bytes 1048576 | tf_op jit(solution)/shard_map/all_to_all | solution.py:289
  35.8 16.5 %all-to-all-done.1 = bf16[32,64,128]{2,1,0:T(8,128)(2,1)S(1)} async-done(((bf16[32,64,128]{2,1,0:T(8,128)(2,1)}), bf16[32,64,128]{2,1,0:T(8,128)(2,1)S(1)}, u32[]{:S(2)}, u32[]{:S(2)}) %all-to-all-start.1) | async-done | bytes 524320 | tf_op jit(solution)/shard_map/all_to_all | solution.py:289
  52.2 0.0 copy-start.1
  52.2 0.0 copy-start.2
  52.2 0.0 copy-start.3
  52.2 0.7 copy-done.1
  52.9 0.0 copy-done.2
  52.9 0.0 copy-done.3
  52.9 23.3 %tile.12 = (f32[16,1,64]{2,1,0:T(1,128)}, f32[8,256]{1,0:T(8,128)S(1)}, bf16[64,128]{1,0:T(8,128)(2,1)S(1)}) custom-call(bf16[1024,128]{1,0:T(8,128)(2,1)S(1)} %bitcast.11, bf16[2048,128]{1,0:T(8,128)(2,1)S(1)} %bitcast.10, s32[1,64]{1,0:T(1,128)S(1)} %bitcast.15, s32[1,64]{1,0:T(1,128)S(1)} %bitcast.16, s32[4,128]{1,0:T(4,128)S(1)} %bitcast.14), custom_call_target="tpu_custom_call" | custom-call | tf_op jit(solution)/shard_map/tile/pallas_call | solution.py:232
  76.3 4.7 %all-to-all-start.2 = ((f32[16,1,64]{2,1,0:T(1,128)}), f32[16,1,64]{2,1,0:T(1,128)S(1)}, u32[]{:S(2)}, u32[]{:S(2)}) async-start(f32[16,1,64]{2,1,0:T(1,128)} %get-tuple-element.13), calls=%async_computation.2 | async-start | bytes 16384 | tf_op jit(solution)/shard_map/all_to_all | solution.py:289
  81.0 7.1 %all-to-all-done.2 = f32[16,1,64]{2,1,0:T(1,128)S(1)} async-done(((f32[16,1,64]{2,1,0:T(1,128)}), f32[16,1,64]{2,1,0:T(1,128)S(1)}, u32[]{:S(2)}, u32[]{:S(2)}) %all-to-all-start.2) | async-done | bytes 4128 | tf_op jit(solution)/shard_map/all_to_all | solution.py:289
  88.1 0.1 tile.11
  88.2 0.1 select_add_fusion
  88.3 14.6 %all_to_all.36 = f32[32,8,256]{2,1,0:T(8,128)S(1)} all-to-all(f32[32,8,256]{2,1,0:T(8,128)S(1)} %broadcast_in_dim.33), channel_id=1, replica_groups=mesh['z_lo'=2,'y'=8,'core'=2,'x'=4,'z_hi'=4] {'z_lo','x','z_hi'}, dimensions={0} | all-to-all | bytes 524288 | tf_op jit(solution)/shard_map/all_to_all | solution.py:289
  102.9 0.0 copy-start
  103.0 15.2 %all_to_all.37 = f32[16,8,256]{2,1,0:T(8,128)S(1)} all-to-all(f32[16,8,256]{2,1,0:T(8,128)S(1)} %broadcast_in_dim.34), channel_id=1, replica_groups=mesh['z_lo'=2,'y'=8,'core'=2,'x'=4,'z_hi'=4] {'y','core'}, dimensions={0} | all-to-all | bytes 262144 | tf_op jit(solution)/shard_map/all_to_all | solution.py:289
  118.2 0.0 copy-done
  118.2 0.8 patch.1
  119.0 11.6 %all_to_all.38 = f32[16,4,512]{2,1,0:T(4,128)S(1)} all-to-all(f32[16,4,512]{2,1,0:T(4,128)S(1)} %get-tuple-element.15), channel_id=1, replica_groups=mesh['z_lo'=2,'y'=8,'core'=2,'x'=4,'z_hi'=4] {'y','core'}, dimensions={0} | all-to-all | bytes 262144 | tf_op jit(solution)/shard_map/all_to_all | solution.py:289
  130.7 13.4 %all_to_all.39 = f32[32,2,512]{2,1,0:T(2,128)S(1)} all-to-all(f32[32,2,512]{2,1,0:T(2,128)S(1)} %bitcast.17), channel_id=1, replica_groups=mesh['z_lo'=2,'y'=8,'core'=2,'x'=4,'z_hi'=4] {'z_lo','x','z_hi'}, dimensions={0} | all-to-all | bytes 262144 | tf_op jit(solution)/shard_map/all_to_all | solution.py:289
  144.1 0.7 reduce_sum.39
  (11 shorter events, 0.2 us)
Async XLA Ops:
  24.6 27.7 %all-to-all-start.1 = ((bf16[32,64,128]{2,1,0:T(8,128)(2,1)}), bf16[32,64,128]{2,1,0:T(8,128)(2,1)S(1)}, u32[]{:S(2)}, u32[]{:S(2)}) async-start(bf16[32,64,128]{2,1,0:T(8,128)(2,1)} %get-tuple-element.10), calls=%async_computation.1 | async-start | bytes 1048576 | tf_op jit(solution)/shard_map/all_to_all | solution.py:289
  52.2 0.7 copy-start.1
  52.2 0.7 copy-start.2
  52.2 0.7 copy-start.3
  76.3 11.8 %all-to-all-start.2 = ((f32[16,1,64]{2,1,0:T(1,128)}), f32[16,1,64]{2,1,0:T(1,128)S(1)}, u32[]{:S(2)}, u32[]{:S(2)}) async-start(f32[16,1,64]{2,1,0:T(1,128)} %get-tuple-element.13), calls=%async_computation.2 | async-start | bytes 16384 | tf_op jit(solution)/shard_map/all_to_all | solution.py:289
  102.9 15.3 %copy-start = (bf16[1,256,512]{2,1,0:T(8,128)(2,1)S(1)}, bf16[1,256,512]{2,1,0:T(8,128)(2,1)}, u32[]{:S(2)}) copy-start(bf16[1,256,512]{2,1,0:T(8,128)(2,1)} %param.14) | copy-start | bytes 786436

commit v3 on v2

v3 whole, which is shorter than its diff:
```python
import jax
import jax.numpy as jnp
import numpy as np
from jax import lax
from jax.experimental import pallas as pl
from jax.experimental.pallas import tpu as pltpu
from jax.sharding import Mesh
from jax.sharding import PartitionSpec as P

F32 = jnp.float32
BF16 = jnp.bfloat16
BPAN = 256
NPATCH = 64
NBLK = 128
LANES = 128
wave_number = 6.0
inv_four_pi = 0.07957747154594767

TURNS = wave_number / (2.0 * np.pi)
DEGREE = 5


def cosine_coefficients():
    k = np.arange(64)
    nodes = 0.125 + 0.125 * np.cos(np.pi * (2 * k + 1) / 128)
    fit = np.polynomial.chebyshev.Chebyshev.fit(
        nodes, np.cos(2 * np.pi * np.sqrt(nodes)), DEGREE, domain=[0.0, 0.25]
    )
    return fit.convert(kind=np.polynomial.Polynomial).coef


COEF = cosine_coefficients()
LEAD = float(COEF[-1])
MONIC = [float(c / COEF[-1]) for c in COEF[:-1]]
ROUNDER = float(3 << 22)
AREA_SCALE = float(TURNS**2 * inv_four_pi)
WAVE_SCALE = float(2.0 * wave_number * inv_four_pi * LEAD)

PARTS = {"z_lo": 2, "y": 8, "core": 2, "x": 4, "z_hi": 4}
NAMES = tuple(PARTS)
TGT_AXES = ("y", "core")
SRC_AXES = ("z_lo", "x", "z_hi")
NTGT = PARTS["y"] * PARTS["core"]
NSRC = PARTS["z_lo"] * PARTS["x"] * PARTS["z_hi"]

COLS = 64
HALF = 32
DEPTH = 40
X, Y, Z = (0, 2, 4), (1, 3, 5), (8, 9, 10)
NX, NY, NZ = (6, 7), (11, 12), (13, 14, 15)
AREA = (11, 12, 13)


def split3(v):
    hi = v.astype(BF16)
    rest = v - hi.astype(F32)
    mid = rest.astype(BF16)
    lo = (rest - mid.astype(F32)).astype(BF16)
    return hi, mid, lo


def pack_kernel(pos_ref, nrm_ref, area_ref, dir_ref, adj_ref, tgt_ref, src_ref):
    pos = pos_ref[...]
    row = lax.broadcasted_iota(jnp.int32, pos.shape, 0)
    pos = jnp.where(row == 2, 0.5 * (pos - 1.2), pos) * TURNS
    p = [v.astype(F32) for v in split3(pos)]
    n = [v.astype(F32) for v in split3(nrm_ref[...])]
    a = [v.astype(F32) for v in split3(area_ref[...] * TURNS**2)]
    flat = [v[0:2] for v in p]
    deep = [v[2:3] for v in p]
    none = jnp.zeros((2, pos.shape[1]), F32)

    def lay(cols, left, right, ref):
        geo = jnp.concatenate([jnp.concatenate(left, axis=0), jnp.concatenate(right, axis=0)], axis=1)
        top = jnp.concatenate([cols[:HALF].astype(F32), cols[HALF:].astype(F32)], axis=1)
        piece = jnp.concatenate([top, geo], axis=0).astype(BF16)
        for k in range(ref.shape[0]):
            ref[k] = piece

    lay(adj_ref[...], flat + [v[0:1] for v in n[:2]], deep + [v[1:2] for v in n[:2]] + [v[2:3] for v in n], tgt_ref)
    lay(dir_ref[...], flat + [none], deep + a + [none], src_ref)


def pack(positions, normals, areas, direct, adjoint):
    panels = positions.shape[1]
    out = [jax.ShapeDtypeStruct((count, DEPTH, LANES), BF16) for count in (NTGT, NSRC)]
    return pl.pallas_call(pack_kernel, out_shape=out, name="pack")(
        positions, normals, areas.reshape(1, panels), direct, adjoint
    )


def unpack(ref, k, cols):
    geo = []
    for m in (k, k + 1):
        piece = ref[m].astype(F32)
        cols[m * COLS : m * COLS + HALF, :] = piece[:HALF, :COLS].astype(BF16)
        cols[m * COLS + HALF : (m + 1) * COLS, :] = piece[:HALF, COLS:].astype(BF16)
        geo.append(piece[HALF:])
    return (
        jnp.concatenate([geo[0][:, :COLS], geo[1][:, :COLS]], axis=1),
        jnp.concatenate([geo[0][:, COLS:], geo[1][:, COLS:]], axis=1),
    )


ROWS = 16
CHUNK = 256


def device_place():
    at = {name: lax.axis_index(name) for name in NAMES}
    rho = at["y"] * PARTS["core"] + at["core"]
    return rho, (at["z_lo"] * PARTS["x"] + at["x"]) * PARTS["z_hi"] + at["z_hi"]


def mix_rows(counts_ref, owner_ref, lists_ref, mix_ref):
    rho, gamma = device_place()
    nx, ncol = PARTS["x"], PARTS["x"] * PARTS["z_hi"]
    holder = ((gamma // ncol) * NTGT + rho) * ncol + gamma % ncol

    def iota(shape, dim):
        return lax.broadcasted_iota(jnp.int32, shape, dim)

    square = (NPATCH, NPATCH)
    counts = jnp.broadcast_to(counts_ref[...], square)
    eye = iota(square, 0) == iota(square, 1)
    starts = jnp.sum(jnp.where(iota(square, 1) < iota(square, 0), counts, 0).astype(F32), axis=1, keepdims=True)
    own_counts = jnp.sum(jnp.where(eye, counts, 0).astype(F32), axis=1, keepdims=True)
    lines = (NPATCH, NBLK)
    ids = iota(lines, 1).astype(F32)
    inside = (starts <= ids) & (ids < starts + own_counts)
    owner = jnp.broadcast_to(owner_ref[...], square)
    place = iota(square, 0)
    output = ((place % 4) // 2) * (2 * NTGT) + 2 * (place // 4) + place % 2
    owned = jnp.where(owner == output, 1.0, 0.0).astype(BF16)
    listed = jnp.max(jnp.where(lists_ref[...] == holder, 1.0, 0.0), axis=0, keepdims=True)
    member = jnp.where(inside, jnp.broadcast_to(listed, lines), 0.0).astype(BF16)
    by_block = jnp.dot(owned, member, preferred_element_type=F32).astype(BF16)
    cut = (NBLK, NBLK // 2)
    k = iota(cut, 1)
    for high in range(2):
        rho_k = high * 8 + k % 8
        block = (k // (8 * nx)) * (NTGT * nx) + rho_k * nx + (k // 8) % nx
        order = jnp.where(iota(cut, 0) == block, 1.0, 0.0).astype(BF16)
        part = jnp.dot(by_block, order, preferred_element_type=F32).astype(BF16)
        mix_ref[high * NPATCH : (high + 1) * NPATCH, :] = part


def tile_kernel(
    tgt_ref, src_ref, counts_ref, owner_ref, lists_ref, row_ref, col_ref, mix_ref, own_ref,
    tcols, scols, tgeo, sgeo, images, rowacc, colacc,
):
    mix_rows(counts_ref, owner_ref, lists_ref, mix_ref)
    rho, _ = device_place()
    at_row = lax.broadcasted_iota(jnp.int32, own_ref.shape, 0) == rho % 8
    at_lane = lax.broadcasted_iota(jnp.int32, own_ref.shape, 1) // COLS == rho // 8
    own_ref[...] = jnp.where(at_row & at_lane, 1.0, 0.0)
    targets, sources = tcols.shape[0], scols.shape[0]
    contract_first, contract_last = (((0,), (0,)), ((), ())), (((1,), (1,)), ((), ()))
    part = lax.broadcasted_iota(jnp.int32, (16, LANES), 0)
    chosen = []
    for parts in (X, Y, Z, NX, NY, NZ):
        hit = part == parts[0]
        for m in parts[1:]:
            hit = hit | (part == m)
        chosen.append(jnp.where(hit, 1.0, 0.0))
    chosen = jnp.concatenate(chosen, axis=1).astype(BF16)
    for g in range(targets // LANES):
        here = slice(g * LANES, (g + 1) * LANES)
        geo = jnp.concatenate(unpack(tgt_ref, 2 * g, tcols), axis=0).astype(BF16)
        wide = lax.dot_general(geo, chosen, contract_first, preferred_element_type=F32)
        for k in range(6):
            tgeo[k, here, :] = wide[:, k * LANES : (k + 1) * LANES]
        z, nz = wide[:, 2 * LANES : 3 * LANES], wide[:, 5 * LANES :]
        tgeo[6, here, :] = (WAVE_SCALE * nz) * jnp.exp((wave_number / TURNS) * z)
    for g in range(sources // LANES):
        here = slice(g * LANES, (g + 1) * LANES)
        left, right = unpack(src_ref, 2 * g, scols)

        def line(value, parts):
            a, b, c = (value[m % 8 : m % 8 + 1, :] for m in parts)
            return jnp.broadcast_to(a + b + c, (8, LANES))

        z, area = line(right, Z), line(right, AREA)
        sgeo[0, :, here] = line(left, X)
        sgeo[1, :, here] = line(left, Y)
        sgeo[2, :, here] = z
        sgeo[3, :, here] = area
        sgeo[4, :, here] = (area * (1.0 / TURNS**2)) * jnp.exp((wave_number / TURNS) * z)
        sgeo[5, :, here] = area * (AREA_SCALE / TURNS**2)
    rowacc[...] = jnp.zeros_like(rowacc)

    def chunk(j, _):
        s0 = pl.multiple_of(j * CHUNK, CHUNK)
        images[...] = lax.dot_general(
            tcols[...],
            scols[pl.ds(s0, CHUNK), :],
            contract_last,
            preferred_element_type=F32,
        )
        halves = range(CHUNK // LANES)

        def wide(k, h):
            v = sgeo[k, :, pl.ds(pl.multiple_of(s0 + h * LANES, LANES), LANES)]
            return jnp.concatenate([v] * (ROWS // 8), axis=0)

        src = [[wide(k, h) for k in range(6)] for h in halves]

        def step(i, acc):
            t0 = pl.multiple_of(i * ROWS, ROWS)
            xt, yt, zt, nx, ny, nz, amp = (tgeo[k, pl.ds(t0, ROWS), :] for k in range(7))
            zt4, nz2 = 4.0 * zt, 2.0 * nz
            new, total = [], rowacc[pl.ds(t0, ROWS), :]
            for h in halves:
                xs, ys, zs, area, ebb, share = src[h]
                dx, dy, dz = xt - xs, yt - ys, zt - zs
                flat = dx * dx + dy * dy + area
                near = flat + dz * dz
                mirror = near + zt4 * zs
                top = nx * dx + ny * dy + nz * dz
                topi = top + nz2 * zs
                i1, i2, i3 = lax.rsqrt(near), lax.rsqrt(mirror), lax.rsqrt(flat)
                pair = top * (i1 * i1 * i1) + topi * (i2 * i2 * i2)
                phase = flat * i3
                f = phase - ((phase + ROUNDER) - ROUNDER)
                g = f * f
                p = g + MONIC[-1]
                for c in MONIC[-2::-1]:
                    p = p * g + c
                kern = share * pair - (amp * ebb) * p
                w = kern.astype(BF16).astype(F32) * images[pl.ds(t0, ROWS), h * LANES : (h + 1) * LANES]
                new.append(acc[h] + w)
                total = total + w
            rowacc[pl.ds(t0, ROWS), :] = total
            return tuple(new)

        zero = jnp.zeros((ROWS, LANES), F32)
        acc = lax.fori_loop(0, targets // ROWS, step, (zero,) * len(halves), unroll=4)
        for h in halves:
            colacc[0:1, pl.ds(pl.multiple_of(s0 + h * LANES, LANES), LANES)] = jnp.sum(acc[h], axis=0, keepdims=True)
        return 0

    lax.fori_loop(0, sources // CHUNK, chunk, 0)
    panels = col_ref.shape[2]
    for k in range(col_ref.shape[0]):
        col_ref[k] = colacc[0:1, k * panels : (k + 1) * panels]
    for g in range(targets // LANES):
        line = jnp.sum(rowacc[g * LANES : (g + 1) * LANES, :].T, axis=0, keepdims=True)
        for k in range(2):
            low, high = (2 * g + k) % 8, (2 * g + k) // 8
            row_ref[low : low + 1, high * panels : (high + 1) * panels] = line[:, k * panels : (k + 1) * panels]


def tile(tgt, src, patch_counts, patch_owner, block_lists, panels):
    targets, sources = tgt.shape[0] * panels, src.shape[0] * panels
    return pl.pallas_call(
        tile_kernel,
        out_shape=(
            jax.ShapeDtypeStruct((8, LANES), F32),
            jax.ShapeDtypeStruct((src.shape[0], 1, panels), F32),
            jax.ShapeDtypeStruct((2 * NPATCH, NBLK // 2), BF16),
            jax.ShapeDtypeStruct((8, LANES), F32),
        ),
        scratch_shapes=[
            pltpu.VMEM((targets, COLS), BF16),
            pltpu.VMEM((sources, COLS), BF16),
            pltpu.VMEM((7, targets, LANES), F32),
            pltpu.VMEM((6, 8, sources), F32),
            pltpu.VMEM((targets, CHUNK), F32),
            pltpu.VMEM((targets, LANES), F32),
            pltpu.VMEM((1, sources), F32),
        ],
        compiler_params=pltpu.CompilerParams(vmem_limit_bytes=24 << 20),
        name="tile",
    )(tgt, src, patch_counts.reshape(1, NPATCH), patch_owner.reshape(1, NPATCH), block_lists.T)


def patch_kernel(mix_ref, dens_ref, spline_ref, out_ref, own_ref):
    quarters = PARTS["z_hi"]
    panels = own_ref.shape[1]
    dens = jnp.concatenate(
        [
            jnp.concatenate([dens_ref[k] for k in range(q, dens_ref.shape[0], quarters)], axis=0)
            for q in range(quarters)
        ],
        axis=1,
    )
    mix = mix_ref[...]
    both = sum(jnp.dot(mix, part, preferred_element_type=F32) for part in split3(dens)[::-1])
    got = jnp.concatenate(
        [
            both[:NPATCH, q * LANES : q * LANES + panels] + both[NPATCH:, q * LANES + panels : (q + 1) * LANES]
            for q in range(quarters)
        ],
        axis=1,
    )
    spline = spline_ref[...]
    rows = sum(jnp.dot(part, spline, preferred_element_type=F32) for part in split3(got)[::-1])
    depth = out_ref.shape[1]
    for piece in range(out_ref.shape[0]):
        out_ref[piece] = rows[piece * depth : (piece + 1) * depth]
    rho, gamma = device_place()
    line = dens_ref[gamma, pl.ds(rho % 8, 1), :]
    own_ref[...] = jnp.where(rho // 8 == 0, line[:, :panels], line[:, panels:])


def patch(mix, blocks, spline, panels):
    return pl.pallas_call(
        patch_kernel,
        out_shape=(
            jax.ShapeDtypeStruct((NTGT, NPATCH // NTGT, spline.shape[1]), F32),
            jax.ShapeDtypeStruct((1, panels), F32),
        ),
        compiler_params=pltpu.CompilerParams(vmem_limit_bytes=16 << 20),
        name="patch",
    )(mix, blocks, spline)


def exchange(pieces, axes):
    return lax.all_to_all(pieces, axes, 0, 0, tiled=True)


def copies(value, count):
    return jnp.broadcast_to(value[None], (count,) + value.shape)


def on_device(
    positions, normals, areas, direct, adjoint, spline, block_lists, patch_counts, patch_owner
):
    panels = positions.shape[1]
    tgt, src = pack(positions, normals, areas, direct, adjoint)
    src_all = exchange(src, SRC_AXES)
    tgt_all = exchange(tgt, TGT_AXES)
    row_part, col_part, mix, own_place = tile(tgt_all, src_all, patch_counts, patch_owner, block_lists, panels)

    mine = jnp.sum(exchange(col_part, SRC_AXES), axis=0)
    row_part = row_part + own_place * jnp.tile(mine, (1, 2))
    dens = jnp.sum(exchange(copies(row_part, NTGT), TGT_AXES), axis=0)
    blocks = exchange(copies(dens, NSRC), SRC_AXES)

    contrib, own = patch(mix, blocks, spline[0], panels)
    rows = jnp.sum(exchange(contrib, TGT_AXES), axis=0)
    low = PARTS["z_lo"]
    rows = rows.reshape(low, 1, rows.shape[0] // low, rows.shape[1])
    rows = jnp.broadcast_to(rows, (low, NSRC // low) + rows.shape[2:]).reshape((NSRC,) + rows.shape[2:])
    patch_grad = jnp.sum(exchange(rows, SRC_AXES), axis=0)
    return own.reshape(panels), patch_grad


def solution(mesh):
    fine = Mesh(mesh.devices.reshape(tuple(PARTS.values())), NAMES)
    placed = (
        P(None, NAMES),
        P(None, NAMES),
        P(NAMES),
        P(NAMES, None),
        P(NAMES, None),
        P(NAMES, None, None),
        P(),
        P(),
        P(),
    )
    return jax.shard_map(
        on_device,
        mesh=fine,
        in_specs=placed,
        out_specs=(P(NAMES), P(("z_lo", "y", "core"), None)),
        check_vma=False,
    )
```

time: 145 us -> 134 us (0.924)
  blocking collectives: 76.9 us -> 109 us
  waiting for transfers between devices: 23.5 us -> 0 us
  starting transfers between devices: 15.9 us -> 0 us
  Pallas kernels: 26 us -> 22 us
    all_to_all x5 -> x7, blocking collectives: 76.9 us -> 109 us  [exchange(): return lax.all_to_all(pieces, axes, 0, 0, tiled=True)]
    all_to_all x2 -> x0, waiting for transfers between devices: 23.5 us -> none  [exchange(): return lax.all_to_all(pieces, axes, 0, 0, tiled=True)]
    all_to_all x2 -> x0, starting transfers between devices: 15.9 us -> none  [exchange(): return lax.all_to_all(pieces, axes, 0, 0, tiled=True)]
    pallas_call x1, Pallas kernels: 23.3 us -> 19.4 us  [tile(): pl.pallas_call(tile_kernel, out_shape=(jax.ShapeDtypeStruct((8, LANES), F...]
  transfers between devices with their start and end apart: 2 -> 0, of which waited for: 2 -> 0; matrix products, arithmetic and copies ran while one was open for 0% -> 0% of each run, Pallas kernels for 0% -> 0%
where the time goes in v3:
time: 134 us; the launch traced here: 133 us
  blocking collectives  109 us (81%)
  Pallas kernels  22 us (16%)
    all_to_all x7, blocking collectives, exchange(): return lax.all_to_all(pieces, axes, 0, 0, tiled=True)  109 us
    pallas_call x1, Pallas kernels, tile(): pl.pallas_call(tile_kernel, out_shape=(jax.ShapeDtypeStruct((8, LANES), F...  19.4 us

profile of v3, /device:TPU:1, one launch (start us, length us, event | category | flops | bytes accessed | tf_op | source)
XLA Modules:
  0.0 133.1 jit_solution(15335114816645241580)
XLA Ops:
  0.6 1.7 %pack.1 = (bf16[16,40,128]{2,1,0:T(8,128)(2,1)}, bf16[32,40,128]{2,1,0:T(8,128)(2,1)}) custom-call(f32[3,64]{1,0:T(4,128)} %pos_ref.1, f32[3,64]{1,0:T(4,128)} %nrm_ref.1, f32[1,64]{1,0:T(1,128)} %bitcast.12, bf16[64,64]{1,0:T(8,128)(2,1)} %dir_ref.1, bf16[64,64]{1,0:T(8,128)(2,1)} %adj_ref.1), custom_call_target="tpu_custom_call" | custom-call | tf_op jit(solution)/shard_map/pack/pallas_call | solution.py:87
  2.3 0.0 copy-start.4
  2.3 20.2 %all_to_all.35.tgt_ref = bf16[16,40,128]{2,1,0:T(8,128)(2,1)S(1)} all-to-all(bf16[16,40,128]{2,1,0:T(8,128)(2,1)} %get-tuple-element.10), channel_id=1, replica_groups=mesh['z_lo'=2,'y'=8,'core'=2,'x'=4,'z_hi'=4] {'y','core'}, dimensions={0} | all-to-all | bytes 327680 | tf_op jit(solution)/shard_map/all_to_all | solution.py:319
  22.5 0.0 copy-done.4
  22.5 23.5 %all_to_all.36.src_ref = bf16[32,40,128]{2,1,0:T(8,128)(2,1)S(1)} all-to-all(bf16[32,40,128]{2,1,0:T(8,128)(2,1)S(1)} %copy-done.4), channel_id=1, replica_groups=mesh['z_lo'=2,'y'=8,'core'=2,'x'=4,'z_hi'=4] {'z_lo','x','z_hi'}, dimensions={0} | all-to-all | bytes 655360 | tf_op jit(solution)/shard_map/all_to_all | solution.py:319
  46.0 0.0 copy-start.1
  46.0 0.0 copy-start.2
  46.0 0.0 copy-start.3
  46.0 0.7 copy-done.1
  46.7 0.0 copy-done.2
  46.7 0.0 copy-done.3
  46.7 19.4 %tile.12 = (f32[8,128]{1,0:T(8,128)S(1)}, f32[32,1,64]{2,1,0:T(1,128)S(1)}, bf16[128,64]{1,0:T(8,128)(2,1)S(1)}, f32[8,128]{1,0:T(8,128)S(1)}) custom-call(bf16[16,40,128]{2,1,0:T(8,128)(2,1)S(1)} %all_to_all.35.tgt_ref, bf16[32,40,128]{2,1,0:T(8,128)(2,1)S(1)} %all_to_all.36.src_ref, s32[1,64]{1,0:T(1,128)S(1)} %bitcast.9, s32[1,64]{1,0:T(1,128)S(1)} %bitcast.10, ...), custom_call_target="tpu_custom_call" | custom-call | tf_op jit(solution)/shard_map/tile/pallas_call | solution.py:255
  66.1 13.6 %all_to_all.37 = f32[32,1,64]{2,1,0:T(1,128)S(1)} all-to-all(f32[32,1,64]{2,1,0:T(1,128)S(1)} %get-tuple-element.15), channel_id=1, replica_groups=mesh['z_lo'=2,'y'=8,'core'=2,'x'=4,'z_hi'=4] {'z_lo','x','z_hi'}, dimensions={0} | all-to-all | bytes 16384 | tf_op jit(solution)/shard_map/all_to_all | solution.py:319
  79.6 0.1 reduce_sum.36
  79.7 0.1 tile.11
  79.8 12.5 %all_to_all.38 = f32[16,8,128]{2,1,0:T(8,128)S(1)} all-to-all(f32[16,8,128]{2,1,0:T(8,128)S(1)} %broadcast_in_dim.8), channel_id=1, replica_groups=mesh['z_lo'=2,'y'=8,'core'=2,'x'=4,'z_hi'=4] {'y','core'}, dimensions={0} | all-to-all | bytes 131072 | tf_op jit(solution)/shard_map/all_to_all | solution.py:319
  92.3 0.0 copy-start
  92.3 12.8 %all_to_all.39.dens_ref = f32[32,8,128]{2,1,0:T(8,128)S(1)} all-to-all(f32[32,8,128]{2,1,0:T(8,128)S(1)} %broadcast_in_dim.9), channel_id=1, replica_groups=mesh['z_lo'=2,'y'=8,'core'=2,'x'=4,'z_hi'=4] {'z_lo','x','z_hi'}, dimensions={0} | all-to-all | bytes 262144 | tf_op jit(solution)/shard_map/all_to_all | solution.py:319
  105.1 0.0 copy-done
  105.1 1.0 patch.1
  106.1 12.9 %all_to_all.40 = f32[16,4,512]{2,1,0:T(4,128)S(1)} all-to-all(f32[16,4,512]{2,1,0:T(4,128)S(1)} %get-tuple-element.17), channel_id=1, replica_groups=mesh['z_lo'=2,'y'=8,'core'=2,'x'=4,'z_hi'=4] {'y','core'}, dimensions={0} | all-to-all | bytes 262144 | tf_op jit(solution)/shard_map/all_to_all | solution.py:319
  119.1 13.3 %all_to_all.41 = f32[32,2,512]{2,1,0:T(2,128)S(1)} all-to-all(f32[32,2,512]{2,1,0:T(2,128)S(1)} %bitcast.11), channel_id=1, replica_groups=mesh['z_lo'=2,'y'=8,'core'=2,'x'=4,'z_hi'=4] {'z_lo','x','z_hi'}, dimensions={0} | all-to-all | bytes 262144 | tf_op jit(solution)/shard_map/all_to_all | solution.py:319
  132.4 0.7 reduce_sum.39
  (8 shorter events, 0.1 us)
Async XLA Ops:
  2.3 20.2 %copy-start.4 = (bf16[32,40,128]{2,1,0:T(8,128)(2,1)S(1)}, bf16[32,40,128]{2,1,0:T(8,128)(2,1)}, u32[]{:S(2)}) copy-start(bf16[32,40,128]{2,1,0:T(8,128)(2,1)} %get-tuple-element.11) | copy-start | bytes 983044
  46.0 0.7 copy-start.1
  46.0 0.7 copy-start.2
  46.0 0.7 copy-start.3
  92.3 12.8 %copy-start = (bf16[1,256,512]{2,1,0:T(8,128)(2,1)S(1)}, bf16[1,256,512]{2,1,0:T(8,128)(2,1)}, u32[]{:S(2)}) copy-start(bf16[1,256,512]{2,1,0:T(8,128)(2,1)} %param.14) | copy-start | bytes 786436

commit v4 on v3

--- a/solution.py
+++ b/solution.py
@@ -47,8 +47,53 @@
 HALF = 32
 DEPTH = 40
 X, Y, Z = (0, 2, 4), (1, 3, 5), (8, 9, 10)
-NX, NY, NZ = (6, 7), (11, 12), (13, 14, 15)
+NX, NY, NZ = (6, 7), (11, 12), (13, 14)
 AREA = (11, 12, 13)
+
+T_DOT, T_AMP, T_SQUARE, T_ONE, T_ROWS = 16, 19, 22, 25, 32
+S_MOMENT, S_SHARE, S_SQUARE, S_ONE, S_ROWS = 16, 25, 28, 31, 32
+
+
+def product_lanes():
+    left, right = [], [{}, {}, {}]
+    for d, n in enumerate((NX, NY, NZ)):
+        for a in range(2):
+            for b in range(3):
+                lane = len(left)
+                left.append(n[a])
+                right[0][lane] = (S_MOMENT + 3 * d + b, -1.0)
+                right[1][lane] = (S_MOMENT + 3 * d + b, 1.0 if d == 2 else -1.0)
+    for a in range(3):
+        for b in range(3):
+            lane = len(left)
+            left.append(T_DOT + a)
+            right[0][lane] = right[1][lane] = (S_SHARE + b, 1.0)
+    for d, p in enumerate((X, Y, Z)):
+        for a in range(3):
+            for b in range(3):
+                right[2][len(left)] = (p[b], 2.0 if d == 2 else -2.0)
+                left.append(p[a])
+    for a in range(3):
+        right[2][len(left)] = (S_ONE, 1.0)
+        left.append(T_SQUARE + a)
+    for b in range(3):
+        right[2][len(left)] = (S_SQUARE + b, 1.0)
+        left.append(T_ONE)
+    return dict(enumerate(left)), right
+
+
+LEFT, RIGHT = product_lanes()
+
+
+def selector(rows, entries):
+    lane = lax.broadcasted_iota(jnp.int32, (8, LANES), 1)
+    where, value = jnp.full((8, LANES), -1, jnp.int32), jnp.zeros((8, LANES), F32)
+    for key, (row, sign) in entries.items():
+        where = jnp.where(lane == key, row, where)
+        value = jnp.where(lane == key, sign, value)
+    at = lax.broadcasted_iota(jnp.int32, (rows, LANES), 0)
+    many = (rows // 8, 1)
+    return jnp.where(at == jnp.tile(where, many), jnp.tile(value, many), 0.0)
 
 
 def split3(v):
@@ -70,15 +115,116 @@
     deep = [v[2:3] for v in p]
     none = jnp.zeros((2, pos.shape[1]), F32)
 
-    def lay(cols, left, right, ref):
+    def lay(top, left, right, ref):
         geo = jnp.concatenate([jnp.concatenate(left, axis=0), jnp.concatenate(right, axis=0)], axis=1)
-        top = jnp.concatenate([cols[:HALF].astype(F32), cols[HALF:].astype(F32)], axis=1)
+        top = jnp.concatenate([top[:HALF], top[HALF:]], axis=1)
         piece = jnp.concatenate([top, geo], axis=0).astype(BF16)
         for k in range(ref.shape[0]):
             ref[k] = piece
 
-    lay(adj_ref[...], flat + [v[0:1] for v in n[:2]], deep + [v[1:2] for v in n[:2]] + [v[2:3] for v in n], tgt_ref)
-    lay(dir_ref[...], flat + [none], deep + a + [none], src_ref)
+    nx, ny, nz = ([v[k : k + 1] for v in n[:2]] for k in range(3))
+    lay(adj_ref[...].astype(F32), flat + nx, deep + ny + nz + [none[:1]], tgt_ref)
+    lay(dir_ref[...].astype(F32).T, flat + [none], deep + a + [none], src_ref)
+
+
+def pack(positions, normals, areas, direct, adjoint):
+    panels = positions.shape[1]
+    out = [jax.ShapeDtypeStruct((count, DEPTH, LANES), BF16) for count in (NTGT, NSRC)]
+    return pl.pallas_call(pack_kernel, out_shape=out, name="pack")(
+        positions, normals, areas.reshape(1, panels), direct, adjoint
+    )
+
+
+def beside(a, b):
+    return (
+        jnp.concatenate([a[:, :COLS], b[:, :COLS]], axis=1),
+        jnp.concatenate([a[:, COLS:], b[:, COLS:]], axis=1),
+    )
+
+
+def total(value, parts):
+    return sum(value[m : m + 1, :] for m in parts)
+
+
+def three(v):
+    return [part.astype(F32) for part in split3(v)]
+
+
+ROWS = 16, 19, 22, 25, 32
+S_MOMENT, S_SHARE, S_SQUARE, S_ONE, S_ROWS = 16, 25, 28, 31, 32
+
+
+def product_lanes():
+    left, right = [], [{}, {}, {}]
+    for d, n in enumerate((NX, NY, NZ)):
+        for a in range(2):
+            for b in range(3):
+                lane = len(left)
+                left.append(n[a])
+                right[0][lane] = (S_MOMENT + 3 * d + b, -1.0)
+                right[1][lane] = (S_MOMENT + 3 * d + b, 1.0 if d == 2 else -1.0)
+    for a in range(3):
+        for b in range(3):
+            lane = len(left)
+            left.append(T_DOT + a)
+            right[0][lane] = right[1][lane] = (S_SHARE + b, 1.0)
+    for d, p in enumerate((X, Y, Z)):
+        for a in range(3):
+            for b in range(3):
+                right[2][len(left)] = (p[b], 2.0 if d == 2 else -2.0)
+                left.append(p[a])
+    for a in range(3):
+        right[2][len(left)] = (S_ONE, 1.0)
+        left.append(T_SQUARE + a)
+    for b in range(3):
+        right[2][len(left)] = (S_SQUARE + b, 1.0)
+        left.append(T_ONE)
+    return dict(enumerate(left)), right
+
+
+LEFT, RIGHT = product_lanes()
+
+
+def selector(rows, entries):
+    lane = lax.broadcasted_iota(jnp.int32, (8, LANES), 1)
+    where, value = jnp.full((8, LANES), -1, jnp.int32), jnp.zeros((8, LANES), F32)
+    for key, (row, sign) in entries.items():
+        where = jnp.where(lane == key, row, where)
+        value = jnp.where(lane == key, sign, value)
+    at = lax.broadcasted_iota(jnp.int32, (rows, LANES), 0)
+    many = (rows // 8, 1)
+    return jnp.where(at == jnp.tile(where, many), jnp.tile(value, many), 0.0)
+
+
+def split3(v):
+    hi = v.astype(BF16)
+    rest = v - hi.astype(F32)
+    mid = rest.astype(BF16)
+    lo = (rest - mid.astype(F32)).astype(BF16)
+    return hi, mid, lo
+
+
+def pack_kernel(pos_ref, nrm_ref, area_ref, dir_ref, adj_ref, tgt_ref, src_ref):
+    pos = pos_ref[...]
+    row = lax.broadcasted_iota(jnp.int32, pos.shape, 0)
+    pos = jnp.where(row == 2, 0.5 * (pos - 1.2), pos) * TURNS
+    p = [v.astype(F32) for v in split3(pos)]
+    n = [v.astype(F32) for v in split3(nrm_ref[...])]
+    a = [v.astype(F32) for v in split3(area_ref[...] * TURNS**2)]
+    flat = [v[0:2] for v in p]
+    deep = [v[2:3] for v in p]
+    none = jnp.zeros((2, pos.shape[1]), F32)
+
+    def lay(top, left, right, ref):
+        geo = jnp.concatenate([jnp.concatenate(left, axis=0), jnp.concatenate(right, axis=0)], axis=1)
+        top = jnp.concatenate([top[:HALF], top[HALF:]], axis=1)
+        piece = jnp.concatenate([top, geo], axis=0).astype(BF16)
+        for k in range(ref.shape[0]):
+            ref[k] = piece
+
+    nx, ny, nz = ([v[k : k + 1] for v in n[:2]] for k in range(3))
+    lay(adj_ref[...].astype(F32), flat + nx, deep + ny + nz + [none[:1]], tgt_ref)
+    lay(dir_ref[...].astype(F32).T, flat + [none], deep + a + [none], src_ref)
 
 
 def pack(positions, normals, areas, direct, adjoint):
@@ -104,6 +250,7 @@
 
 ROWS = 16
 CHUNK = 256
+STEP = 256
 
 
 def device_place():
@@ -147,77 +294,86 @@
 
 def tile_kernel(
     tgt_ref, src_ref, counts_ref, owner_ref, lists_ref, row_ref, col_ref, mix_ref, own_ref,
-    tcols, scols, tgeo, sgeo, images, rowacc, colacc,
+    tcols, scols, tfeat, sfeat, tgeo, sgeo, even, odd, rowacc, colacc,
 ):
     mix_rows(counts_ref, owner_ref, lists_ref, mix_ref)
     rho, _ = device_place()
     at_row = lax.broadcasted_iota(jnp.int32, own_ref.shape, 0) == rho % 8
     at_lane = lax.broadcasted_iota(jnp.int32, own_ref.shape, 1) // COLS == rho // 8
     own_ref[...] = jnp.where(at_row & at_lane, 1.0, 0.0)
-    targets, sources = tcols.shape[0], scols.shape[0]
-    contract_first, contract_last = (((0,), (0,)), ((), ())), (((1,), (1,)), ((), ()))
-    part = lax.broadcasted_iota(jnp.int32, (16, LANES), 0)
-    chosen = []
-    for parts in (X, Y, Z, NX, NY, NZ):
-        hit = part == parts[0]
-        for m in parts[1:]:
-            hit = hit | (part == m)
-        chosen.append(jnp.where(hit, 1.0, 0.0))
+    targets, sources = tcols.shape[0], scols.shape[1]
+    scale = wave_number / TURNS
+
+    part = lax.broadcasted_iota(jnp.int32, (T_ROWS, LANES), 0)
+    chosen = [selector(T_ROWS, {lane: (row, 1.0) for lane, row in LEFT.items()})]
+    for parts in (X, Y, Z, tuple(range(T_AMP, T_AMP + 3))):
+        chosen.append(jnp.where((part == parts[0]) | (part == parts[1]) | (part == parts[2]), 1.0, 0.0))
     chosen = jnp.concatenate(chosen, axis=1).astype(BF16)
     for g in range(targets // LANES):
         here = slice(g * LANES, (g + 1) * LANES)
-        geo = jnp.concatenate(unpack(tgt_ref, 2 * g, tcols), axis=0).astype(BF16)
-        wide = lax.dot_general(geo, chosen, contract_first, preferred_element_type=F32)
-        for k in range(6):
-            tgeo[k, here, :] = wide[:, k * LANES : (k + 1) * LANES]
-        z, nz = wide[:, 2 * LANES : 3 * LANES], wide[:, 5 * LANES :]
-        tgeo[6, here, :] = (WAVE_SCALE * nz) * jnp.exp((wave_number / TURNS) * z)
+        pieces = [tgt_ref[m].astype(F32) for m in (2 * g, 2 * g + 1)]
+        for m, piece in enumerate(pieces):
+            row = g * LANES + m * COLS
+            tcols[row : row + HALF, :] = piece[:HALF, :COLS].astype(BF16)
+            tcols[row + HALF : row + COLS, :] = piece[:HALF, COLS:].astype(BF16)
+        geo = jnp.concatenate(beside(*(p[HALF:] for p in pieces)), axis=0)
+        x, y, z, nx, ny, nz = (total(geo, parts) for parts in (X, Y, Z, NX, NY, NZ))
+        rows = three(nx * x + ny * y + nz * z) + three((WAVE_SCALE * nz) * jnp.exp(scale * z)) + three(x * x + y * y + z * z)
+        rows = [geo] + rows + [jnp.ones_like(x), jnp.zeros((T_ROWS - T_ONE - 1, LANES), F32)]
+        wide = lax.dot_general(
+            jnp.concatenate(rows, axis=0).astype(BF16), chosen, (((0,), (0,)), ((), ())), preferred_element_type=F32
+        )
+        tfeat[here, :] = wide[:, :LANES].astype(BF16)
+        for k in range(4):
+            tgeo[k, here, :] = wide[:, (k + 1) * LANES : (k + 2) * LANES]
+    rights = [selector(S_ROWS, entries).T.astype(BF16) for entries in RIGHT]
     for g in range(sources // LANES):
         here = slice(g * LANES, (g + 1) * LANES)
-        left, right = unpack(src_ref, 2 * g, scols)
-
-        def line(value, parts):
-            a, b, c = (value[m % 8 : m % 8 + 1, :] for m in parts)
-            return jnp.broadcast_to(a + b + c, (8, LANES))
-
-        z, area = line(right, Z), line(right, AREA)
-        sgeo[0, :, here] = line(left, X)
-        sgeo[1, :, here] = line(left, Y)
-        sgeo[2, :, here] = z
-        sgeo[3, :, here] = area
-        sgeo[4, :, here] = (area * (1.0 / TURNS**2)) * jnp.exp((wave_number / TURNS) * z)
-        sgeo[5, :, here] = area * (AREA_SCALE / TURNS**2)
+        left, right = beside(*(src_ref[m].astype(F32) for m in (2 * g, 2 * g + 1)))
+        scols[:HALF, here] = left[:HALF].astype(BF16)
+        scols[HALF:, here] = right[:HALF].astype(BF16)
+        geo = jnp.concatenate([left[HALF:], right[HALF:]], axis=0)
+        x, y, z, area = (total(geo, parts) for parts in (X, Y, Z, AREA))
+        share = area * (AREA_SCALE / TURNS**2)
+        rows = three(share * x) + three(share * y) + three(share * z) + three(share)
+        rows += three(x * x + y * y + z * z + area)
+        rows = jnp.concatenate([geo] + rows + [jnp.ones_like(x)], axis=0).astype(BF16)
+        for k in range(3):
+            sfeat[k, :, here] = jnp.dot(rights[k], rows, preferred_element_type=F32).astype(BF16)
+        for k, v in enumerate((x, y, z, area, (area * (1.0 / TURNS**2)) * jnp.exp(scale * z))):
+            sgeo[k, :, here] = jnp.broadcast_to(v, (8, LANES))
     rowacc[...] = jnp.zeros_like(rowacc)
-
-    def chunk(j, _):
-        s0 = pl.multiple_of(j * CHUNK, CHUNK)
-        images[...] = lax.dot_general(
-            tcols[...],
-            scols[pl.ds(s0, CHUNK), :],
-            contract_last,
-            preferred_element_type=F32,
-        )
-        halves = range(CHUNK // LANES)
-
-        def wide(k, h):
-            v = sgeo[k, :, pl.ds(pl.multiple_of(s0 + h * LANES, LANES), LANES)]
-            return jnp.concatenate([v] * (ROWS // 8), axis=0)
-
-        src = [[wide(k, h) for k in range(6)] for h in halves]
-
-        def step(i, acc):
-            t0 = pl.multiple_of(i * ROWS, ROWS)
-            xt, yt, zt, nx, ny, nz, amp = (tgeo[k, pl.ds(t0, ROWS), :] for k in range(7))
-            zt4, nz2 = 4.0 * zt, 2.0 * nz
-            new, total = [], rowacc[pl.ds(t0, ROWS), :]
+    colacc[...] = jnp.zeros_like(colacc)
+    blocks = targets // STEP
+    steps = blocks * (sources // CHUNK)
+
+    def corner(k):
+        return pl.multiple_of(lax.rem(k, blocks) * STEP, STEP), pl.multiple_of(lax.div(k, blocks) * CHUNK, CHUNK)
+
+    def products(k, into):
+        t0, s0 = corner(k)
+        features = tfeat[pl.ds(t0, STEP), :]
+        for m in range(3):
+            into[m] = jnp.dot(features, sfeat[m, :, pl.ds(s0, CHUNK)], preferred_element_type=F32)
+        into[3] = jnp.dot(tcols[pl.ds(t0, STEP), :], scols[:, pl.ds(s0, CHUNK)], preferred_element_type=F32)
+
+    halves = range(CHUNK // LANES)
+
+    def elements(k, made):
+        t0, s0 = corner(k)
+        lanes = [pl.ds(pl.multiple_of(s0 + h * LANES, LANES), LANES) for h in halves]
+        src = [[jnp.concatenate([sgeo[m, :, lanes[h]]] * (ROWS // 8), axis=0) for m in range(5)] for h in halves]
+        acc = [None for _ in halves]
+        for r in range(0, STEP, ROWS):
+            rows = pl.ds(pl.multiple_of(t0 + r, ROWS), ROWS)
+            xt, yt, zt, amp = (tgeo[m, rows, :] for m in range(4))
+            along = rowacc[rows, :]
             for h in halves:
-                xs, ys, zs, area, ebb, share = src[h]
+                top, topi, mirror, image = (made[m, r : r + ROWS, h * LANES : (h + 1) * LANES] for m in range(4))
+                xs, ys, zs, area, ebb = src[h]
                 dx, dy, dz = xt - xs, yt - ys, zt - zs
                 flat = dx * dx + dy * dy + area
                 near = flat + dz * dz
-                mirror = near + zt4 * zs
-                top = nx * dx + ny * dy + nz * dz
-                topi = top + nz2 * zs
                 i1, i2, i3 = lax.rsqrt(near), lax.rsqrt(mirror), lax.rsqrt(flat)
                 pair = top * (i1 * i1 * i1) + topi * (i2 * i2 * i2)
                 phase = flat * i3
@@ -226,20 +382,27 @@
                 p = g + MONIC[-1]
                 for c in MONIC[-2::-1]:
                     p = p * g + c
-                kern = share * pair - (amp * ebb) * p
-                w = kern.astype(BF16).astype(F32) * images[pl.ds(t0, ROWS), h * LANES : (h + 1) * LANES]
-                new.append(acc[h] + w)
-                total = total + w
-            rowacc[pl.ds(t0, ROWS), :] = total
-            return tuple(new)
-
-        zero = jnp.zeros((ROWS, LANES), F32)
-        acc = lax.fori_loop(0, targets // ROWS, step, (zero,) * len(halves), unroll=4)
+                kern = pair - (amp * ebb) * p
+                w = kern.astype(BF16).astype(F32) * image
+                acc[h] = w if acc[h] is None else acc[h] + w
+                along = along + w
+            rowacc[rows, :] = along
         for h in halves:
-            colacc[0:1, pl.ds(pl.multiple_of(s0 + h * LANES, LANES), LANES)] = jnp.sum(acc[h], axis=0, keepdims=True)
+            colacc[:, lanes[h]] += sum(acc[h][m : m + 8] for m in range(0, ROWS, 8))
+
+    products(0, even)
+
+    def two(k, _):
+        elements(2 * k, even)
+        products(2 * k + 1, odd)
+        elements(2 * k + 1, odd)
+        products(jnp.minimum(2 * k + 2, steps - 1), even)
         return 0
 
-    lax.fori_loop(0, sources // CHUNK, chunk, 0)
+    lax.fori_loop(0, steps // 2, two, 0)
+    for g in range(sources // LANES):
+        here = slice(g * LANES, (g + 1) * LANES)
+        colacc[0:1, here] = jnp.sum(colacc[:, here], axis=0, keepdims=True)
     panels = col_ref.shape[2]
     for k in range(col_ref.shape[0]):
         col_ref[k] = colacc[0:1, k * panels : (k + 1) * panels]
@@ -262,12 +425,15 @@
         ),
         scratch_shapes=[
             pltpu.VMEM((targets, COLS), BF16),
-            pltpu.VMEM((sources, COLS), BF16),
-            pltpu.VMEM((7, targets, LANES), F32),
-            pltpu.VMEM((6, 8, sources), F32),
-            pltpu.VMEM((targets, CHUNK), F32),
+            pltpu.VMEM((COLS, sources), BF16),
+            pltpu.VMEM((targets, LANES), BF16),
+            pltpu.VMEM((3, LANES, sources), BF16),
+            pltpu.VMEM((4, targets, LANES), F32),
+            pltpu.VMEM((5, 8, sources), F32),
+            pltpu.VMEM((4, STEP, CHUNK), F32),
+            pltpu.VMEM((4, STEP, CHUNK), F32),
             pltpu.VMEM((targets, LANES), F32),
-            pltpu.VMEM((1, sources), F32),
+            pltpu.VMEM((8, sources), F32),
         ],
         compiler_params=pltpu.CompilerParams(vmem_limit_bytes=24 << 20),
         name="tile",

time: 134 us -> 129 us (0.963)
  Pallas kernels: 22 us -> 17.3 us
    pallas_call x1, Pallas kernels: 19.4 us -> 14.6 us  [tile(): pl.pallas_call(tile_kernel, out_shape=(jax.ShapeDtypeStruct((8, LANES), F...]
where the time goes in v4:
time: 129 us; the launch traced here: 128 us
  blocking collectives  109 us (84%)
  Pallas kernels  17.3 us (13%)
    all_to_all x7, blocking collectives, exchange(): return lax.all_to_all(pieces, axes, 0, 0, tiled=True)  109 us
    pallas_call x1, Pallas kernels, tile(): pl.pallas_call(tile_kernel, out_shape=(jax.ShapeDtypeStruct((8, LANES), F...  14.6 us

profile of v4, /device:TPU:1, one launch (start us, length us, event | category | flops | bytes accessed | tf_op | source)
XLA Modules:
  0.0 128.3 jit_solution(2518311764918987459)
XLA Ops:
  0.6 1.7 %pack.1 = (bf16[16,40,128]{2,1,0:T(8,128)(2,1)}, bf16[32,40,128]{2,1,0:T(8,128)(2,1)}) custom-call(f32[3,64]{1,0:T(4,128)} %pos_ref.1, f32[3,64]{1,0:T(4,128)} %nrm_ref.1, f32[1,64]{1,0:T(1,128)} %bitcast.12, bf16[64,64]{1,0:T(8,128)(2,1)} %dir_ref.1, bf16[64,64]{1,0:T(8,128)(2,1)} %adj_ref.1), custom_call_target="tpu_custom_call" | custom-call | tf_op jit(solution)/shard_map/pack/pallas_call | solution.py:233
  2.3 0.0 copy-start.4
  2.3 20.2 %all_to_all.35.tgt_ref = bf16[16,40,128]{2,1,0:T(8,128)(2,1)S(1)} all-to-all(bf16[16,40,128]{2,1,0:T(8,128)(2,1)} %get-tuple-element.10), channel_id=1, replica_groups=mesh['z_lo'=2,'y'=8,'core'=2,'x'=4,'z_hi'=4] {'y','core'}, dimensions={0} | all-to-all | bytes 327680 | tf_op jit(solution)/shard_map/all_to_all | solution.py:485
  22.5 0.0 copy-done.4
  22.5 23.5 %all_to_all.36.src_ref = bf16[32,40,128]{2,1,0:T(8,128)(2,1)S(1)} all-to-all(bf16[32,40,128]{2,1,0:T(8,128)(2,1)S(1)} %copy-done.4), channel_id=1, replica_groups=mesh['z_lo'=2,'y'=8,'core'=2,'x'=4,'z_hi'=4] {'z_lo','x','z_hi'}, dimensions={0} | all-to-all | bytes 655360 | tf_op jit(solution)/shard_map/all_to_all | solution.py:485
  46.0 0.0 copy-start.1
  46.0 0.0 copy-start.2
  46.0 0.0 copy-start.3
  46.0 0.7 copy-done.1
  46.7 0.0 copy-done.2
  46.7 0.0 copy-done.3
  46.7 14.6 %tile.12 = (f32[8,128]{1,0:T(8,128)S(1)}, f32[32,1,64]{2,1,0:T(1,128)S(1)}, bf16[128,64]{1,0:T(8,128)(2,1)S(1)}, f32[8,128]{1,0:T(8,128)S(1)}) custom-call(bf16[16,40,128]{2,1,0:T(8,128)(2,1)S(1)} %all_to_all.35.tgt_ref, bf16[32,40,128]{2,1,0:T(8,128)(2,1)S(1)} %all_to_all.36.src_ref, s32[1,64]{1,0:T(1,128)S(1)} %bitcast.9, s32[1,64]{1,0:T(1,128)S(1)} %bitcast.10, ...), custom_call_target="tpu_custom_call" | custom-call | tf_op jit(solution)/shard_map/tile/pallas_call | solution.py:418
  61.3 13.6 %all_to_all.37 = f32[32,1,64]{2,1,0:T(1,128)S(1)} all-to-all(f32[32,1,64]{2,1,0:T(1,128)S(1)} %get-tuple-element.15), channel_id=1, replica_groups=mesh['z_lo'=2,'y'=8,'core'=2,'x'=4,'z_hi'=4] {'z_lo','x','z_hi'}, dimensions={0} | all-to-all | bytes 16384 | tf_op jit(solution)/shard_map/all_to_all | solution.py:485
  74.9 0.1 reduce_sum.36
  74.9 0.1 tile.11
  75.0 12.5 %all_to_all.38 = f32[16,8,128]{2,1,0:T(8,128)S(1)} all-to-all(f32[16,8,128]{2,1,0:T(8,128)S(1)} %broadcast_in_dim.8), channel_id=1, replica_groups=mesh['z_lo'=2,'y'=8,'core'=2,'x'=4,'z_hi'=4] {'y','core'}, dimensions={0} | all-to-all | bytes 131072 | tf_op jit(solution)/shard_map/all_to_all | solution.py:485
  87.5 0.0 copy-start
  87.5 12.8 %all_to_all.39.dens_ref = f32[32,8,128]{2,1,0:T(8,128)S(1)} all-to-all(f32[32,8,128]{2,1,0:T(8,128)S(1)} %broadcast_in_dim.9), channel_id=1, replica_groups=mesh['z_lo'=2,'y'=8,'core'=2,'x'=4,'z_hi'=4] {'z_lo','x','z_hi'}, dimensions={0} | all-to-all | bytes 262144 | tf_op jit(solution)/shard_map/all_to_all | solution.py:485
  100.3 0.0 copy-done
  100.3 1.0 patch.1
  101.3 12.9 %all_to_all.40 = f32[16,4,512]{2,1,0:T(4,128)S(1)} all-to-all(f32[16,4,512]{2,1,0:T(4,128)S(1)} %get-tuple-element.17), channel_id=1, replica_groups=mesh['z_lo'=2,'y'=8,'core'=2,'x'=4,'z_hi'=4] {'y','core'}, dimensions={0} | all-to-all | bytes 262144 | tf_op jit(solution)/shard_map/all_to_all | solution.py:485
  114.3 13.3 %all_to_all.41 = f32[32,2,512]{2,1,0:T(2,128)S(1)} all-to-all(f32[32,2,512]{2,1,0:T(2,128)S(1)} %bitcast.11), channel_id=1, replica_groups=mesh['z_lo'=2,'y'=8,'core'=2,'x'=4,'z_hi'=4] {'z_lo','x','z_hi'}, dimensions={0} | all-to-all | bytes 262144 | tf_op jit(solution)/shard_map/all_to_all | solution.py:485
  127.6 0.7 reduce_sum.39
  (8 shorter events, 0.1 us)
Async XLA Ops:
  2.3 20.2 %copy-start.4 = (bf16[32,40,128]{2,1,0:T(8,128)(2,1)S(1)}, bf16[32,40,128]{2,1,0:T(8,128)(2,1)}, u32[]{:S(2)}) copy-start(bf16[32,40,128]{2,1,0:T(8,128)(2,1)} %get-tuple-element.11) | copy-start | bytes 983044
  46.0 0.7 copy-start.1
  46.0 0.7 copy-start.2
  46.0 0.7 copy-start.3
  87.5 12.8 %copy-start = (bf16[1,256,512]{2,1,0:T(8,128)(2,1)S(1)}, bf16[1,256,512]{2,1,0:T(8,128)(2,1)}, u32[]{:S(2)}) copy-start(bf16[1,256,512]{2,1,0:T(8,128)(2,1)} %param.14) | copy-start | bytes 786436

commit v5 on v4

--- a/solution.py
+++ b/solution.py
@@ -17,19 +17,17 @@
 inv_four_pi = 0.07957747154594767
 
 TURNS = wave_number / (2.0 * np.pi)
-DEGREE = 5
-
-
-def cosine_coefficients():
+DEGREE = 3
+
+
+def sine_coefficients():
     k = np.arange(64)
-    nodes = 0.125 + 0.125 * np.cos(np.pi * (2 * k + 1) / 128)
-    fit = np.polynomial.chebyshev.Chebyshev.fit(
-        nodes, np.cos(2 * np.pi * np.sqrt(nodes)), DEGREE, domain=[0.0, 0.25]
-    )
-    return fit.convert(kind=np.polynomial.Polynomial).coef
-
-
-COEF = cosine_coefficients()
+    nodes = 0.25 * np.cos(np.pi * (2 * k + 1) / 128)
+    fit = np.polynomial.chebyshev.Chebyshev.fit(nodes, np.sin(2 * np.pi * nodes), 2 * DEGREE + 1, domain=[-0.25, 0.25])
+    return fit.convert(kind=np.polynomial.Polynomial).coef[1::2]
+
+
+COEF = sine_coefficients()
 LEAD = float(COEF[-1])
 MONIC = [float(c / COEF[-1]) for c in COEF[:-1]]
 ROUNDER = float(3 << 22)
@@ -104,35 +102,39 @@
     return hi, mid, lo
 
 
-def pack_kernel(pos_ref, nrm_ref, area_ref, dir_ref, adj_ref, tgt_ref, src_ref):
-    pos = pos_ref[...]
+def three(v):
+    return [part.astype(F32) for part in split3(v)]
+
+
+def scaled(pos):
     row = lax.broadcasted_iota(jnp.int32, pos.shape, 0)
-    pos = jnp.where(row == 2, 0.5 * (pos - 1.2), pos) * TURNS
-    p = [v.astype(F32) for v in split3(pos)]
-    n = [v.astype(F32) for v in split3(nrm_ref[...])]
-    a = [v.astype(F32) for v in split3(area_ref[...] * TURNS**2)]
-    flat = [v[0:2] for v in p]
-    deep = [v[2:3] for v in p]
-    none = jnp.zeros((2, pos.shape[1]), F32)
-
-    def lay(top, left, right, ref):
-        geo = jnp.concatenate([jnp.concatenate(left, axis=0), jnp.concatenate(right, axis=0)], axis=1)
-        top = jnp.concatenate([top[:HALF], top[HALF:]], axis=1)
-        piece = jnp.concatenate([top, geo], axis=0).astype(BF16)
-        for k in range(ref.shape[0]):
-            ref[k] = piece
-
-    nx, ny, nz = ([v[k : k + 1] for v in n[:2]] for k in range(3))
-    lay(adj_ref[...].astype(F32), flat + nx, deep + ny + nz + [none[:1]], tgt_ref)
-    lay(dir_ref[...].astype(F32).T, flat + [none], deep + a + [none], src_ref)
-
-
-def pack(positions, normals, areas, direct, adjoint):
-    panels = positions.shape[1]
-    out = [jax.ShapeDtypeStruct((count, DEPTH, LANES), BF16) for count in (NTGT, NSRC)]
-    return pl.pallas_call(pack_kernel, out_shape=out, name="pack")(
-        positions, normals, areas.reshape(1, panels), direct, adjoint
-    )
+    parts = three(jnp.where(row == 2, 0.5 * (pos - 1.2), pos) * TURNS)
+    return [v[0:2] for v in parts], [v[2:3] for v in parts]
+
+
+def lay(top, left, right, ref):
+    geo = jnp.concatenate([jnp.concatenate(left, axis=0), jnp.concatenate(right, axis=0)], axis=1)
+    top = jnp.concatenate([top[:HALF], top[HALF:]], axis=1)
+    piece = jnp.concatenate([top, geo], axis=0).astype(BF16)
+    for k in range(ref.shape[0]):
+        ref[k] = piece
+
+
+def pack_targets_kernel(pos_ref, nrm_ref, adj_ref, ref):
+    flat, deep = scaled(pos_ref[...])
+    nx, ny, nz = ([v[k : k + 1] for v in three(nrm_ref[...])[:2]] for k in range(3))
+    lay(adj_ref[...].astype(F32), flat + nx, deep + ny + nz + [jnp.zeros_like(deep[0])], ref)
+
+
+def pack_sources_kernel(pos_ref, area_ref, dir_ref, ref):
+    flat, deep = scaled(pos_ref[...])
+    none = jnp.zeros((2, pos_ref.shape[1]), F32)
+    lay(dir_ref[...].astype(F32).T, flat + [none], deep + three(area_ref[...] * TURNS**2) + [none], ref)
+
+
+def pack(kernel, count, *arrays):
+    out = jax.ShapeDtypeStruct((count, DEPTH, LANES), BF16)
+    return pl.pallas_call(kernel, out_shape=out, name="pack")(*arrays)
 
 
 def beside(a, b):
@@ -146,111 +148,9 @@
     return sum(value[m : m + 1, :] for m in parts)
 
 
-def three(v):
-    return [part.astype(F32) for part in split3(v)]
-
-
-ROWS = 16, 19, 22, 25, 32
-S_MOMENT, S_SHARE, S_SQUARE, S_ONE, S_ROWS = 16, 25, 28, 31, 32
-
-
-def product_lanes():
-    left, right = [], [{}, {}, {}]
-    for d, n in enumerate((NX, NY, NZ)):
-        for a in range(2):
-            for b in range(3):
-                lane = len(left)
-                left.append(n[a])
-                right[0][lane] = (S_MOMENT + 3 * d + b, -1.0)
-                right[1][lane] = (S_MOMENT + 3 * d + b, 1.0 if d == 2 else -1.0)
-    for a in range(3):
-        for b in range(3):
-            lane = len(left)
-            left.append(T_DOT + a)
-            right[0][lane] = right[1][lane] = (S_SHARE + b, 1.0)
-    for d, p in enumerate((X, Y, Z)):
-        for a in range(3):
-            for b in range(3):
-                right[2][len(left)] = (p[b], 2.0 if d == 2 else -2.0)
-                left.append(p[a])
-    for a in range(3):
-        right[2][len(left)] = (S_ONE, 1.0)
-        left.append(T_SQUARE + a)
-    for b in range(3):
-        right[2][len(left)] = (S_SQUARE + b, 1.0)
-        left.append(T_ONE)
-    return dict(enumerate(left)), right
-
-
-LEFT, RIGHT = product_lanes()
-
-
-def selector(rows, entries):
-    lane = lax.broadcasted_iota(jnp.int32, (8, LANES), 1)
-    where, value = jnp.full((8, LANES), -1, jnp.int32), jnp.zeros((8, LANES), F32)
-    for key, (row, sign) in entries.items():
-        where = jnp.where(lane == key, row, where)
-        value = jnp.where(lane == key, sign, value)
-    at = lax.broadcasted_iota(jnp.int32, (rows, LANES), 0)
-    many = (rows // 8, 1)
-    return jnp.where(at == jnp.tile(where, many), jnp.tile(value, many), 0.0)
-
-
-def split3(v):
-    hi = v.astype(BF16)
-    rest = v - hi.astype(F32)
-    mid = rest.astype(BF16)
-    lo = (rest - mid.astype(F32)).astype(BF16)
-    return hi, mid, lo
-
-
-def pack_kernel(pos_ref, nrm_ref, area_ref, dir_ref, adj_ref, tgt_ref, src_ref):
-    pos = pos_ref[...]
-    row = lax.broadcasted_iota(jnp.int32, pos.shape, 0)
-    pos = jnp.where(row == 2, 0.5 * (pos - 1.2), pos) * TURNS
-    p = [v.astype(F32) for v in split3(pos)]
-    n = [v.astype(F32) for v in split3(nrm_ref[...])]
-    a = [v.astype(F32) for v in split3(area_ref[...] * TURNS**2)]
-    flat = [v[0:2] for v in p]
-    deep = [v[2:3] for v in p]
-    none = jnp.zeros((2, pos.shape[1]), F32)
-
-    def lay(top, left, right, ref):
-        geo = jnp.concatenate([jnp.concatenate(left, axis=0), jnp.concatenate(right, axis=0)], axis=1)
-        top = jnp.concatenate([top[:HALF], top[HALF:]], axis=1)
-        piece = jnp.concatenate([top, geo], axis=0).astype(BF16)
-        for k in range(ref.shape[0]):
-            ref[k] = piece
-
-    nx, ny, nz = ([v[k : k + 1] for v in n[:2]] for k in range(3))
-    lay(adj_ref[...].astype(F32), flat + nx, deep + ny + nz + [none[:1]], tgt_ref)
-    lay(dir_ref[...].astype(F32).T, flat + [none], deep + a + [none], src_ref)
-
-
-def pack(positions, normals, areas, direct, adjoint):
-    panels = positions.shape[1]
-    out = [jax.ShapeDtypeStruct((count, DEPTH, LANES), BF16) for count in (NTGT, NSRC)]
-    return pl.pallas_call(pack_kernel, out_shape=out, name="pack")(
-        positions, normals, areas.reshape(1, panels), direct, adjoint
-    )
-
-
-def unpack(ref, k, cols):
-    geo = []
-    for m in (k, k + 1):
-        piece = ref[m].astype(F32)
-        cols[m * COLS : m * COLS + HALF, :] = piece[:HALF, :COLS].astype(BF16)
-        cols[m * COLS + HALF : (m + 1) * COLS, :] = piece[:HALF, COLS:].astype(BF16)
-        geo.append(piece[HALF:])
-    return (
-        jnp.concatenate([geo[0][:, :COLS], geo[1][:, :COLS]], axis=1),
-        jnp.concatenate([geo[0][:, COLS:], geo[1][:, COLS:]], axis=1),
-    )
-
-
 ROWS = 16
 CHUNK = 256
-STEP = 256
+STEP = 512
 
 
 def device_place():
@@ -259,7 +159,7 @@
     return rho, (at["z_lo"] * PARTS["x"] + at["x"]) * PARTS["z_hi"] + at["z_hi"]
 
 
-def mix_rows(counts_ref, owner_ref, lists_ref, mix_ref):
+def mixing_kernel(counts_ref, owner_ref, lists_ref, mix_ref):
     rho, gamma = device_place()
     nx, ncol = PARTS["x"], PARTS["x"] * PARTS["z_hi"]
     holder = ((gamma // ncol) * NTGT + rho) * ncol + gamma % ncol
@@ -292,11 +192,17 @@
         mix_ref[high * NPATCH : (high + 1) * NPATCH, :] = part
 
 
+def mixing(patch_counts, patch_owner, block_lists):
+    return pl.pallas_call(
+        mixing_kernel,
+        out_shape=jax.ShapeDtypeStruct((2 * NPATCH, NBLK // 2), BF16),
+        name="mixing",
+    )(patch_counts.reshape(1, NPATCH), patch_owner.reshape(1, NPATCH), block_lists.T)
+
+
 def tile_kernel(
-    tgt_ref, src_ref, counts_ref, owner_ref, lists_ref, row_ref, col_ref, mix_ref, own_ref,
-    tcols, scols, tfeat, sfeat, tgeo, sgeo, even, odd, rowacc, colacc,
+    tgt_ref, src_ref, row_ref, col_ref, own_ref, tcols, scols, tfeat, sfeat, tgeo, sgeo, even, odd, rowacc, colacc
 ):
-    mix_rows(counts_ref, owner_ref, lists_ref, mix_ref)
     rho, _ = device_place()
     at_row = lax.broadcasted_iota(jnp.int32, own_ref.shape, 0) == rho % 8
     at_lane = lax.broadcasted_iota(jnp.int32, own_ref.shape, 1) // COLS == rho // 8
@@ -378,11 +284,12 @@
                 pair = top * (i1 * i1 * i1) + topi * (i2 * i2 * i2)
                 phase = flat * i3
                 f = phase - ((phase + ROUNDER) - ROUNDER)
-                g = f * f
+                turn = 0.25 - jnp.abs(f)
+                g = turn * turn
                 p = g + MONIC[-1]
                 for c in MONIC[-2::-1]:
                     p = p * g + c
-                kern = pair - (amp * ebb) * p
+                kern = pair - (amp * ebb) * (turn * p)
                 w = kern.astype(BF16).astype(F32) * image
                 acc[h] = w if acc[h] is None else acc[h] + w
                 along = along + w
@@ -413,14 +320,13 @@
             row_ref[low : low + 1, high * panels : (high + 1) * panels] = line[:, k * panels : (k + 1) * panels]
 
 
-def tile(tgt, src, patch_counts, patch_owner, block_lists, panels):
+def tile(tgt, src, panels):
     targets, sources = tgt.shape[0] * panels, src.shape[0] * panels
     return pl.pallas_call(
         tile_kernel,
         out_shape=(
             jax.ShapeDtypeStruct((8, LANES), F32),
             jax.ShapeDtypeStruct((src.shape[0], 1, panels), F32),
-            jax.ShapeDtypeStruct((2 * NPATCH, NBLK // 2), BF16),
             jax.ShapeDtypeStruct((8, LANES), F32),
         ),
         scratch_shapes=[
@@ -437,7 +343,7 @@
         ],
         compiler_params=pltpu.CompilerParams(vmem_limit_bytes=24 << 20),
         name="tile",
-    )(tgt, src, patch_counts.reshape(1, NPATCH), patch_owner.reshape(1, NPATCH), block_lists.T)
+    )(tgt, src)
 
 
 def patch_kernel(mix_ref, dens_ref, spline_ref, out_ref, own_ref):
@@ -493,10 +399,12 @@
     positions, normals, areas, direct, adjoint, spline, block_lists, patch_counts, patch_owner
 ):
     panels = positions.shape[1]
-    tgt, src = pack(positions, normals, areas, direct, adjoint)
+    tgt = pack(pack_targets_kernel, NTGT, positions, normals, adjoint)
+    src = pack(pack_sources_kernel, NSRC, positions, areas.reshape(1, panels), direct)
+    mix = mixing(patch_counts, patch_owner, block_lists)
+    tgt_all = exchange(tgt, TGT_AXES)
     src_all = exchange(src, SRC_AXES)
-    tgt_all = exchange(tgt, TGT_AXES)
-    row_part, col_part, mix, own_place = tile(tgt_all, src_all, patch_counts, patch_owner, block_lists, panels)
+    row_part, col_part, own_place = tile(tgt_all, src_all, panels)
 
     mine = jnp.sum(exchange(col_part, SRC_AXES), axis=0)
     row_part = row_part + own_place * jnp.tile(mine, (1, 2))

time: 129 us -> 130 us (level)
  blocking collectives: 109 us -> 76 us
  waiting for transfers between devices: 0 us -> 16.3 us
  starting transfers between devices: 0 us -> 14 us
  Pallas kernels: 17.3 us -> 19.7 us
    all_to_all x7 -> x5, blocking collectives: 109 us -> 76 us  [exchange(): return lax.all_to_all(pieces, axes, 0, 0, tiled=True)]
    all_to_all x0 -> x2, waiting for transfers between devices: none -> 16.3 us  [exchange(): return lax.all_to_all(pieces, axes, 0, 0, tiled=True)]
    all_to_all x0 -> x2, starting transfers between devices: none -> 14 us  [exchange(): return lax.all_to_all(pieces, axes, 0, 0, tiled=True)]
    pallas_call x1 -> x3, Pallas kernels: 1.67 us -> 4.78 us  [the longest x2 3.13 us: pack(): return pl.pallas_call(kernel, out_shape=out, name='pack')(*arrays)]
  transfers between devices with their start and end apart: 0 -> 2, of which waited for: 0 -> 2; matrix products, arithmetic and copies ran while one was open for 0% -> 0% of each run, Pallas kernels for 0% -> 3%
where the time goes in v5:
time: 130 us; the launch traced here: 129 us
  blocking collectives  76 us (58%)
  Pallas kernels  19.7 us (15%)
  waiting for transfers between devices  16.3 us (13%)
  starting transfers between devices  14 us (11%)
  local copies, waits for them, and re-layouts  1.57 us (1%)
    all_to_all x5, blocking collectives, exchange(): return lax.all_to_all(pieces, axes, 0, 0, tiled=True)  76 us
    all_to_all x2, waiting for transfers between devices, exchange(): return lax.all_to_all(pieces, axes, 0, 0, tiled=True)  16.3 us
    all_to_all x2, starting transfers between devices, exchange(): return lax.all_to_all(pieces, axes, 0, 0, tiled=True)  14 us
    pallas_call x1, Pallas kernels, tile(): pl.pallas_call(tile_kernel, out_shape=(jax.ShapeDtypeStruct((8, LANES), F...  14 us
    pallas_call x2, Pallas kernels, pack(): return pl.pallas_call(kernel, out_shape=out, name='pack')(*arrays)  3.13 us
  transfers between devices with their start and end apart: 2, of which 2 were waited for; matrix products, arithmetic and copies ran while one was open for 0% of the time, Pallas kernels for 3%

profile of v5, /device:TPU:1, one launch (start us, length us, event | category | flops | bytes accessed | tf_op | source)
XLA Modules:
  0.0 129.0 jit_solution(3197130963108660818)
XLA Ops:
  0.6 1.5 %pack.2 = bf16[16,40,128]{2,1,0:T(8,128)(2,1)} custom-call(f32[3,64]{1,0:T(4,128)} %pos_ref.3, f32[3,64]{1,0:T(4,128)} %nrm_ref.1, bf16[64,64]{1,0:T(8,128)(2,1)} %adj_ref.1), custom_call_target="tpu_custom_call" | custom-call | tf_op jit(solution)/shard_map/pack/pallas_call | solution.py:137
  2.1 10.2 %all-to-all-start = ((bf16[16,40,128]{2,1,0:T(8,128)(2,1)}), bf16[16,40,128]{2,1,0:T(8,128)(2,1)S(1)}, u32[]{:S(2)}, u32[]{:S(2)}) async-start(bf16[16,40,128]{2,1,0:T(8,128)(2,1)} %pack.2), calls=%async_computation | async-start | bytes 327680 | tf_op jit(solution)/shard_map/all_to_all | solution.py:391
  12.3 1.6 %pack.3 = bf16[32,40,128]{2,1,0:T(8,128)(2,1)} custom-call(f32[3,64]{1,0:T(4,128)} %pos_ref.3, f32[1,64]{1,0:T(1,128)} %bitcast.10, bf16[64,64]{1,0:T(8,128)(2,1)} %dir_ref.1), custom_call_target="tpu_custom_call" | custom-call | tf_op jit(solution)/shard_map/pack/pallas_call | solution.py:137
  13.9 8.3 %all-to-all-done.tgt_ref = bf16[16,40,128]{2,1,0:T(8,128)(2,1)S(1)} async-done(((bf16[16,40,128]{2,1,0:T(8,128)(2,1)}), bf16[16,40,128]{2,1,0:T(8,128)(2,1)S(1)}, u32[]{:S(2)}, u32[]{:S(2)}) %all-to-all-start) | async-done | bytes 163872 | tf_op jit(solution)/shard_map/all_to_all | solution.py:391
  22.2 23.7 %all_to_all.35.src_ref = bf16[32,40,128]{2,1,0:T(8,128)(2,1)S(1)} all-to-all(bf16[32,40,128]{2,1,0:T(8,128)(2,1)} %pack.3), channel_id=1, replica_groups=mesh['z_lo'=2,'y'=8,'core'=2,'x'=4,'z_hi'=4] {'z_lo','x','z_hi'}, dimensions={0} | all-to-all | bytes 655360 | tf_op jit(solution)/shard_map/all_to_all | solution.py:391
  45.9 14.0 %tile.12 = (f32[8,128]{1,0:T(8,128)S(1)}, f32[32,1,64]{2,1,0:T(1,128)S(1)}, f32[8,128]{1,0:T(8,128)S(1)}) custom-call(bf16[16,40,128]{2,1,0:T(8,128)(2,1)S(1)} %all-to-all-done.tgt_ref, bf16[32,40,128]{2,1,0:T(8,128)(2,1)S(1)} %all_to_all.35.src_ref), custom_call_target="tpu_custom_call" | custom-call | tf_op jit(solution)/shard_map/tile/pallas_call | solution.py:325
  59.9 13.6 %all_to_all.36 = f32[32,1,64]{2,1,0:T(1,128)S(1)} all-to-all(f32[32,1,64]{2,1,0:T(1,128)S(1)} %get-tuple-element.9), channel_id=1, replica_groups=mesh['z_lo'=2,'y'=8,'core'=2,'x'=4,'z_hi'=4] {'z_lo','x','z_hi'}, dimensions={0} | all-to-all | bytes 16384 | tf_op jit(solution)/shard_map/all_to_all | solution.py:391
  73.5 0.1 reduce_sum.36
  73.6 0.1 tile.11
  73.7 12.4 %all_to_all.37 = f32[16,8,128]{2,1,0:T(8,128)S(1)} all-to-all(f32[16,8,128]{2,1,0:T(8,128)S(1)} %broadcast_in_dim.8), channel_id=1, replica_groups=mesh['z_lo'=2,'y'=8,'core'=2,'x'=4,'z_hi'=4] {'y','core'}, dimensions={0} | all-to-all | bytes 131072 | tf_op jit(solution)/shard_map/all_to_all | solution.py:391
  86.1 0.0 copy-start
  86.1 0.6 broadcast_in_dim.9
  86.8 3.9 %all-to-all-start.4 = ((f32[32,8,128]{2,1,0:T(8,128)}), f32[32,8,128]{2,1,0:T(8,128)S(1)}, u32[]{:S(2)}, u32[]{:S(2)}) async-start(f32[32,8,128]{2,1,0:T(8,128)} %broadcast_in_dim.9), calls=%async_computation.4 | async-start | bytes 262144 | tf_op jit(solution)/shard_map/all_to_all | solution.py:391
  90.6 1.6 %mixing.1.mix_ref = bf16[128,64]{1,0:T(8,128)(2,1)} custom-call(s32[1,64]{1,0:T(1,128)} %bitcast.11, s32[1,64]{1,0:T(1,128)} %bitcast.12, s32[4,128]{1,0:T(4,128)} %bitcast.9), custom_call_target="tpu_custom_call" | custom-call | tf_op jit(solution)/shard_map/mixing/pallas_call | solution.py:196
  92.3 8.0 %all-to-all-done.4.dens_ref = f32[32,8,128]{2,1,0:T(8,128)S(1)} async-done(((f32[32,8,128]{2,1,0:T(8,128)}), f32[32,8,128]{2,1,0:T(8,128)S(1)}, u32[]{:S(2)}, u32[]{:S(2)}) %all-to-all-start.4) | async-done | bytes 131104 | tf_op jit(solution)/shard_map/all_to_all | solution.py:391
  100.3 0.0 copy-done
  100.3 0.0 copy-start.1
  100.3 0.8 copy-done.1
  101.1 1.0 patch.1
  102.1 12.9 %all_to_all.38 = f32[16,4,512]{2,1,0:T(4,128)S(1)} all-to-all(f32[16,4,512]{2,1,0:T(4,128)S(1)} %get-tuple-element.11), channel_id=1, replica_groups=mesh['z_lo'=2,'y'=8,'core'=2,'x'=4,'z_hi'=4] {'y','core'}, dimensions={0} | all-to-all | bytes 262144 | tf_op jit(solution)/shard_map/all_to_all | solution.py:391
  115.1 13.3 %all_to_all.39 = f32[32,2,512]{2,1,0:T(2,128)S(1)} all-to-all(f32[32,2,512]{2,1,0:T(2,128)S(1)} %bitcast.8), channel_id=1, replica_groups=mesh['z_lo'=2,'y'=8,'core'=2,'x'=4,'z_hi'=4] {'z_lo','x','z_hi'}, dimensions={0} | all-to-all | bytes 262144 | tf_op jit(solution)/shard_map/all_to_all | solution.py:391
  128.4 0.7 reduce_sum.39
  (7 shorter events, 0.1 us)
Async XLA Ops:
  2.1 20.1 %all-to-all-start = ((bf16[16,40,128]{2,1,0:T(8,128)(2,1)}), bf16[16,40,128]{2,1,0:T(8,128)(2,1)S(1)}, u32[]{:S(2)}, u32[]{:S(2)}) async-start(bf16[16,40,128]{2,1,0:T(8,128)(2,1)} %pack.2), calls=%async_computation | async-start | bytes 327680 | tf_op jit(solution)/shard_map/all_to_all | solution.py:391
  86.1 14.2 %copy-start = (bf16[1,256,512]{2,1,0:T(8,128)(2,1)S(1)}, bf16[1,256,512]{2,1,0:T(8,128)(2,1)}, u32[]{:S(2)}) copy-start(bf16[1,256,512]{2,1,0:T(8,128)(2,1)} %param.14) | copy-start | bytes 786436
  86.8 13.5 %all-to-all-start.4 = ((f32[32,8,128]{2,1,0:T(8,128)}), f32[32,8,128]{2,1,0:T(8,128)S(1)}, u32[]{:S(2)}, u32[]{:S(2)}) async-start(f32[32,8,128]{2,1,0:T(8,128)} %broadcast_in_dim.9), calls=%async_computation.4 | async-start | bytes 262144 | tf_op jit(solution)/shard_map/all_to_all | solution.py:391
  100.3 0.8 copy-start.1

commit v6 on v5

--- a/solution.py
+++ b/solution.py
@@ -367,9 +367,11 @@
     )
     spline = spline_ref[...]
     rows = sum(jnp.dot(part, spline, preferred_element_type=F32) for part in split3(got)[::-1])
-    depth = out_ref.shape[1]
     for piece in range(out_ref.shape[0]):
-        out_ref[piece] = rows[piece * depth : (piece + 1) * depth]
+        for k in range(out_ref.shape[1] // 2):
+            low, lanes = divmod(k, spline.shape[1] // LANES)
+            row = 4 * piece + 2 * low
+            out_ref[piece, 2 * k : 2 * k + 2, :] = rows[row : row + 2, lanes * LANES : (lanes + 1) * LANES]
     rho, gamma = device_place()
     line = dens_ref[gamma, pl.ds(rho % 8, 1), :]
     own_ref[...] = jnp.where(rho // 8 == 0, line[:, :panels], line[:, panels:])
@@ -379,7 +381,7 @@
     return pl.pallas_call(
         patch_kernel,
         out_shape=(
-            jax.ShapeDtypeStruct((NTGT, NPATCH // NTGT, spline.shape[1]), F32),
+            jax.ShapeDtypeStruct((NTGT, NPATCH // NTGT * spline.shape[1] // LANES, LANES), F32),
             jax.ShapeDtypeStruct((1, panels), F32),
         ),
         compiler_params=pltpu.CompilerParams(vmem_limit_bytes=16 << 20),
@@ -403,6 +405,7 @@
     src = pack(pack_sources_kernel, NSRC, positions, areas.reshape(1, panels), direct)
     mix = mixing(patch_counts, patch_owner, block_lists)
     tgt_all = exchange(tgt, TGT_AXES)
+    src, mix = lax.optimization_barrier((src, mix))
     src_all = exchange(src, SRC_AXES)
     row_part, col_part, own_place = tile(tgt_all, src_all, panels)
 
@@ -414,9 +417,10 @@
     contrib, own = patch(mix, blocks, spline[0], panels)
     rows = jnp.sum(exchange(contrib, TGT_AXES), axis=0)
     low = PARTS["z_lo"]
-    rows = rows.reshape(low, 1, rows.shape[0] // low, rows.shape[1])
-    rows = jnp.broadcast_to(rows, (low, NSRC // low) + rows.shape[2:]).reshape((NSRC,) + rows.shape[2:])
-    patch_grad = jnp.sum(exchange(rows, SRC_AXES), axis=0)
+    rows = rows.reshape(low, 1, 8, LANES)
+    rows = jnp.broadcast_to(rows, (low, NSRC // low, 8, LANES)).reshape(NSRC, 8, LANES)
+    rows = jnp.sum(exchange(rows, SRC_AXES), axis=0)
+    patch_grad = rows.reshape(4, 2, LANES).transpose(1, 0, 2).reshape(2, 4 * LANES)
     return own.reshape(panels), patch_grad
 
 

time: 130 us -> 128 us (0.985)
  blocking collectives: 76 us -> 88.8 us
  waiting for transfers between devices: 16.3 us -> 6.62 us
  starting transfers between devices: 14 us -> 10.2 us
  local copies, waits for them, and re-layouts: 1.57 us -> 0.13 us
    all_to_all x5 -> x6, blocking collectives: 76 us -> 88.8 us  [exchange(): return lax.all_to_all(pieces, axes, 0, 0, tiled=True)]
    all_to_all x2 -> x1, waiting for transfers between devices: 16.3 us -> 6.62 us  [exchange(): return lax.all_to_all(pieces, axes, 0, 0, tiled=True)]
    all_to_all x2 -> x1, starting transfers between devices: 14 us -> 10.2 us  [exchange(): return lax.all_to_all(pieces, axes, 0, 0, tiled=True)]
  transfers between devices with their start and end apart: 2 -> 1, of which waited for: 2 -> 1; matrix products, arithmetic and copies ran while one was open for 0% -> 0% of each run, Pallas kernels for 3% -> 3%
where the time goes in v6:
time: 128 us; the launch traced here: 127 us
  blocking collectives  88.8 us (69%)
  Pallas kernels  19.7 us (15%)
  starting transfers between devices  10.2 us (8%)
  waiting for transfers between devices  6.62 us (5%)
    all_to_all x6, blocking collectives, exchange(): return lax.all_to_all(pieces, axes, 0, 0, tiled=True)  88.8 us
    pallas_call x1, Pallas kernels, tile(): pl.pallas_call(tile_kernel, out_shape=(jax.ShapeDtypeStruct((8, LANES), F...  14 us
    all_to_all x1, starting transfers between devices, exchange(): return lax.all_to_all(pieces, axes, 0, 0, tiled=True)  10.2 us
    all_to_all x1, waiting for transfers between devices, exchange(): return lax.all_to_all(pieces, axes, 0, 0, tiled=True)  6.62 us
    pallas_call x2, Pallas kernels, pack(): return pl.pallas_call(kernel, out_shape=out, name='pack')(*arrays)  3.13 us
  transfers between devices with their start and end apart: 1, of which 1 were waited for; matrix products, arithmetic and copies ran while one was open for 0% of the time, Pallas kernels for 3%

profile of v6, /device:TPU:1, one launch (start us, length us, event | category | flops | bytes accessed | tf_op | source)
XLA Modules:
  0.0 126.8 jit_solution(2913042717198841681)
XLA Ops:
  0.6 1.5 %pack.3 = bf16[16,40,128]{2,1,0:T(8,128)(2,1)} custom-call(f32[3,64]{1,0:T(4,128)} %pos_ref.3, f32[3,64]{1,0:T(4,128)} %nrm_ref.1, bf16[64,64]{1,0:T(8,128)(2,1)} %adj_ref.1), custom_call_target="tpu_custom_call" | custom-call | tf_op jit(solution)/shard_map/pack/pallas_call | solution.py:137
  2.1 10.2 %all-to-all-start = ((bf16[16,40,128]{2,1,0:T(8,128)(2,1)}), bf16[16,40,128]{2,1,0:T(8,128)(2,1)S(1)}, u32[]{:S(2)}, u32[]{:S(2)}) async-start(bf16[16,40,128]{2,1,0:T(8,128)(2,1)} %pack.3), calls=%async_computation | async-start | bytes 327680 | tf_op jit(solution)/shard_map/all_to_all | solution.py:393
  12.3 1.6 %pack.2 = bf16[32,40,128]{2,1,0:T(8,128)(2,1)} custom-call(f32[3,64]{1,0:T(4,128)} %pos_ref.3, f32[1,64]{1,0:T(1,128)} %bitcast.18, bf16[64,64]{1,0:T(8,128)(2,1)} %dir_ref.1), custom_call_target="tpu_custom_call" | custom-call | tf_op jit(solution)/shard_map/pack/pallas_call | solution.py:137
  13.9 1.6 %mixing.1.mix_ref = bf16[128,64]{1,0:T(8,128)(2,1)} custom-call(s32[1,64]{1,0:T(1,128)} %bitcast.19, s32[1,64]{1,0:T(1,128)} %bitcast.20, s32[4,128]{1,0:T(4,128)} %bitcast.17), custom_call_target="tpu_custom_call" | custom-call | tf_op jit(solution)/shard_map/mixing/pallas_call | solution.py:196
  15.6 6.6 %all-to-all-done.tgt_ref = bf16[16,40,128]{2,1,0:T(8,128)(2,1)S(1)} async-done(((bf16[16,40,128]{2,1,0:T(8,128)(2,1)}), bf16[16,40,128]{2,1,0:T(8,128)(2,1)S(1)}, u32[]{:S(2)}, u32[]{:S(2)}) %all-to-all-start) | async-done | bytes 163872 | tf_op jit(solution)/shard_map/all_to_all | solution.py:393
  22.2 23.7 %all_to_all.35.src_ref = bf16[32,40,128]{2,1,0:T(8,128)(2,1)S(1)} all-to-all(bf16[32,40,128]{2,1,0:T(8,128)(2,1)} %pack.2), channel_id=1, replica_groups=mesh['z_lo'=2,'y'=8,'core'=2,'x'=4,'z_hi'=4] {'z_lo','x','z_hi'}, dimensions={0} | all-to-all | bytes 655360 | tf_op jit(solution)/shard_map/all_to_all | solution.py:393
  45.9 14.0 %tile.12 = (f32[8,128]{1,0:T(8,128)S(1)}, f32[32,1,64]{2,1,0:T(1,128)S(1)}, f32[8,128]{1,0:T(8,128)S(1)}) custom-call(bf16[16,40,128]{2,1,0:T(8,128)(2,1)S(1)} %all-to-all-done.tgt_ref, bf16[32,40,128]{2,1,0:T(8,128)(2,1)S(1)} %all_to_all.35.src_ref), custom_call_target="tpu_custom_call" | custom-call | tf_op jit(solution)/shard_map/tile/pallas_call | solution.py:325
  59.9 13.6 %all_to_all.36 = f32[32,1,64]{2,1,0:T(1,128)S(1)} all-to-all(f32[32,1,64]{2,1,0:T(1,128)S(1)} %get-tuple-element.13), channel_id=1, replica_groups=mesh['z_lo'=2,'y'=8,'core'=2,'x'=4,'z_hi'=4] {'z_lo','x','z_hi'}, dimensions={0} | all-to-all | bytes 16384 | tf_op jit(solution)/shard_map/all_to_all | solution.py:393
  73.5 0.1 reduce_sum.36
  73.5 0.1 tile.11
  73.6 12.5 %all_to_all.37 = f32[16,8,128]{2,1,0:T(8,128)S(1)} all-to-all(f32[16,8,128]{2,1,0:T(8,128)S(1)} %broadcast_in_dim.8), channel_id=1, replica_groups=mesh['z_lo'=2,'y'=8,'core'=2,'x'=4,'z_hi'=4] {'y','core'}, dimensions={0} | all-to-all | bytes 131072 | tf_op jit(solution)/shard_map/all_to_all | solution.py:393
  86.1 0.0 copy-start
  86.2 0.0 copy-start.1
  86.2 12.8 %all_to_all.38.dens_ref = f32[32,8,128]{2,1,0:T(8,128)S(1)} all-to-all(f32[32,8,128]{2,1,0:T(8,128)S(1)} %broadcast_in_dim.9), channel_id=1, replica_groups=mesh['z_lo'=2,'y'=8,'core'=2,'x'=4,'z_hi'=4] {'z_lo','x','z_hi'}, dimensions={0} | all-to-all | bytes 262144 | tf_op jit(solution)/shard_map/all_to_all | solution.py:393
  98.9 0.0 copy-done
  98.9 0.0 copy-done.1
  99.0 1.0 patch.1
  100.0 12.9 %all_to_all.39 = f32[16,16,128]{2,1,0:T(8,128)S(1)} all-to-all(f32[16,16,128]{2,1,0:T(8,128)S(1)} %get-tuple-element.15), channel_id=1, replica_groups=mesh['z_lo'=2,'y'=8,'core'=2,'x'=4,'z_hi'=4] {'y','core'}, dimensions={0} | all-to-all | bytes 262144 | tf_op jit(solution)/shard_map/all_to_all | solution.py:393
  112.9 13.3 %all_to_all.40 = f32[32,8,128]{2,1,0:T(8,128)S(1)} all-to-all(f32[32,8,128]{2,1,0:T(8,128)S(1)} %bitcast.14), channel_id=1, replica_groups=mesh['z_lo'=2,'y'=8,'core'=2,'x'=4,'z_hi'=4] {'z_lo','x','z_hi'}, dimensions={0} | all-to-all | bytes 262144 | tf_op jit(solution)/shard_map/all_to_all | solution.py:393
  126.2 0.6 reduce_sum.39
  (7 shorter events, 0.1 us)
Async XLA Ops:
  2.1 20.1 %all-to-all-start = ((bf16[16,40,128]{2,1,0:T(8,128)(2,1)}), bf16[16,40,128]{2,1,0:T(8,128)(2,1)S(1)}, u32[]{:S(2)}, u32[]{:S(2)}) async-start(bf16[16,40,128]{2,1,0:T(8,128)(2,1)} %pack.3), calls=%async_computation | async-start | bytes 327680 | tf_op jit(solution)/shard_map/all_to_all | solution.py:393
  86.1 12.8 %copy-start = (bf16[1,256,512]{2,1,0:T(8,128)(2,1)S(1)}, bf16[1,256,512]{2,1,0:T(8,128)(2,1)}, u32[]{:S(2)}) copy-start(bf16[1,256,512]{2,1,0:T(8,128)(2,1)} %param.14) | copy-start | bytes 786436
  86.2 12.8 %copy-start.1 = (bf16[128,64]{1,0:T(8,128)(2,1)S(1)}, bf16[128,64]{1,0:T(8,128)(2,1)}, u32[]{:S(2)}) copy-start(bf16[128,64]{1,0:T(8,128)(2,1)} %mixing.1.mix_ref) | copy-start | bytes 49156

commit v7 on v6

--- a/solution.py
+++ b/solution.py
@@ -36,8 +36,8 @@
 
 PARTS = {"z_lo": 2, "y": 8, "core": 2, "x": 4, "z_hi": 4}
 NAMES = tuple(PARTS)
-TGT_AXES = ("y", "core")
-SRC_AXES = ("z_lo", "x", "z_hi")
+TGT_AXES = ("core", "y")
+SRC_AXES = ("x", "z_lo", "z_hi")
 NTGT = PARTS["y"] * PARTS["core"]
 NSRC = PARTS["z_lo"] * PARTS["x"] * PARTS["z_hi"]
 
@@ -155,14 +155,13 @@
 
 def device_place():
     at = {name: lax.axis_index(name) for name in NAMES}
-    rho = at["y"] * PARTS["core"] + at["core"]
-    return rho, (at["z_lo"] * PARTS["x"] + at["x"]) * PARTS["z_hi"] + at["z_hi"]
+    rho = at["core"] * PARTS["y"] + at["y"]
+    return rho, (at["x"] * PARTS["z_lo"] + at["z_lo"]) * PARTS["z_hi"] + at["z_hi"]
 
 
 def mixing_kernel(counts_ref, owner_ref, lists_ref, mix_ref):
-    rho, gamma = device_place()
-    nx, ncol = PARTS["x"], PARTS["x"] * PARTS["z_hi"]
-    holder = ((gamma // ncol) * NTGT + rho) * ncol + gamma % ncol
+    holder = lax.axis_index(NAMES)
+    nx, ncore, ny, nlow = (PARTS[name] for name in ("x", "core", "y", "z_lo"))
 
     def iota(shape, dim):
         return lax.broadcasted_iota(jnp.int32, shape, dim)
@@ -177,16 +176,16 @@
     inside = (starts <= ids) & (ids < starts + own_counts)
     owner = jnp.broadcast_to(owner_ref[...], square)
     place = iota(square, 0)
-    output = ((place % 4) // 2) * (2 * NTGT) + 2 * (place // 4) + place % 2
+    rho = place // 4
+    output = ((place % 4) // 2) * (2 * NTGT) + 2 * ((rho % ny) * ncore + rho // ny) + place % 2
     owned = jnp.where(owner == output, 1.0, 0.0).astype(BF16)
     listed = jnp.max(jnp.where(lists_ref[...] == holder, 1.0, 0.0), axis=0, keepdims=True)
     member = jnp.where(inside, jnp.broadcast_to(listed, lines), 0.0).astype(BF16)
     by_block = jnp.dot(owned, member, preferred_element_type=F32).astype(BF16)
     cut = (NBLK, NBLK // 2)
     k = iota(cut, 1)
-    for high in range(2):
-        rho_k = high * 8 + k % 8
-        block = (k // (8 * nx)) * (NTGT * nx) + rho_k * nx + (k // 8) % nx
+    for high in range(ncore):
+        block = ((k // ny) % nlow) * (NTGT * nx) + ((k % ny) * ncore + high) * nx + k // (ny * nlow)
         order = jnp.where(iota(cut, 0) == block, 1.0, 0.0).astype(BF16)
         part = jnp.dot(by_block, order, preferred_element_type=F32).astype(BF16)
         mix_ref[high * NPATCH : (high + 1) * NPATCH, :] = part
@@ -417,8 +416,8 @@
     contrib, own = patch(mix, blocks, spline[0], panels)
     rows = jnp.sum(exchange(contrib, TGT_AXES), axis=0)
     low = PARTS["z_lo"]
-    rows = rows.reshape(low, 1, 8, LANES)
-    rows = jnp.broadcast_to(rows, (low, NSRC // low, 8, LANES)).reshape(NSRC, 8, LANES)
+    rows = rows.reshape(1, low, 1, 8, LANES)
+    rows = jnp.broadcast_to(rows, (PARTS["x"], low, PARTS["z_hi"], 8, LANES)).reshape(NSRC, 8, LANES)
     rows = jnp.sum(exchange(rows, SRC_AXES), axis=0)
     patch_grad = rows.reshape(4, 2, LANES).transpose(1, 0, 2).reshape(2, 4 * LANES)
     return own.reshape(panels), patch_grad

time: 128 us -> 125 us (0.977)
  waiting for transfers between devices: 6.62 us -> 4.54 us
  blocking collectives: 88.8 us -> 87.4 us
    all_to_all x1, waiting for transfers between devices: 6.62 us -> 4.54 us  [exchange(): return lax.all_to_all(pieces, axes, 0, 0, tiled=True)]
    all_to_all x6, blocking collectives: 88.8 us -> 87.4 us  [exchange(): return lax.all_to_all(pieces, axes, 0, 0, tiled=True)]
where the time goes in v7:
time: 125 us; the launch traced here: 123 us
  blocking collectives  87.4 us (70%)
  Pallas kernels  19.7 us (16%)
  starting transfers between devices  10.2 us (8%)
  waiting for transfers between devices  4.54 us (4%)
    all_to_all x6, blocking collectives, exchange(): return lax.all_to_all(pieces, axes, 0, 0, tiled=True)  87.4 us
    pallas_call x1, Pallas kernels, tile(): pl.pallas_call(tile_kernel, out_shape=(jax.ShapeDtypeStruct((8, LANES), F...  14 us
    all_to_all x1, starting transfers between devices, exchange(): return lax.all_to_all(pieces, axes, 0, 0, tiled=True)  10.2 us
    all_to_all x1, waiting for transfers between devices, exchange(): return lax.all_to_all(pieces, axes, 0, 0, tiled=True)  4.54 us
    pallas_call x2, Pallas kernels, pack(): return pl.pallas_call(kernel, out_shape=out, name='pack')(*arrays)  3.13 us
  transfers between devices with their start and end apart: 1, of which 1 were waited for; matrix products, arithmetic and copies ran while one was open for 0% of the time, Pallas kernels for 3%

profile of v7, /device:TPU:1, one launch (start us, length us, event | category | flops | bytes accessed | tf_op | source)
XLA Modules:
  0.0 123.4 jit_solution(3811339864549034729)
XLA Ops:
  0.6 1.5 %pack.3 = bf16[16,40,128]{2,1,0:T(8,128)(2,1)} custom-call(f32[3,64]{1,0:T(4,128)} %pos_ref.3, f32[3,64]{1,0:T(4,128)} %nrm_ref.1, bf16[64,64]{1,0:T(8,128)(2,1)} %adj_ref.1), custom_call_target="tpu_custom_call" | custom-call | tf_op jit(solution)/shard_map/pack/pallas_call | solution.py:137
  2.1 10.2 %all-to-all-start = ((bf16[16,40,128]{2,1,0:T(8,128)(2,1)}), bf16[16,40,128]{2,1,0:T(8,128)(2,1)S(1)}, u32[]{:S(2)}, u32[]{:S(2)}) async-start(bf16[16,40,128]{2,1,0:T(8,128)(2,1)} %pack.3), calls=%async_computation | async-start | bytes 327680 | tf_op jit(solution)/shard_map/all_to_all | solution.py:392
  12.4 1.6 %pack.2 = bf16[32,40,128]{2,1,0:T(8,128)(2,1)} custom-call(f32[3,64]{1,0:T(4,128)} %pos_ref.3, f32[1,64]{1,0:T(1,128)} %bitcast.18, bf16[64,64]{1,0:T(8,128)(2,1)} %dir_ref.1), custom_call_target="tpu_custom_call" | custom-call | tf_op jit(solution)/shard_map/pack/pallas_call | solution.py:137
  14.0 1.6 %mixing.1.mix_ref = bf16[128,64]{1,0:T(8,128)(2,1)} custom-call(s32[1,64]{1,0:T(1,128)} %bitcast.19, s32[1,64]{1,0:T(1,128)} %bitcast.20, s32[4,128]{1,0:T(4,128)} %bitcast.17), custom_call_target="tpu_custom_call" | custom-call | tf_op jit(solution)/shard_map/mixing/pallas_call | solution.py:195
  15.6 4.5 %all-to-all-done.tgt_ref = bf16[16,40,128]{2,1,0:T(8,128)(2,1)S(1)} async-done(((bf16[16,40,128]{2,1,0:T(8,128)(2,1)}), bf16[16,40,128]{2,1,0:T(8,128)(2,1)S(1)}, u32[]{:S(2)}, u32[]{:S(2)}) %all-to-all-start) | async-done | bytes 163872 | tf_op jit(solution)/shard_map/all_to_all | solution.py:392
  20.2 21.7 %all_to_all.35.src_ref = bf16[32,40,128]{2,1,0:T(8,128)(2,1)S(1)} all-to-all(bf16[32,40,128]{2,1,0:T(8,128)(2,1)} %pack.2), channel_id=1, replica_groups=mesh['z_lo'=2,'y'=8,'core'=2,'x'=4,'z_hi'=4] {'x','z_lo','z_hi'}, dimensions={0} | all-to-all | bytes 655360 | tf_op jit(solution)/shard_map/all_to_all | solution.py:392
  41.9 14.0 %tile.12 = (f32[8,128]{1,0:T(8,128)S(1)}, f32[32,1,64]{2,1,0:T(1,128)S(1)}, f32[8,128]{1,0:T(8,128)S(1)}) custom-call(bf16[16,40,128]{2,1,0:T(8,128)(2,1)S(1)} %all-to-all-done.tgt_ref, bf16[32,40,128]{2,1,0:T(8,128)(2,1)S(1)} %all_to_all.35.src_ref), custom_call_target="tpu_custom_call" | custom-call | tf_op jit(solution)/shard_map/tile/pallas_call | solution.py:324
  55.8 15.8 %all_to_all.36 = f32[32,1,64]{2,1,0:T(1,128)S(1)} all-to-all(f32[32,1,64]{2,1,0:T(1,128)S(1)} %get-tuple-element.13), channel_id=1, replica_groups=mesh['z_lo'=2,'y'=8,'core'=2,'x'=4,'z_hi'=4] {'x','z_lo','z_hi'}, dimensions={0} | all-to-all | bytes 16384 | tf_op jit(solution)/shard_map/all_to_all | solution.py:392
  71.6 0.1 reduce_sum.36
  71.7 0.1 tile.11
  71.8 13.5 %all_to_all.37 = f32[16,8,128]{2,1,0:T(8,128)S(1)} all-to-all(f32[16,8,128]{2,1,0:T(8,128)S(1)} %broadcast_in_dim.8), channel_id=1, replica_groups=mesh['z_lo'=2,'y'=8,'core'=2,'x'=4,'z_hi'=4] {'core','y'}, dimensions={0} | all-to-all | bytes 131072 | tf_op jit(solution)/shard_map/all_to_all | solution.py:392
  85.3 0.0 copy-start
  85.3 0.0 copy-start.1
  85.3 12.0 %all_to_all.38.dens_ref = f32[32,8,128]{2,1,0:T(8,128)S(1)} all-to-all(f32[32,8,128]{2,1,0:T(8,128)S(1)} %broadcast_in_dim.9), channel_id=1, replica_groups=mesh['z_lo'=2,'y'=8,'core'=2,'x'=4,'z_hi'=4] {'x','z_lo','z_hi'}, dimensions={0} | all-to-all | bytes 262144 | tf_op jit(solution)/shard_map/all_to_all | solution.py:392
  97.3 0.0 copy-done
  97.3 0.0 copy-done.1
  97.3 1.0 patch.1
  98.3 11.8 %all_to_all.39 = f32[16,16,128]{2,1,0:T(8,128)S(1)} all-to-all(f32[16,16,128]{2,1,0:T(8,128)S(1)} %get-tuple-element.15), channel_id=1, replica_groups=mesh['z_lo'=2,'y'=8,'core'=2,'x'=4,'z_hi'=4] {'core','y'}, dimensions={0} | all-to-all | bytes 262144 | tf_op jit(solution)/shard_map/all_to_all | solution.py:392
  110.2 12.6 %all_to_all.40 = f32[32,8,128]{2,1,0:T(8,128)S(1)} all-to-all(f32[32,8,128]{2,1,0:T(8,128)S(1)} %bitcast.14), channel_id=1, replica_groups=mesh['z_lo'=2,'y'=8,'core'=2,'x'=4,'z_hi'=4] {'x','z_lo','z_hi'}, dimensions={0} | all-to-all | bytes 262144 | tf_op jit(solution)/shard_map/all_to_all | solution.py:392
  122.8 0.6 reduce_sum.39
  (7 shorter events, 0.1 us)
Async XLA Ops:
  2.1 18.1 %all-to-all-start = ((bf16[16,40,128]{2,1,0:T(8,128)(2,1)}), bf16[16,40,128]{2,1,0:T(8,128)(2,1)S(1)}, u32[]{:S(2)}, u32[]{:S(2)}) async-start(bf16[16,40,128]{2,1,0:T(8,128)(2,1)} %pack.3), calls=%async_computation | async-start | bytes 327680 | tf_op jit(solution)/shard_map/all_to_all | solution.py:392
  85.3 12.0 %copy-start = (bf16[1,256,512]{2,1,0:T(8,128)(2,1)S(1)}, bf16[1,256,512]{2,1,0:T(8,128)(2,1)}, u32[]{:S(2)}) copy-start(bf16[1,256,512]{2,1,0:T(8,128)(2,1)} %param.14) | copy-start | bytes 786436
  85.3 12.0 %copy-start.1 = (bf16[128,64]{1,0:T(8,128)(2,1)S(1)}, bf16[128,64]{1,0:T(8,128)(2,1)}, u32[]{:S(2)}) copy-start(bf16[128,64]{1,0:T(8,128)(2,1)} %mixing.1.mix_ref) | copy-start | bytes 49156

commit v8 on v7

--- a/solution.py
+++ b/solution.py
@@ -367,10 +367,12 @@
     spline = spline_ref[...]
     rows = sum(jnp.dot(part, spline, preferred_element_type=F32) for part in split3(got)[::-1])
     for piece in range(out_ref.shape[0]):
+        lines = []
         for k in range(out_ref.shape[1] // 2):
             low, lanes = divmod(k, spline.shape[1] // LANES)
             row = 4 * piece + 2 * low
-            out_ref[piece, 2 * k : 2 * k + 2, :] = rows[row : row + 2, lanes * LANES : (lanes + 1) * LANES]
+            lines.append(rows[row : row + 2, lanes * LANES : (lanes + 1) * LANES])
+        out_ref[piece] = jnp.concatenate(lines, axis=0).astype(BF16)
     rho, gamma = device_place()
     line = dens_ref[gamma, pl.ds(rho % 8, 1), :]
     own_ref[...] = jnp.where(rho // 8 == 0, line[:, :panels], line[:, panels:])
@@ -380,7 +382,7 @@
     return pl.pallas_call(
         patch_kernel,
         out_shape=(
-            jax.ShapeDtypeStruct((NTGT, NPATCH // NTGT * spline.shape[1] // LANES, LANES), F32),
+            jax.ShapeDtypeStruct((NTGT, NPATCH // NTGT * spline.shape[1] // LANES, LANES), BF16),
             jax.ShapeDtypeStruct((1, panels), F32),
         ),
         compiler_params=pltpu.CompilerParams(vmem_limit_bytes=16 << 20),
@@ -414,11 +416,11 @@
     blocks = exchange(copies(dens, NSRC), SRC_AXES)
 
     contrib, own = patch(mix, blocks, spline[0], panels)
-    rows = jnp.sum(exchange(contrib, TGT_AXES), axis=0)
+    rows = jnp.sum(exchange(contrib, TGT_AXES).astype(F32), axis=0).astype(BF16)
     low = PARTS["z_lo"]
     rows = rows.reshape(1, low, 1, 8, LANES)
     rows = jnp.broadcast_to(rows, (PARTS["x"], low, PARTS["z_hi"], 8, LANES)).reshape(NSRC, 8, LANES)
-    rows = jnp.sum(exchange(rows, SRC_AXES), axis=0)
+    rows = jnp.sum(exchange(rows, SRC_AXES).astype(F32), axis=0)
     patch_grad = rows.reshape(4, 2, LANES).transpose(1, 0, 2).reshape(2, 4 * LANES)
     return own.reshape(panels), patch_grad
 

time: 125 us -> 124 us (level)
  no operation moved by 1% of the time
where the time goes in v8:
time: 124 us; the launch traced here: 123 us
  blocking collectives  87 us (70%)
  Pallas kernels  19.7 us (16%)
  starting transfers between devices  10.2 us (8%)
  waiting for transfers between devices  4.54 us (4%)
    all_to_all x6, blocking collectives, exchange(): return lax.all_to_all(pieces, axes, 0, 0, tiled=True)  87 us
    pallas_call x1, Pallas kernels, tile(): pl.pallas_call(tile_kernel, out_shape=(jax.ShapeDtypeStruct((8, LANES), F...  14 us
    all_to_all x1, starting transfers between devices, exchange(): return lax.all_to_all(pieces, axes, 0, 0, tiled=True)  10.2 us
    all_to_all x1, waiting for transfers between devices, exchange(): return lax.all_to_all(pieces, axes, 0, 0, tiled=True)  4.54 us
    pallas_call x2, Pallas kernels, pack(): return pl.pallas_call(kernel, out_shape=out, name='pack')(*arrays)  3.13 us
  transfers between devices with their start and end apart: 1, of which 1 were waited for; matrix products, arithmetic and copies ran while one was open for 0% of the time, Pallas kernels for 3%

profile of v8, /device:TPU:1, one launch (start us, length us, event | category | flops | bytes accessed | tf_op | source)
XLA Modules:
  0.0 123.0 jit_solution(17344621569242687520)
XLA Ops:
  0.6 1.5 %pack.3 = bf16[16,40,128]{2,1,0:T(8,128)(2,1)} custom-call(f32[3,64]{1,0:T(4,128)} %pos_ref.3, f32[3,64]{1,0:T(4,128)} %nrm_ref.1, bf16[64,64]{1,0:T(8,128)(2,1)} %adj_ref.1), custom_call_target="tpu_custom_call" | custom-call | tf_op jit(solution)/shard_map/pack/pallas_call | solution.py:137
  2.1 10.2 %all-to-all-start = ((bf16[16,40,128]{2,1,0:T(8,128)(2,1)}), bf16[16,40,128]{2,1,0:T(8,128)(2,1)S(1)}, u32[]{:S(2)}, u32[]{:S(2)}) async-start(bf16[16,40,128]{2,1,0:T(8,128)(2,1)} %pack.3), calls=%async_computation | async-start | bytes 327680 | tf_op jit(solution)/shard_map/all_to_all | solution.py:394
  12.4 1.6 %pack.2 = bf16[32,40,128]{2,1,0:T(8,128)(2,1)} custom-call(f32[3,64]{1,0:T(4,128)} %pos_ref.3, f32[1,64]{1,0:T(1,128)} %bitcast.18, bf16[64,64]{1,0:T(8,128)(2,1)} %dir_ref.1), custom_call_target="tpu_custom_call" | custom-call | tf_op jit(solution)/shard_map/pack/pallas_call | solution.py:137
  14.0 1.6 %mixing.1.mix_ref = bf16[128,64]{1,0:T(8,128)(2,1)} custom-call(s32[1,64]{1,0:T(1,128)} %bitcast.19, s32[1,64]{1,0:T(1,128)} %bitcast.20, s32[4,128]{1,0:T(4,128)} %bitcast.17), custom_call_target="tpu_custom_call" | custom-call | tf_op jit(solution)/shard_map/mixing/pallas_call | solution.py:195
  15.6 4.5 %all-to-all-done.tgt_ref = bf16[16,40,128]{2,1,0:T(8,128)(2,1)S(1)} async-done(((bf16[16,40,128]{2,1,0:T(8,128)(2,1)}), bf16[16,40,128]{2,1,0:T(8,128)(2,1)S(1)}, u32[]{:S(2)}, u32[]{:S(2)}) %all-to-all-start) | async-done | bytes 163872 | tf_op jit(solution)/shard_map/all_to_all | solution.py:394
  20.2 21.7 %all_to_all.35.src_ref = bf16[32,40,128]{2,1,0:T(8,128)(2,1)S(1)} all-to-all(bf16[32,40,128]{2,1,0:T(8,128)(2,1)} %pack.2), channel_id=1, replica_groups=mesh['z_lo'=2,'y'=8,'core'=2,'x'=4,'z_hi'=4] {'x','z_lo','z_hi'}, dimensions={0} | all-to-all | bytes 655360 | tf_op jit(solution)/shard_map/all_to_all | solution.py:394
  41.9 14.0 %tile.12 = (f32[8,128]{1,0:T(8,128)S(1)}, f32[32,1,64]{2,1,0:T(1,128)S(1)}, f32[8,128]{1,0:T(8,128)S(1)}) custom-call(bf16[16,40,128]{2,1,0:T(8,128)(2,1)S(1)} %all-to-all-done.tgt_ref, bf16[32,40,128]{2,1,0:T(8,128)(2,1)S(1)} %all_to_all.35.src_ref), custom_call_target="tpu_custom_call" | custom-call | tf_op jit(solution)/shard_map/tile/pallas_call | solution.py:324
  55.8 15.8 %all_to_all.36 = f32[32,1,64]{2,1,0:T(1,128)S(1)} all-to-all(f32[32,1,64]{2,1,0:T(1,128)S(1)} %get-tuple-element.13), channel_id=1, replica_groups=mesh['z_lo'=2,'y'=8,'core'=2,'x'=4,'z_hi'=4] {'x','z_lo','z_hi'}, dimensions={0} | all-to-all | bytes 16384 | tf_op jit(solution)/shard_map/all_to_all | solution.py:394
  71.6 0.1 reduce_sum.39
  71.7 0.1 tile.11
  71.8 13.5 %all_to_all.37 = f32[16,8,128]{2,1,0:T(8,128)S(1)} all-to-all(f32[16,8,128]{2,1,0:T(8,128)S(1)} %broadcast_in_dim.8), channel_id=1, replica_groups=mesh['z_lo'=2,'y'=8,'core'=2,'x'=4,'z_hi'=4] {'core','y'}, dimensions={0} | all-to-all | bytes 131072 | tf_op jit(solution)/shard_map/all_to_all | solution.py:394
  85.3 0.0 copy-start
  85.3 0.0 copy-start.1
  85.3 12.0 %all_to_all.38.dens_ref = f32[32,8,128]{2,1,0:T(8,128)S(1)} all-to-all(f32[32,8,128]{2,1,0:T(8,128)S(1)} %broadcast_in_dim.9), channel_id=1, replica_groups=mesh['z_lo'=2,'y'=8,'core'=2,'x'=4,'z_hi'=4] {'x','z_lo','z_hi'}, dimensions={0} | all-to-all | bytes 262144 | tf_op jit(solution)/shard_map/all_to_all | solution.py:394
  97.3 0.0 copy-done
  97.3 0.0 copy-done.1
  97.3 1.0 patch.1
  98.3 11.6 %all_to_all.39 = bf16[16,16,128]{2,1,0:T(8,128)(2,1)S(1)} all-to-all(bf16[16,16,128]{2,1,0:T(8,128)(2,1)S(1)} %get-tuple-element.15), channel_id=1, replica_groups=mesh['z_lo'=2,'y'=8,'core'=2,'x'=4,'z_hi'=4] {'core','y'}, dimensions={0} | all-to-all | bytes 131072 | tf_op jit(solution)/shard_map/all_to_all | solution.py:394
  110.0 12.4 %all_to_all.40 = bf16[32,8,128]{2,1,0:T(8,128)(2,1)S(1)} all-to-all(bf16[32,8,128]{2,1,0:T(8,128)(2,1)S(1)} %bitcast.14), channel_id=1, replica_groups=mesh['z_lo'=2,'y'=8,'core'=2,'x'=4,'z_hi'=4] {'x','z_lo','z_hi'}, dimensions={0} | all-to-all | bytes 131072 | tf_op jit(solution)/shard_map/all_to_all | solution.py:394
  122.4 0.6 convert_reduce_fusion
  (7 shorter events, 0.1 us)
Async XLA Ops:
  2.1 18.1 %all-to-all-start = ((bf16[16,40,128]{2,1,0:T(8,128)(2,1)}), bf16[16,40,128]{2,1,0:T(8,128)(2,1)S(1)}, u32[]{:S(2)}, u32[]{:S(2)}) async-start(bf16[16,40,128]{2,1,0:T(8,128)(2,1)} %pack.3), calls=%async_computation | async-start | bytes 327680 | tf_op jit(solution)/shard_map/all_to_all | solution.py:394
  85.3 12.0 %copy-start = (bf16[1,256,512]{2,1,0:T(8,128)(2,1)S(1)}, bf16[1,256,512]{2,1,0:T(8,128)(2,1)}, u32[]{:S(2)}) copy-start(bf16[1,256,512]{2,1,0:T(8,128)(2,1)} %param.14) | copy-start | bytes 786436
  85.3 12.0 %copy-start.1 = (bf16[128,64]{1,0:T(8,128)(2,1)S(1)}, bf16[128,64]{1,0:T(8,128)(2,1)}, u32[]{:S(2)}) copy-start(bf16[128,64]{1,0:T(8,128)(2,1)} %mixing.1.mix_ref) | copy-start | bytes 49156

commit v9 on v7

--- a/solution.py
+++ b/solution.py
@@ -150,7 +150,7 @@
 
 ROWS = 16
 CHUNK = 256
-STEP = 512
+STEP = 1024
 
 
 def device_place():
@@ -356,7 +356,7 @@
         axis=1,
     )
     mix = mix_ref[...]
-    both = sum(jnp.dot(mix, part, preferred_element_type=F32) for part in split3(dens)[::-1])
+    both = sum(jnp.dot(mix, part, preferred_element_type=F32) for part in split3(dens)[1::-1])
     got = jnp.concatenate(
         [
             both[:NPATCH, q * LANES : q * LANES + panels] + both[NPATCH:, q * LANES + panels : (q + 1) * LANES]
@@ -365,7 +365,7 @@
         axis=1,
     )
     spline = spline_ref[...]
-    rows = sum(jnp.dot(part, spline, preferred_element_type=F32) for part in split3(got)[::-1])
+    rows = sum(jnp.dot(part, spline, preferred_element_type=F32) for part in split3(got)[1::-1])
     for piece in range(out_ref.shape[0]):
         for k in range(out_ref.shape[1] // 2):
             low, lanes = divmod(k, spline.shape[1] // LANES)

time: 125 us -> 125 us (level)
  no operation moved by 1% of the time
where the time goes in v9:
time: 125 us; the launch traced here: 123 us
  blocking collectives  87.4 us (70%)
  Pallas kernels  19.1 us (15%)
  starting transfers between devices  10.2 us (8%)
  waiting for transfers between devices  4.54 us (4%)
    all_to_all x6, blocking collectives, exchange(): return lax.all_to_all(pieces, axes, 0, 0, tiled=True)  87.4 us
    pallas_call x1, Pallas kernels, tile(): pl.pallas_call(tile_kernel, out_shape=(jax.ShapeDtypeStruct((8, LANES), F...  13.4 us
    all_to_all x1, starting transfers between devices, exchange(): return lax.all_to_all(pieces, axes, 0, 0, tiled=True)  10.2 us
    all_to_all x1, waiting for transfers between devices, exchange(): return lax.all_to_all(pieces, axes, 0, 0, tiled=True)  4.54 us
    pallas_call x2, Pallas kernels, pack(): return pl.pallas_call(kernel, out_shape=out, name='pack')(*arrays)  3.13 us
  transfers between devices with their start and end apart: 1, of which 1 were waited for; matrix products, arithmetic and copies ran while one was open for 0% of the time, Pallas kernels for 3%

profile of v9, /device:TPU:1, one launch (start us, length us, event | category | flops | bytes accessed | tf_op | source)
XLA Modules:
  0.0 122.8 jit_solution(6886104495222075779)
XLA Ops:
  0.6 1.5 %pack.3 = bf16[16,40,128]{2,1,0:T(8,128)(2,1)} custom-call(f32[3,64]{1,0:T(4,128)} %pos_ref.3, f32[3,64]{1,0:T(4,128)} %nrm_ref.1, bf16[64,64]{1,0:T(8,128)(2,1)} %adj_ref.1), custom_call_target="tpu_custom_call" | custom-call | tf_op jit(solution)/shard_map/pack/pallas_call | solution.py:137
  2.1 10.2 %all-to-all-start = ((bf16[16,40,128]{2,1,0:T(8,128)(2,1)}), bf16[16,40,128]{2,1,0:T(8,128)(2,1)S(1)}, u32[]{:S(2)}, u32[]{:S(2)}) async-start(bf16[16,40,128]{2,1,0:T(8,128)(2,1)} %pack.3), calls=%async_computation | async-start | bytes 327680 | tf_op jit(solution)/shard_map/all_to_all | solution.py:392
  12.4 1.6 %pack.2 = bf16[32,40,128]{2,1,0:T(8,128)(2,1)} custom-call(f32[3,64]{1,0:T(4,128)} %pos_ref.3, f32[1,64]{1,0:T(1,128)} %bitcast.18, bf16[64,64]{1,0:T(8,128)(2,1)} %dir_ref.1), custom_call_target="tpu_custom_call" | custom-call | tf_op jit(solution)/shard_map/pack/pallas_call | solution.py:137
  14.0 1.6 %mixing.1.mix_ref = bf16[128,64]{1,0:T(8,128)(2,1)} custom-call(s32[1,64]{1,0:T(1,128)} %bitcast.19, s32[1,64]{1,0:T(1,128)} %bitcast.20, s32[4,128]{1,0:T(4,128)} %bitcast.17), custom_call_target="tpu_custom_call" | custom-call | tf_op jit(solution)/shard_map/mixing/pallas_call | solution.py:195
  15.6 4.5 %all-to-all-done.tgt_ref = bf16[16,40,128]{2,1,0:T(8,128)(2,1)S(1)} async-done(((bf16[16,40,128]{2,1,0:T(8,128)(2,1)}), bf16[16,40,128]{2,1,0:T(8,128)(2,1)S(1)}, u32[]{:S(2)}, u32[]{:S(2)}) %all-to-all-start) | async-done | bytes 163872 | tf_op jit(solution)/shard_map/all_to_all | solution.py:392
  20.2 21.7 %all_to_all.35.src_ref = bf16[32,40,128]{2,1,0:T(8,128)(2,1)S(1)} all-to-all(bf16[32,40,128]{2,1,0:T(8,128)(2,1)} %pack.2), channel_id=1, replica_groups=mesh['z_lo'=2,'y'=8,'core'=2,'x'=4,'z_hi'=4] {'x','z_lo','z_hi'}, dimensions={0} | all-to-all | bytes 655360 | tf_op jit(solution)/shard_map/all_to_all | solution.py:392
  41.9 13.4 %tile.12 = (f32[8,128]{1,0:T(8,128)S(1)}, f32[32,1,64]{2,1,0:T(1,128)S(1)}, f32[8,128]{1,0:T(8,128)S(1)}) custom-call(bf16[16,40,128]{2,1,0:T(8,128)(2,1)S(1)} %all-to-all-done.tgt_ref, bf16[32,40,128]{2,1,0:T(8,128)(2,1)S(1)} %all_to_all.35.src_ref), custom_call_target="tpu_custom_call" | custom-call | tf_op jit(solution)/shard_map/tile/pallas_call | solution.py:324
  55.3 15.8 %all_to_all.36 = f32[32,1,64]{2,1,0:T(1,128)S(1)} all-to-all(f32[32,1,64]{2,1,0:T(1,128)S(1)} %get-tuple-element.13), channel_id=1, replica_groups=mesh['z_lo'=2,'y'=8,'core'=2,'x'=4,'z_hi'=4] {'x','z_lo','z_hi'}, dimensions={0} | all-to-all | bytes 16384 | tf_op jit(solution)/shard_map/all_to_all | solution.py:392
  71.1 0.1 reduce_sum.36
  71.2 0.1 tile.11
  71.3 13.4 %all_to_all.37 = f32[16,8,128]{2,1,0:T(8,128)S(1)} all-to-all(f32[16,8,128]{2,1,0:T(8,128)S(1)} %broadcast_in_dim.8), channel_id=1, replica_groups=mesh['z_lo'=2,'y'=8,'core'=2,'x'=4,'z_hi'=4] {'core','y'}, dimensions={0} | all-to-all | bytes 131072 | tf_op jit(solution)/shard_map/all_to_all | solution.py:392
  84.7 0.0 copy-start
  84.8 0.0 copy-start.1
  84.8 12.0 %all_to_all.38.dens_ref = f32[32,8,128]{2,1,0:T(8,128)S(1)} all-to-all(f32[32,8,128]{2,1,0:T(8,128)S(1)} %broadcast_in_dim.9), channel_id=1, replica_groups=mesh['z_lo'=2,'y'=8,'core'=2,'x'=4,'z_hi'=4] {'x','z_lo','z_hi'}, dimensions={0} | all-to-all | bytes 262144 | tf_op jit(solution)/shard_map/all_to_all | solution.py:392
  96.8 0.0 copy-done
  96.8 0.0 copy-done.1
  96.8 0.9 patch.1
  97.7 11.8 %all_to_all.39 = f32[16,16,128]{2,1,0:T(8,128)S(1)} all-to-all(f32[16,16,128]{2,1,0:T(8,128)S(1)} %get-tuple-element.15), channel_id=1, replica_groups=mesh['z_lo'=2,'y'=8,'core'=2,'x'=4,'z_hi'=4] {'core','y'}, dimensions={0} | all-to-all | bytes 262144 | tf_op jit(solution)/shard_map/all_to_all | solution.py:392
  109.6 12.6 %all_to_all.40 = f32[32,8,128]{2,1,0:T(8,128)S(1)} all-to-all(f32[32,8,128]{2,1,0:T(8,128)S(1)} %bitcast.14), channel_id=1, replica_groups=mesh['z_lo'=2,'y'=8,'core'=2,'x'=4,'z_hi'=4] {'x','z_lo','z_hi'}, dimensions={0} | all-to-all | bytes 262144 | tf_op jit(solution)/shard_map/all_to_all | solution.py:392
  122.2 0.6 reduce_sum.39
  (7 shorter events, 0.1 us)
Async XLA Ops:
  2.1 18.1 %all-to-all-start = ((bf16[16,40,128]{2,1,0:T(8,128)(2,1)}), bf16[16,40,128]{2,1,0:T(8,128)(2,1)S(1)}, u32[]{:S(2)}, u32[]{:S(2)}) async-start(bf16[16,40,128]{2,1,0:T(8,128)(2,1)} %pack.3), calls=%async_computation | async-start | bytes 327680 | tf_op jit(solution)/shard_map/all_to_all | solution.py:392
  84.7 12.0 %copy-start = (bf16[1,256,512]{2,1,0:T(8,128)(2,1)S(1)}, bf16[1,256,512]{2,1,0:T(8,128)(2,1)}, u32[]{:S(2)}) copy-start(bf16[1,256,512]{2,1,0:T(8,128)(2,1)} %param.14) | copy-start | bytes 786436
  84.8 12.0 %copy-start.1 = (bf16[128,64]{1,0:T(8,128)(2,1)S(1)}, bf16[128,64]{1,0:T(8,128)(2,1)}, u32[]{:S(2)}) copy-start(bf16[128,64]{1,0:T(8,128)(2,1)} %mixing.1.mix_ref) | copy-start | bytes 49156

commit v10 on v9

--- a/solution.py
+++ b/solution.py
@@ -403,9 +403,9 @@
     tgt = pack(pack_targets_kernel, NTGT, positions, normals, adjoint)
     src = pack(pack_sources_kernel, NSRC, positions, areas.reshape(1, panels), direct)
     mix = mixing(patch_counts, patch_owner, block_lists)
+    src_all = exchange(src, SRC_AXES)
+    tgt, mix, src_all = lax.optimization_barrier((tgt, mix, src_all))
     tgt_all = exchange(tgt, TGT_AXES)
-    src, mix = lax.optimization_barrier((src, mix))
-    src_all = exchange(src, SRC_AXES)
     row_part, col_part, own_place = tile(tgt_all, src_all, panels)
 
     mine = jnp.sum(exchange(col_part, SRC_AXES), axis=0)

time: 125 us -> 125 us (level)
  blocking collectives: 87.4 us -> 80.9 us
  starting transfers between devices: 10.2 us -> 13.7 us
  waiting for transfers between devices: 4.54 us -> 7.66 us
    all_to_all x6, blocking collectives: 87.4 us -> 80.9 us  [exchange(): return lax.all_to_all(pieces, axes, 0, 0, tiled=True)]
    all_to_all x1, starting transfers between devices: 10.2 us -> 13.7 us  [exchange(): return lax.all_to_all(pieces, axes, 0, 0, tiled=True)]
    all_to_all x1, waiting for transfers between devices: 4.54 us -> 7.66 us  [exchange(): return lax.all_to_all(pieces, axes, 0, 0, tiled=True)]
where the time goes in v10:
time: 125 us; the launch traced here: 123 us
  blocking collectives  80.9 us (65%)
  Pallas kernels  19.1 us (15%)
  starting transfers between devices  13.7 us (11%)
  waiting for transfers between devices  7.66 us (6%)
    all_to_all x6, blocking collectives, exchange(): return lax.all_to_all(pieces, axes, 0, 0, tiled=True)  80.9 us
    all_to_all x1, starting transfers between devices, exchange(): return lax.all_to_all(pieces, axes, 0, 0, tiled=True)  13.7 us
    pallas_call x1, Pallas kernels, tile(): pl.pallas_call(tile_kernel, out_shape=(jax.ShapeDtypeStruct((8, LANES), F...  13.4 us
    all_to_all x1, waiting for transfers between devices, exchange(): return lax.all_to_all(pieces, axes, 0, 0, tiled=True)  7.66 us
    pallas_call x2, Pallas kernels, pack(): return pl.pallas_call(kernel, out_shape=out, name='pack')(*arrays)  3.13 us
  transfers between devices with their start and end apart: 1, of which 1 were waited for; matrix products, arithmetic and copies ran while one was open for 0% of the time, Pallas kernels for 3%

profile of v10, /device:TPU:1, one launch (start us, length us, event | category | flops | bytes accessed | tf_op | source)
XLA Modules:
  0.0 123.0 jit_solution(13333417052018011461)
XLA Ops:
  0.6 1.6 %pack.3 = bf16[32,40,128]{2,1,0:T(8,128)(2,1)} custom-call(f32[3,64]{1,0:T(4,128)} %pos_ref.3, f32[1,64]{1,0:T(1,128)} %bitcast.18, bf16[64,64]{1,0:T(8,128)(2,1)} %dir_ref.1), custom_call_target="tpu_custom_call" | custom-call | tf_op jit(solution)/shard_map/pack/pallas_call | solution.py:137
  2.3 13.7 %all-to-all-start = ((bf16[32,40,128]{2,1,0:T(8,128)(2,1)}), bf16[32,40,128]{2,1,0:T(8,128)(2,1)S(1)}, u32[]{:S(2)}, u32[]{:S(2)}) async-start(bf16[32,40,128]{2,1,0:T(8,128)(2,1)} %pack.3), calls=%async_computation | async-start | bytes 655360 | tf_op jit(solution)/shard_map/all_to_all | solution.py:392
  16.0 1.5 %pack.2 = bf16[16,40,128]{2,1,0:T(8,128)(2,1)} custom-call(f32[3,64]{1,0:T(4,128)} %pos_ref.3, f32[3,64]{1,0:T(4,128)} %nrm_ref.1, bf16[64,64]{1,0:T(8,128)(2,1)} %adj_ref.1), custom_call_target="tpu_custom_call" | custom-call | tf_op jit(solution)/shard_map/pack/pallas_call | solution.py:137
  17.5 1.6 %mixing.1.mix_ref = bf16[128,64]{1,0:T(8,128)(2,1)} custom-call(s32[1,64]{1,0:T(1,128)} %bitcast.19, s32[1,64]{1,0:T(1,128)} %bitcast.20, s32[4,128]{1,0:T(4,128)} %bitcast.17), custom_call_target="tpu_custom_call" | custom-call | tf_op jit(solution)/shard_map/mixing/pallas_call | solution.py:195
  19.1 7.7 %all-to-all-done.src_ref = bf16[32,40,128]{2,1,0:T(8,128)(2,1)S(1)} async-done(((bf16[32,40,128]{2,1,0:T(8,128)(2,1)}), bf16[32,40,128]{2,1,0:T(8,128)(2,1)S(1)}, u32[]{:S(2)}, u32[]{:S(2)}) %all-to-all-start) | async-done | bytes 327712 | tf_op jit(solution)/shard_map/all_to_all | solution.py:392
  26.8 18.0 %all_to_all.35.tgt_ref = bf16[16,40,128]{2,1,0:T(8,128)(2,1)S(1)} all-to-all(bf16[16,40,128]{2,1,0:T(8,128)(2,1)} %pack.2), channel_id=1, replica_groups=mesh['z_lo'=2,'y'=8,'core'=2,'x'=4,'z_hi'=4] {'core','y'}, dimensions={0} | all-to-all | bytes 327680 | tf_op jit(solution)/shard_map/all_to_all | solution.py:392
  44.8 13.4 %tile.12 = (f32[8,128]{1,0:T(8,128)S(1)}, f32[32,1,64]{2,1,0:T(1,128)S(1)}, f32[8,128]{1,0:T(8,128)S(1)}) custom-call(bf16[16,40,128]{2,1,0:T(8,128)(2,1)S(1)} %all_to_all.35.tgt_ref, bf16[32,40,128]{2,1,0:T(8,128)(2,1)S(1)} %all-to-all-done.src_ref), custom_call_target="tpu_custom_call" | custom-call | tf_op jit(solution)/shard_map/tile/pallas_call | solution.py:324
  58.2 13.4 %all_to_all.36 = f32[32,1,64]{2,1,0:T(1,128)S(1)} all-to-all(f32[32,1,64]{2,1,0:T(1,128)S(1)} %get-tuple-element.15), channel_id=1, replica_groups=mesh['z_lo'=2,'y'=8,'core'=2,'x'=4,'z_hi'=4] {'x','z_lo','z_hi'}, dimensions={0} | all-to-all | bytes 16384 | tf_op jit(solution)/shard_map/all_to_all | solution.py:392
  71.7 0.1 reduce_sum.36
  71.8 0.1 tile.11
  71.9 13.0 %all_to_all.37 = f32[16,8,128]{2,1,0:T(8,128)S(1)} all-to-all(f32[16,8,128]{2,1,0:T(8,128)S(1)} %broadcast_in_dim.8), channel_id=1, replica_groups=mesh['z_lo'=2,'y'=8,'core'=2,'x'=4,'z_hi'=4] {'core','y'}, dimensions={0} | all-to-all | bytes 131072 | tf_op jit(solution)/shard_map/all_to_all | solution.py:392
  84.9 0.0 copy-start
  84.9 0.0 copy-start.1
  84.9 12.0 %all_to_all.38.dens_ref = f32[32,8,128]{2,1,0:T(8,128)S(1)} all-to-all(f32[32,8,128]{2,1,0:T(8,128)S(1)} %broadcast_in_dim.9), channel_id=1, replica_groups=mesh['z_lo'=2,'y'=8,'core'=2,'x'=4,'z_hi'=4] {'x','z_lo','z_hi'}, dimensions={0} | all-to-all | bytes 262144 | tf_op jit(solution)/shard_map/all_to_all | solution.py:392
  96.9 0.0 copy-done
  96.9 0.0 copy-done.1
  96.9 0.9 patch.1
  97.8 11.8 %all_to_all.39 = f32[16,16,128]{2,1,0:T(8,128)S(1)} all-to-all(f32[16,16,128]{2,1,0:T(8,128)S(1)} %get-tuple-element.17), channel_id=1, replica_groups=mesh['z_lo'=2,'y'=8,'core'=2,'x'=4,'z_hi'=4] {'core','y'}, dimensions={0} | all-to-all | bytes 262144 | tf_op jit(solution)/shard_map/all_to_all | solution.py:392
  109.7 12.6 %all_to_all.40 = f32[32,8,128]{2,1,0:T(8,128)S(1)} all-to-all(f32[32,8,128]{2,1,0:T(8,128)S(1)} %bitcast.14), channel_id=1, replica_groups=mesh['z_lo'=2,'y'=8,'core'=2,'x'=4,'z_hi'=4] {'x','z_lo','z_hi'}, dimensions={0} | all-to-all | bytes 262144 | tf_op jit(solution)/shard_map/all_to_all | solution.py:392
  122.3 0.6 reduce_sum.39
  (7 shorter events, 0.1 us)
Async XLA Ops:
  2.3 24.5 %all-to-all-start = ((bf16[32,40,128]{2,1,0:T(8,128)(2,1)}), bf16[32,40,128]{2,1,0:T(8,128)(2,1)S(1)}, u32[]{:S(2)}, u32[]{:S(2)}) async-start(bf16[32,40,128]{2,1,0:T(8,128)(2,1)} %pack.3), calls=%async_computation | async-start | bytes 655360 | tf_op jit(solution)/shard_map/all_to_all | solution.py:392
  84.9 12.0 %copy-start = (bf16[1,256,512]{2,1,0:T(8,128)(2,1)S(1)}, bf16[1,256,512]{2,1,0:T(8,128)(2,1)}, u32[]{:S(2)}) copy-start(bf16[1,256,512]{2,1,0:T(8,128)(2,1)} %param.14) | copy-start | bytes 786436
  84.9 12.0 %copy-start.1 = (bf16[128,64]{1,0:T(8,128)(2,1)S(1)}, bf16[128,64]{1,0:T(8,128)(2,1)}, u32[]{:S(2)}) copy-start(bf16[128,64]{1,0:T(8,128)(2,1)} %mixing.1.mix_ref) | copy-start | bytes 49156

commit v11 on v9

--- a/solution.py
+++ b/solution.py
@@ -148,7 +148,7 @@
     return sum(value[m : m + 1, :] for m in parts)
 
 
-ROWS = 16
+ROWS = 32
 CHUNK = 256
 STEP = 1024
 

time: 125 us -> 125 us (level)
  no operation moved by 1% of the time
where the time goes in v11:
time: 125 us; the launch traced here: 123 us
  blocking collectives  87.4 us (70%)
  Pallas kernels  19.1 us (15%)
  starting transfers between devices  10.2 us (8%)
  waiting for transfers between devices  4.54 us (4%)
    all_to_all x6, blocking collectives, exchange(): return lax.all_to_all(pieces, axes, 0, 0, tiled=True)  87.4 us
    pallas_call x1, Pallas kernels, tile(): pl.pallas_call(tile_kernel, out_shape=(jax.ShapeDtypeStruct((8, LANES), F...  13.4 us
    all_to_all x1, starting transfers between devices, exchange(): return lax.all_to_all(pieces, axes, 0, 0, tiled=True)  10.2 us
    all_to_all x1, waiting for transfers between devices, exchange(): return lax.all_to_all(pieces, axes, 0, 0, tiled=True)  4.54 us
    pallas_call x2, Pallas kernels, pack(): return pl.pallas_call(kernel, out_shape=out, name='pack')(*arrays)  3.13 us
  transfers between devices with their start and end apart: 1, of which 1 were waited for; matrix products, arithmetic and copies ran while one was open for 0% of the time, Pallas kernels for 3%

profile of v11, /device:TPU:1, one launch (start us, length us, event | category | flops | bytes accessed | tf_op | source)
XLA Modules:
  0.0 122.8 jit_solution(888584575478972338)
XLA Ops:
  0.6 1.5 %pack.3 = bf16[16,40,128]{2,1,0:T(8,128)(2,1)} custom-call(f32[3,64]{1,0:T(4,128)} %pos_ref.3, f32[3,64]{1,0:T(4,128)} %nrm_ref.1, bf16[64,64]{1,0:T(8,128)(2,1)} %adj_ref.1), custom_call_target="tpu_custom_call" | custom-call | tf_op jit(solution)/shard_map/pack/pallas_call | solution.py:137
  2.1 10.2 %all-to-all-start = ((bf16[16,40,128]{2,1,0:T(8,128)(2,1)}), bf16[16,40,128]{2,1,0:T(8,128)(2,1)S(1)}, u32[]{:S(2)}, u32[]{:S(2)}) async-start(bf16[16,40,128]{2,1,0:T(8,128)(2,1)} %pack.3), calls=%async_computation | async-start | bytes 327680 | tf_op jit(solution)/shard_map/all_to_all | solution.py:392
  12.4 1.6 %pack.2 = bf16[32,40,128]{2,1,0:T(8,128)(2,1)} custom-call(f32[3,64]{1,0:T(4,128)} %pos_ref.3, f32[1,64]{1,0:T(1,128)} %bitcast.18, bf16[64,64]{1,0:T(8,128)(2,1)} %dir_ref.1), custom_call_target="tpu_custom_call" | custom-call | tf_op jit(solution)/shard_map/pack/pallas_call | solution.py:137
  14.0 1.6 %mixing.1.mix_ref = bf16[128,64]{1,0:T(8,128)(2,1)} custom-call(s32[1,64]{1,0:T(1,128)} %bitcast.19, s32[1,64]{1,0:T(1,128)} %bitcast.20, s32[4,128]{1,0:T(4,128)} %bitcast.17), custom_call_target="tpu_custom_call" | custom-call | tf_op jit(solution)/shard_map/mixing/pallas_call | solution.py:195
  15.6 4.5 %all-to-all-done.tgt_ref = bf16[16,40,128]{2,1,0:T(8,128)(2,1)S(1)} async-done(((bf16[16,40,128]{2,1,0:T(8,128)(2,1)}), bf16[16,40,128]{2,1,0:T(8,128)(2,1)S(1)}, u32[]{:S(2)}, u32[]{:S(2)}) %all-to-all-start) | async-done | bytes 163872 | tf_op jit(solution)/shard_map/all_to_all | solution.py:392
  20.2 21.7 %all_to_all.35.src_ref = bf16[32,40,128]{2,1,0:T(8,128)(2,1)S(1)} all-to-all(bf16[32,40,128]{2,1,0:T(8,128)(2,1)} %pack.2), channel_id=1, replica_groups=mesh['z_lo'=2,'y'=8,'core'=2,'x'=4,'z_hi'=4] {'x','z_lo','z_hi'}, dimensions={0} | all-to-all | bytes 655360 | tf_op jit(solution)/shard_map/all_to_all | solution.py:392
  41.9 13.4 %tile.12 = (f32[8,128]{1,0:T(8,128)S(1)}, f32[32,1,64]{2,1,0:T(1,128)S(1)}, f32[8,128]{1,0:T(8,128)S(1)}) custom-call(bf16[16,40,128]{2,1,0:T(8,128)(2,1)S(1)} %all-to-all-done.tgt_ref, bf16[32,40,128]{2,1,0:T(8,128)(2,1)S(1)} %all_to_all.35.src_ref), custom_call_target="tpu_custom_call" | custom-call | tf_op jit(solution)/shard_map/tile/pallas_call | solution.py:324
  55.3 15.8 %all_to_all.36 = f32[32,1,64]{2,1,0:T(1,128)S(1)} all-to-all(f32[32,1,64]{2,1,0:T(1,128)S(1)} %get-tuple-element.13), channel_id=1, replica_groups=mesh['z_lo'=2,'y'=8,'core'=2,'x'=4,'z_hi'=4] {'x','z_lo','z_hi'}, dimensions={0} | all-to-all | bytes 16384 | tf_op jit(solution)/shard_map/all_to_all | solution.py:392
  71.1 0.1 reduce_sum.36
  71.2 0.1 tile.11
  71.3 13.5 %all_to_all.37 = f32[16,8,128]{2,1,0:T(8,128)S(1)} all-to-all(f32[16,8,128]{2,1,0:T(8,128)S(1)} %broadcast_in_dim.8), channel_id=1, replica_groups=mesh['z_lo'=2,'y'=8,'core'=2,'x'=4,'z_hi'=4] {'core','y'}, dimensions={0} | all-to-all | bytes 131072 | tf_op jit(solution)/shard_map/all_to_all | solution.py:392
  84.7 0.0 copy-start
  84.8 0.0 copy-start.1
  84.8 12.0 %all_to_all.38.dens_ref = f32[32,8,128]{2,1,0:T(8,128)S(1)} all-to-all(f32[32,8,128]{2,1,0:T(8,128)S(1)} %broadcast_in_dim.9), channel_id=1, replica_groups=mesh['z_lo'=2,'y'=8,'core'=2,'x'=4,'z_hi'=4] {'x','z_lo','z_hi'}, dimensions={0} | all-to-all | bytes 262144 | tf_op jit(solution)/shard_map/all_to_all | solution.py:392
  96.8 0.0 copy-done
  96.8 0.0 copy-done.1
  96.8 0.9 patch.1
  97.7 11.8 %all_to_all.39 = f32[16,16,128]{2,1,0:T(8,128)S(1)} all-to-all(f32[16,16,128]{2,1,0:T(8,128)S(1)} %get-tuple-element.15), channel_id=1, replica_groups=mesh['z_lo'=2,'y'=8,'core'=2,'x'=4,'z_hi'=4] {'core','y'}, dimensions={0} | all-to-all | bytes 262144 | tf_op jit(solution)/shard_map/all_to_all | solution.py:392
  109.6 12.6 %all_to_all.40 = f32[32,8,128]{2,1,0:T(8,128)S(1)} all-to-all(f32[32,8,128]{2,1,0:T(8,128)S(1)} %bitcast.14), channel_id=1, replica_groups=mesh['z_lo'=2,'y'=8,'core'=2,'x'=4,'z_hi'=4] {'x','z_lo','z_hi'}, dimensions={0} | all-to-all | bytes 262144 | tf_op jit(solution)/shard_map/all_to_all | solution.py:392
  122.2 0.6 reduce_sum.39
  (7 shorter events, 0.1 us)
Async XLA Ops:
  2.1 18.1 %all-to-all-start = ((bf16[16,40,128]{2,1,0:T(8,128)(2,1)}), bf16[16,40,128]{2,1,0:T(8,128)(2,1)S(1)}, u32[]{:S(2)}, u32[]{:S(2)}) async-start(bf16[16,40,128]{2,1,0:T(8,128)(2,1)} %pack.3), calls=%async_computation | async-start | bytes 327680 | tf_op jit(solution)/shard_map/all_to_all | solution.py:392
  84.7 12.0 %copy-start = (bf16[1,256,512]{2,1,0:T(8,128)(2,1)S(1)}, bf16[1,256,512]{2,1,0:T(8,128)(2,1)}, u32[]{:S(2)}) copy-start(bf16[1,256,512]{2,1,0:T(8,128)(2,1)} %param.14) | copy-start | bytes 786436
  84.8 12.0 %copy-start.1 = (bf16[128,64]{1,0:T(8,128)(2,1)S(1)}, bf16[128,64]{1,0:T(8,128)(2,1)}, u32[]{:S(2)}) copy-start(bf16[128,64]{1,0:T(8,128)(2,1)} %mixing.1.mix_ref) | copy-start | bytes 49156
